TPU v7x, 32 devices: a whole 2x2x4 slice. The times are simulated.
32 devices in a mesh: groups: 2 (over x), space: 4 (over y, core), frame: 4 (over z).
Axes of the slice: x: 2, y: 2, z: 4, core: 2. Of those that a mesh axis runs over, the one named last changes fastest.
Arguments:
- tokens: bfloat16 [4, 64, 128, 512], P('frame', ('groups', 'space')), parts along dimension 1, may hold values from -6 to 6
- src_brick: int32 [3, 64], P(None, 'groups'), parts along dimension 1, may hold values from 0 to 31, as said below
- merge_num: int32 [3, 64], P(None, 'groups'), parts along dimension 1, may hold values from 1 to 4
- gain_attn: float32 [512], replicated, may hold values from 0.1 to 1.9
- w_query: bfloat16 [512, 512], replicated, may hold values from -4 to 4
- w_key: bfloat16 [512, 512], replicated, may hold values from -4 to 4
- w_value: bfloat16 [512, 512], replicated, may hold values from -0.25 to 0.25
- w_out: bfloat16 [512, 512], replicated, may hold values from -0.25 to 0.25
- gain_mlp: float32 [512], replicated, may hold values from 0.1 to 1.9
- w_in: bfloat16 [512, 2048], replicated, may hold values from -0.25 to 0.25
- w_back: bfloat16 [2048, 512], replicated, may hold values from -0.125 to 0.125
Outputs:
- output: bfloat16 [4, 64, 128, 512], P('frame', ('groups', 'space')), parts along dimension 1
There are 2 independent parts, one for each index of `groups`. A program takes and returns all parts, laid end to end along the dimension named above; an argument that names none is the same for every part. Nothing has to cross between parts.
Inputs may be any that keep to these rules, and one draw needn't show every extreme that they name: `src_brick`: group the bricks in aligned groups of 8. Over all frames, at most 7 entries pair a target brick of one group with a source brick of one group, and for every target group some source group is paired exactly 7 times.
All inputs are finite; a program needn't handle non-finite values.
Results may differ from a plain program's by a relative error of at most 0.0069.
Values may be sent and summed in bfloat16 or wider, within the bound.
No kernel may reach another device: no remote copies, remote signals or barrier semaphores. Data moves between devices by JAX's collectives and lax.ppermute only.
A program may use at most 64 MiB of HBM per device.

v0:
```python
import jax
import jax.numpy as jnp
from jax import lax
from jax.sharding import PartitionSpec as P

D = 512
HD = 64


def rms_norm(values_in, gain):
    as_float = values_in.astype(jnp.float32)
    mean_sq = jnp.mean(as_float * as_float, axis=-1, keepdims=True)
    return (as_float * lax.rsqrt(mean_sq + 1e-06) * gain).astype(jnp.bfloat16)


def temporal_block(merged, gain_attn, w_query, w_key, w_value, w_out, gain_mlp, w_in, w_back):
    frames_all, rows_all = (merged.shape[0], merged.shape[1])
    heads = D // HD
    normed = rms_norm(merged, gain_attn)
    queries = jnp.dot(normed, w_query, preferred_element_type=jnp.float32).astype(jnp.bfloat16)
    keys_proj = jnp.dot(normed, w_key, preferred_element_type=jnp.float32).astype(jnp.bfloat16)
    values_proj = jnp.dot(normed, w_value, preferred_element_type=jnp.float32).astype(jnp.bfloat16)
    query_heads = queries.reshape(frames_all, rows_all, heads, HD)
    key_heads = keys_proj.reshape(frames_all, rows_all, heads, HD)
    value_heads = values_proj.reshape(frames_all, rows_all, heads, HD)
    scores = jnp.einsum(
        "fmhd,gmhd->fghm", query_heads, key_heads, preferred_element_type=jnp.float32
    ) * (1.0 / HD**0.5)
    later = jnp.arange(frames_all)[:, None] >= jnp.arange(frames_all)[None, :]
    scores = jnp.where(later[:, :, None, None], scores, -1e30)
    row_max = jnp.max(scores, axis=1, keepdims=True)
    weights_exp = jnp.exp(scores - row_max)
    probs = (weights_exp / jnp.sum(weights_exp, axis=1, keepdims=True)).astype(jnp.bfloat16)
    context = jnp.einsum("fghm,gmhd->fmhd", probs, value_heads, preferred_element_type=jnp.float32)
    context = context.astype(jnp.bfloat16).reshape(frames_all, rows_all, D)
    mid = (
        merged.astype(jnp.float32) + jnp.dot(context, w_out, preferred_element_type=jnp.float32)
    ).astype(jnp.bfloat16)
    normed2 = rms_norm(mid, gain_mlp)
    hidden = jax.nn.gelu(jnp.dot(normed2, w_in, preferred_element_type=jnp.float32)).astype(
        jnp.bfloat16
    )
    return (
        mid.astype(jnp.float32) + jnp.dot(hidden, w_back, preferred_element_type=jnp.float32)
    ).astype(jnp.bfloat16)


def plan_slots(owners_all, source_rows, self_index, space_count, slot_cap, flat_rows):
    onehot = (owners_all[:, :, None] == jnp.arange(space_count)[None, None, :]).astype(jnp.int32)
    slot_rank = jnp.sum((jnp.cumsum(onehot, axis=1) - onehot) * onehot, axis=2)
    matched = (owners_all == self_index)[:, :, None] & (
        slot_rank[:, :, None] == jnp.arange(slot_cap)[None, None, :]
    )
    row_index = jnp.sum(matched.astype(jnp.int32) * source_rows[:, :, None], axis=1)
    is_valid = jnp.any(matched, axis=1)
    picked = jnp.take(flat_rows, row_index, axis=0)
    outgoing = jnp.where(is_valid[:, :, None, None], picked, jnp.zeros_like(picked))
    my_owner = lax.dynamic_index_in_dim(owners_all, self_index, 0, keepdims=False)
    my_rank = lax.dynamic_index_in_dim(slot_rank, self_index, 0, keepdims=False)
    return (outgoing, my_owner, my_rank)


def local(
    tokens, src_brick, merge_num, gain_attn, w_query, w_key, w_value, w_out, gain_mlp, w_in, w_back
):
    bricks_dev = tokens.shape[1]
    space_count = lax.axis_size("space")
    self_index = lax.axis_index("space")
    frames_all = src_brick.shape[0] + 1
    slot_cap = max(2, (frames_all - 1) * bricks_dev // space_count + 1)
    weights_mine = (
        lax.dynamic_slice_in_dim(merge_num, self_index * bricks_dev, bricks_dev, 1).astype(
            jnp.float32
        )
        * 0.25
    )
    stacked = lax.all_to_all(tokens, "frame", split_axis=2, concat_axis=0, tiled=True)
    slice_rows = stacked.shape[2]
    request_total = (frames_all - 1) * bricks_dev
    owners_all = (src_brick // bricks_dev).reshape(frames_all - 1, space_count, bricks_dev)
    owners_all = jnp.transpose(owners_all, (1, 0, 2)).reshape(space_count, request_total)
    local_rows = (src_brick % bricks_dev).reshape(frames_all - 1, space_count, bricks_dev)
    local_rows = jnp.transpose(local_rows, (1, 0, 2)).reshape(space_count, request_total)
    source_rows = (jnp.arange(request_total, dtype=jnp.int32) // bricks_dev * bricks_dev)[
        None, :
    ] + local_rows
    flat_rows = stacked.reshape(frames_all * bricks_dev, slice_rows, D)
    outgoing, my_owner, my_rank = plan_slots(
        owners_all, source_rows, self_index, space_count, slot_cap, flat_rows
    )
    received = lax.all_to_all(outgoing, "space", split_axis=0, concat_axis=0, tiled=True)
    pieces = received[my_owner, my_rank].reshape(frames_all - 1, bricks_dev, slice_rows, D)
    merged_rest = (
        stacked[1:].astype(jnp.float32)
        + weights_mine[:, :, None, None] * pieces.astype(jnp.float32)
    ).astype(jnp.bfloat16)
    merged = jnp.concatenate([stacked[:1], merged_rest], axis=0)
    slice_rows = merged.shape[2]
    rows_view = merged.reshape(frames_all, bricks_dev * slice_rows, D)
    result = temporal_block(
        rows_view, gain_attn, w_query, w_key, w_value, w_out, gain_mlp, w_in, w_back
    )
    result = result.reshape(frames_all, bricks_dev, slice_rows, D)
    return lax.all_to_all(result, "frame", split_axis=0, concat_axis=2, tiled=True)


def solution(mesh):
    in_specs = (
        P("frame", ("groups", "space"), None, None),
        P(None, "groups"),
        P(None, "groups"),
        P(),
        P(),
        P(),
        P(),
        P(),
        P(),
        P(),
        P(),
    )
    out_specs = P("frame", ("groups", "space"), None, None)
    return jax.shard_map(local, mesh=mesh, in_specs=in_specs, out_specs=out_specs, check_vma=False)
```

profile of v0, /device:TPU:0, one launch (start us, length us, event | category | flops | bytes accessed | tf_op | source)
XLA Modules:
  0.0 147.4 jit_solution(5047067707029519933)
XLA Ops:
  0.0 0.0 copy-start
  0.0 2.9 %copy.64 = bf16[1,8,128,512]{3,1,0,2:T(8,128)(2,1)} copy(bf16[1,8,128,512]{3,2,1,0:T(8,128)(2,1)} %param.11) | data formatting | bytes 2097152 | tf_op args[0]
  2.9 6.3 %all-to-all-start = ((bf16[1,8,128,512]{3,1,0,2:T(8,128)(2,1)}), bf16[1,8,128,512]{3,1,0,2:T(8,128)(2,1)S(1)}, u32[]{:S(2)}, u32[]{:S(2)}) async-start(bf16[1,8,128,512]{3,1,0,2:T(8,128)(2,1)} %copy.64), calls=%async_computation | async-start | bytes 2097152 | tf_op jit(solution)/shard_map/all_to_all | solution.py:77
  9.3 0.0 copy-done.6
  9.3 0.1 reshape.191
  9.4 0.1 reshape.192
  9.5 0.1 fusion.46
  9.5 0.1 reshape.193
  9.6 0.1 reshape.194
  9.7 0.1 reduce_window_sum.11
  9.8 0.2 select_reduce_fusion
  10.0 0.2 select_reduce_fusion.1
  10.2 0.1 copy.70
  10.3 0.1 reshape.205
  10.4 0.1 copy.69
  10.6 0.2 fusion.48
  10.8 0.1 copy.67
  10.9 24.1 %all-to-all-done = bf16[1,8,128,512]{3,1,0,2:T(8,128)(2,1)S(1)} async-done(((bf16[1,8,128,512]{3,1,0,2:T(8,128)(2,1)}), bf16[1,8,128,512]{3,1,0,2:T(8,128)(2,1)S(1)}, u32[]{:S(2)}, u32[]{:S(2)}) %all-to-all-start) | async-done | bytes 1048608 | tf_op jit(solution)/shard_map/all_to_all | solution.py:77
  35.0 1.0 copy-done.1
  36.0 1.5 %copy.85 = bf16[1,8,4,32,512]{4,3,1,2,0:T(8,128)(2,1)S(1)} copy(bf16[1,8,4,32,512]{4,1,3,2,0:T(8,128)(2,1)} %bitcast.88) | data formatting | bytes 2097152 | tf_op jit(solution)/shard_map/all_to_all | solution.py:77
  37.5 1.5 %gather_fusion = bf16[28,32,512]{2,1,0:T(8,128)(2,1)} fusion(bf16[32,32,512]{2,1,0:T(8,128)(2,1)S(1)} %bitcast.82, s32[1024]{0:T(1024)S(1)} %pad_clamp_fusion), kind=kCustom, calls=%fused_computation | custom fusion | bytes 1835120 | tf_op jit(solution)/shard_map/jit(_take)/gather | solution.py:56
  39.1 2.3 %select_select_fusion = bf16[4,7,32,512]{3,2,1,0:T(8,128)(2,1)} fusion(bf16[4,7,32,512]{3,2,1,0:T(8,128)(2,1)} %bitcast.90, pred[4,7]{1,0:T(4,128)(4,1)S(1)} %copy.69, pred[4,7]{1,0:T(4,128)(4,1)S(1)} %copy.67), kind=kLoop, calls=%fused_computation.39 | loop fusion | flops 917504 | bytes 1835064 | tf_op jit(solution)/shard_map/jit(_where)/select_n | solution.py:57
  41.4 4.2 %all-to-all-start.1 = ((bf16[4,7,32,512]{3,2,1,0:T(8,128)(2,1)}), bf16[4,7,32,512]{3,2,1,0:T(8,128)(2,1)}, u32[]{:S(2)}, u32[]{:S(2)}) async-start(bf16[4,7,32,512]{3,2,1,0:T(8,128)(2,1)} %select_select_fusion), calls=%async_computation.1 | async-start | bytes 1835008 | tf_op jit(solution)/shard_map/all_to_all | solution.py:91
  45.6 0.0 copy-done.7
  45.6 0.1 convert_multiply_fusion.5
  45.7 0.1 mul.107
  45.7 0.1 mul.108
  45.8 1.0 slice.15
  46.8 0.0 copy-start.2
  46.8 11.9 %all-to-all-done.1 = bf16[4,7,32,512]{3,2,1,0:T(8,128)(2,1)} async-done(((bf16[4,7,32,512]{3,2,1,0:T(8,128)(2,1)}), bf16[4,7,32,512]{3,2,1,0:T(8,128)(2,1)}, u32[]{:S(2)}, u32[]{:S(2)}) %all-to-all-start.1) | async-done | bytes 917536 | tf_op jit(solution)/shard_map/all_to_all | solution.py:91
  58.7 2.8 %gather_fusion.1 = bf16[24,32,512]{2,1,0:T(8,128)(2,1)} fusion(bf16[4,7,32,512]{3,2,1,0:T(8,128)(2,1)} %all-to-all-done.1, s32[24]{0:T(128)S(1)} %or_bitcast_fusion), kind=kCustom, calls=%fused_computation.1 | custom fusion | bytes 1573056 | tf_op jit(solution)/shard_map/gather | solution.py:92
  61.5 0.0 copy-done.2
  61.5 1.5 %fusion.24 = bf16[3,256,512]{2,1,0:T(8,128)(2,1)S(1)} fusion(bf16[3,256,512]{2,1,0:T(8,128)(2,1)S(1)} %bitcast.91, f32[3,256]{1,0:T(4,128)S(1)} %mul.108, bf16[3,256,512]{2,1,0:T(8,128)(2,1)} %bitcast.92), kind=kLoop, calls=%fused_computation.32 | loop fusion | flops 1966080 | bytes 2362368 | tf_op jit(solution)/shard_map/convert_element_type | solution.py:96
  63.0 0.0 copy-start.3
  63.0 0.3 fusion.10
  63.3 0.6 copy-done.3
  63.9 0.0 copy-done.8
  63.9 0.0 copy-done.9
  63.9 1.7 %convolution_convert_fusion = bf16[4,256,512]{2,1,0:T(8,128)(2,1)} fusion(f32[512]{0:T(512)S(1)} %copy-done.9, f32[4,256]{1,0:T(4,128)S(1)} %add_rsqrt_fusion.1, bf16[512,512]{1,0:T(8,128)(2,1)S(1)} %copy-done.8, bf16[3,256,512]{2,1,0:T(8,128)(2,1)S(1)} %fusion.24, bf16[1,256,512]{2,1,0:T(8,128)(2,1)S(1)} %bitcast.96), kind=kOutput, calls=%fused_computation.33 | convolution fusion | flops 540016640 | bytes 2627584 | tf_op jit(solution)/shard_map/dot_general | solution.py:20
  65.6 1.5 copy.73
  67.1 2.5 %copy.75 = bf16[4,256,8,64]{3,0,1,2:T(4,128)(2,1)} copy(bf16[4,256,8,64]{1,3,2,0:T(8,128)(2,1)S(1)} %bitcast.85) | data formatting | bytes 2097152 | tf_op jit(solution)/shard_map/reshape | solution.py:23
  69.6 3.0 %convolution_convert_fusion.1 = bf16[4,256,512]{2,1,0:T(8,128)(2,1)} fusion(f32[512]{0:T(512)S(1)} %copy-done.9, f32[4,256]{1,0:T(4,128)S(1)} %add_rsqrt_fusion.1, bf16[512,512]{1,0:T(8,128)(2,1)} %param.16, bf16[3,256,512]{2,1,0:T(8,128)(2,1)} %copy-done.3, bf16[1,256,512]{2,1,0:T(8,128)(2,1)S(1)} %bitcast.97), kind=kOutput, calls=%fused_computation.34 | convolution fusion | flops 540016640 | bytes 2627584 | tf_op jit(solution)/shard_map/dot_general | solution.py:21
  72.6 1.5 copy.72
  74.1 2.5 %copy.74 = bf16[4,256,8,64]{3,0,1,2:T(4,128)(2,1)} copy(bf16[4,256,8,64]{1,3,2,0:T(8,128)(2,1)S(1)} %bitcast.86) | data formatting | bytes 2097152 | tf_op jit(solution)/shard_map/reshape | solution.py:24
  76.6 6.5 %fusion.58 = f32[8,256,4,4]{3,2,1,0:T(4,128)} fusion(bf16[4,256,8,64]{3,0,1,2:T(4,128)(2,1)} %copy.74, bf16[4,256,8,64]{3,0,1,2:T(4,128)(2,1)} %copy.75), kind=kOutput, calls=%fused_computation.92 | convolution fusion | flops 4194304 | bytes 2228224 | tf_op jit(solution)/shard_map/fmhd,gmhd->fghm/dot_general | solution.py:26
  83.0 2.8 %copy.76 = f32[8,256,4,4]{1,0,2,3:T(8,128)S(1)} copy(f32[8,256,4,4]{3,2,1,0:T(4,128)} %fusion.58) | data formatting | bytes 262144 | tf_op jit(solution)/shard_map/fmhd,gmhd->fghm/dot_general | solution.py:26
  85.9 0.0 copy-start.4
  85.9 0.1 fusion.45
  86.0 0.1 fusion.44
  86.1 0.1 divide_convert_fusion
  86.2 4.3 %copy.78 = bf16[4,4,8,256]{1,0,2,3:T(4,128)(2,1)} copy(bf16[4,4,8,256]{3,2,1,0:T(8,128)(2,1)S(1)} %divide_convert_fusion) | data formatting | bytes 131072 | tf_op jit(solution)/shard_map/convert_element_type | solution.py:33
  90.5 0.0 copy-done.4
  90.5 2.8 %convolution_convert_fusion.2 = bf16[4,256,512]{2,1,0:T(8,128)(2,1)} fusion(f32[512]{0:T(512)S(1)} %copy-done.9, f32[4,256]{1,0:T(4,128)S(1)} %add_rsqrt_fusion.1, bf16[512,512]{1,0:T(8,128)(2,1)} %param.17, bf16[3,256,512]{2,1,0:T(8,128)(2,1)S(1)} %copy-done.4, bf16[1,256,512]{2,1,0:T(8,128)(2,1)S(1)} %bitcast.98), kind=kOutput, calls=%fused_computation.35 | convolution fusion | flops 540016640 | bytes 2627584 | tf_op jit(solution)/shard_map/dot_general | solution.py:22
  93.2 1.5 copy.71
  94.7 3.0 %copy.77 = bf16[4,256,8,64]{3,0,2,1:T(4,128)(2,1)} copy(bf16[4,256,8,64]{1,3,2,0:T(8,128)(2,1)S(1)} %bitcast.87) | data formatting | bytes 2097152 | tf_op jit(solution)/shard_map/reshape | solution.py:25
  97.7 5.9 %convert_bitcast_fusion = bf16[4,256,8,64]{3,0,2,1:T(4,128)(2,1)} fusion(bf16[4,256,8,64]{3,0,2,1:T(4,128)(2,1)} %copy.77, bf16[4,4,8,256]{1,0,2,3:T(4,128)(2,1)} %copy.78), kind=kOutput, calls=%fused_computation.29 | convolution fusion | flops 4718592 | bytes 2162688 | tf_op jit(solution)/shard_map/fghm,gmhd->fmhd/dot_general | solution.py:34
  103.6 4.2 %copy.79 = bf16[4,256,8,64]{1,3,2,0:T(8,128)(2,1)} copy(bf16[4,256,8,64]{3,0,2,1:T(4,128)(2,1)} %convert_bitcast_fusion) | data formatting | bytes 2097152 | tf_op jit(solution)/shard_map/convert_element_type | solution.py:35
  107.8 0.0 copy-done.5
  107.8 3.1 %fusion.14 = (f32[4,256]{1,0:T(4,128)S(1)}, bf16[4,256,512]{2,1,0:T(8,128)(2,1)}) fusion(bf16[4,256,512]{1,2,0:T(8,128)(2,1)} %bitcast.93, bf16[512,512]{1,0:T(8,128)(2,1)} %param.18, bf16[3,256,512]{2,1,0:T(8,128)(2,1)S(1)} %copy-done.5, bf16[1,256,512]{2,1,0:T(8,128)(2,1)S(1)} %bitcast.99), kind=kOutput, calls=%fused_computation.22 | convolution fusion | flops 540539904 | bytes 3674112 | tf_op jit(solution)/shard_map/dot_general | solution.py:37
  110.9 0.0 copy-done
  110.9 0.0 copy-done.10
  110.9 7.1 %fusion.17 = bf16[4,256,512]{2,1,0:T(8,128)(2,1)S(1)} fusion(bf16[4,256,512]{2,1,0:T(8,128)(2,1)} %get-tuple-element.10, bf16[2048,512]{1,0:T(8,128)(2,1)S(1)} %copy-done, bf16[512,2048]{1,0:T(8,128)(2,1)} %param.20, f32[512]{0:T(512)S(1)} %copy-done.10, f32[4,256]{1,0:T(4,128)S(1)} %add_rsqrt_fusion), kind=kOutput, calls=%fused_computation.25 | convolution fusion | flops 4317511680 | bytes 6297600 | tf_op jit(solution)/shard_map/dot_general | solution.py:44
  118.1 28.2 %all_to_all.38 = bf16[4,8,32,512]{3,2,1,0:T(8,128)(2,1)S(1)} all-to-all(bf16[4,8,32,512]{3,2,1,0:T(8,128)(2,1)S(1)} %bitcast.94), channel_id=1, replica_groups=mesh['groups'=2,'space'=4,'frame'=4] {'frame'}, dimensions={0} | all-to-all | bytes 2097152 | tf_op jit(solution)/shard_map/all_to_all | solution.py:104
  146.3 1.0 copy.81
  (21 shorter events, 0.1 us)
Async XLA Ops:
  0.0 110.9 %copy-start = (bf16[2048,512]{1,0:T(8,128)(2,1)S(1)}, bf16[2048,512]{1,0:T(8,128)(2,1)}, u32[]{:S(2)}) copy-start(bf16[2048,512]{1,0:T(8,128)(2,1)} %param.21) | copy-start | bytes 6291460
  0.0 9.3 %copy-start.6 = (s32[3,32]{1,0:T(4,128)S(1)}, s32[3,32]{1,0:T(4,128)}, u32[]{:S(2)}) copy-start(s32[3,32]{1,0:T(4,128)} %param.12) | copy-start | bytes 1156
  2.9 32.0 %all-to-all-start = ((bf16[1,8,128,512]{3,1,0,2:T(8,128)(2,1)}), bf16[1,8,128,512]{3,1,0,2:T(8,128)(2,1)S(1)}, u32[]{:S(2)}, u32[]{:S(2)}) async-start(bf16[1,8,128,512]{3,1,0,2:T(8,128)(2,1)} %copy.64), calls=%async_computation | async-start | bytes 2097152 | tf_op jit(solution)/shard_map/all_to_all | solution.py:77
  35.0 1.0 copy-start.1
  39.1 6.5 %copy-start.7 = (s32[3,32]{1,0:T(4,128)S(1)}, s32[3,32]{1,0:T(4,128)}, u32[]{:S(2)}) copy-start(s32[3,32]{1,0:T(4,128)} %param.13) | copy-start | bytes 1156
  41.4 17.3 %all-to-all-start.1 = ((bf16[4,7,32,512]{3,2,1,0:T(8,128)(2,1)}), bf16[4,7,32,512]{3,2,1,0:T(8,128)(2,1)}, u32[]{:S(2)}, u32[]{:S(2)}) async-start(bf16[4,7,32,512]{3,2,1,0:T(8,128)(2,1)} %select_select_fusion), calls=%async_computation.1 | async-start | bytes 1835008 | tf_op jit(solution)/shard_map/all_to_all | solution.py:91
  46.8 14.6 %copy-start.2 = (bf16[3,1,8,32,512]{4,3,2,0,1:T(8,128)(2,1)S(1)}, bf16[3,1,8,32,512]{4,3,2,0,1:T(8,128)(2,1)}, u32[]{:S(2)}) copy-start(bf16[3,1,8,32,512]{4,3,2,0,1:T(8,128)(2,1)} %slice.15) | copy-start | bytes 2359300
  61.5 2.4 %copy-start.8 = (bf16[512,512]{1,0:T(8,128)(2,1)S(1)}, bf16[512,512]{1,0:T(8,128)(2,1)}, u32[]{:S(2)}) copy-start(bf16[512,512]{1,0:T(8,128)(2,1)} %param.15) | copy-start | bytes 1572868
  61.5 2.4 %copy-start.9 = (f32[512]{0:T(512)S(1)}, f32[512]{0:T(512)}, u32[]{:S(2)}) copy-start(f32[512]{0:T(512)} %param.14) | copy-start | bytes 6148
  63.0 0.9 copy-start.3
  85.9 4.6 %copy-start.4 = (bf16[3,256,512]{2,1,0:T(8,128)(2,1)S(1)}, bf16[3,256,512]{2,1,0:T(8,128)(2,1)}, u32[]{:S(2)}) copy-start(bf16[3,256,512]{2,1,0:T(8,128)(2,1)} %copy-done.3) | copy-start | bytes 2359300
  103.6 4.2 %copy-start.5 = (bf16[3,256,512]{2,1,0:T(8,128)(2,1)S(1)}, bf16[3,256,512]{2,1,0:T(8,128)(2,1)}, u32[]{:S(2)}) copy-start(bf16[3,256,512]{2,1,0:T(8,128)(2,1)} %copy-done.3) | copy-start | bytes 2359300
  107.8 3.2 %copy-start.10 = (f32[512]{0:T(512)S(1)}, f32[512]{0:T(512)}, u32[]{:S(2)}) copy-start(f32[512]{0:T(512)} %param.19) | copy-start | bytes 6148
where the time goes:
time: 148 us; the launch traced here: 147 us
  local copies, waits for them, and re-layouts  37 us (25%)
  waiting for transfers between devices  35.9 us (24%)
  matrix products  30.1 us (20%)
  blocking collectives  28.2 us (19%)
  starting transfers between devices  10.5 us (7%)
  other arithmetic  5.3 us (4%)
    all_to_all x1, blocking collectives, local(): lax.all_to_all(result, 'frame', split_axis=0, concat_axis=2, tiled=True)  28.2 us
    all_to_all x1, waiting for transfers between devices, local(): lax.all_to_all(tokens, 'frame', split_axis=2, concat_axis=0, tiled=True)  24.1 us
    all_to_all x1, waiting for transfers between devices, local(): lax.all_to_all(outgoing, 'space', split_axis=0, concat_axis=0, tiled=True)  11.9 us
    dot_general x1, matrix products, temporal_block(): jnp.dot(hidden, w_back, preferred_element_type=jnp.float32)  7.12 us
    dot_general x1, matrix products, temporal_block(): jnp.einsum('fmhd,gmhd->fghm', query_heads, key_heads, preferred_element_t...  6.46 us
    all_to_all x1, starting transfers between devices, local(): lax.all_to_all(tokens, 'frame', split_axis=2, concat_axis=0, tiled=True)  6.32 us
    dot_general x1, matrix products, temporal_block(): jnp.einsum('fghm,gmhd->fmhd', probs, value_heads, preferred_element_type=...  5.87 us
    unnamed x23, local copies, waits for them, and re-layouts  4.57 us
  transfers between devices with their start and end apart: 2, of which 2 were waited for; matrix products, arithmetic and copies ran while one was open for 2% of the time, Pallas kernels for 0%

commit v1 on v0

v1 whole, which is shorter than its diff:
```python
import functools

import jax
import jax.numpy as jnp
from jax import lax
from jax.experimental import pallas as pl
from jax.experimental.pallas import tpu as pltpu
from jax.sharding import PartitionSpec as P

HD = 64
ROW_TILE = 16
BLOCK_FF = 512

VMEM = pltpu.VMEM
SMEM = pltpu.SMEM


def spec(space):
    return pl.BlockSpec(memory_space=space)


def exchange(values, axis, step):
    size = lax.axis_size(axis)
    return lax.ppermute(values, axis, [(i, i ^ step) for i in range(size)])


def table_kernel(cap, bricks, spaces, ids, src, send_tab, req_tab, count):
    requests = src.shape[0] * bricks
    me = ids[0]
    for owner in range(spaces):
        count[owner] = 0

    def one_request(q, carry):
        source = src[lax.div(q, bricks), me * bricks + lax.rem(q, bricks)]
        owner = lax.div(source, bricks)
        rank = count[owner]
        req_tab[q] = (owner ^ me) * cap + rank
        count[owner] = rank + 1
        return carry

    lax.fori_loop(0, requests, one_request, 0)

    for j in range(spaces):
        target = me ^ j

        def one_send(q, filled, target=target, j=j):
            frame = lax.div(q, bricks)
            source = src[frame, target * bricks + lax.rem(q, bricks)]
            owner = lax.div(source, bricks)
            send_tab[j * cap + filled] = frame * bricks + lax.rem(source, bricks)
            return filled + (owner == me).astype(jnp.int32)

        lax.fori_loop(0, requests, one_send, 0)


def plan_tables(ids, src_brick, cap, bricks, spaces):
    requests = src_brick.shape[0] * bricks
    return pl.pallas_call(
        functools.partial(table_kernel, cap, bricks, spaces),
        out_shape=(
            jax.ShapeDtypeStruct((spaces * cap + 1,), jnp.int32),
            jax.ShapeDtypeStruct((requests,), jnp.int32),
        ),
        in_specs=[spec(SMEM), spec(SMEM)],
        out_specs=(spec(SMEM), spec(SMEM)),
        scratch_shapes=[SMEM((spaces,), jnp.int32)],
        name="plan",
    )(ids, src_brick)


def select_kernel(frames, bricks, cap, spaces, *refs):
    ids, send_tab = refs[:2]
    parts = refs[2 : 2 + frames]
    stacked = refs[2 + frames]
    outs = refs[3 + frames :]
    mine = ids[1]
    for k in range(frames):
        stacked[pl.ds((mine ^ k) * bricks, bricks)] = parts[k][...]
    for j in list(range(1, spaces)) + [0]:
        for m in range(cap):
            outs[j][m] = stacked[send_tab[j * cap + m]]


def select(ids, send_tab, parts, cap, spaces):
    frames = len(parts)
    bricks, rows, width = parts[0].shape
    dtype = parts[0].dtype
    slots = jax.ShapeDtypeStruct((cap, rows, width), dtype)
    return pl.pallas_call(
        functools.partial(select_kernel, frames, bricks, cap, spaces),
        out_shape=(jax.ShapeDtypeStruct((frames * bricks, rows, width), dtype),)
        + (slots,) * spaces,
        in_specs=[spec(SMEM), spec(SMEM)] + [spec(VMEM)] * frames,
        out_specs=(spec(VMEM),) * (1 + spaces),
        compiler_params=pltpu.CompilerParams(vmem_limit_bytes=8 << 20),
        cost_estimate=pl.CostEstimate(flops=0, bytes_accessed=4 << 20, transcendentals=0),
        name="select",
    )(ids, send_tab, *parts)


def normalise(values, gain):
    wide = values.astype(jnp.float32)
    mean_sq = jnp.mean(wide * wide, axis=-1, keepdims=True)
    return (wide * lax.rsqrt(mean_sq + 1e-06) * gain).astype(jnp.bfloat16)


def matmul(a, b):
    return jnp.dot(a, b, preferred_element_type=jnp.float32)


def block_kernel(frames, bricks, cap, spaces, heads, *refs):
    ids, req_tab, merge_num, stacked = refs[:4]
    pieces = refs[4 : 4 + spaces]
    gain_a, w_q, w_k, w_v, w_o, gain_m, w_in, w_back = refs[4 + spaces : 12 + spaces]
    outs = refs[12 + spaces : 12 + spaces + frames]
    slots, merged, hidden, result = refs[12 + spaces + frames :]
    rows, width = stacked.shape[1:]
    per_frame = bricks * rows
    for j in range(spaces):
        slots[j * cap : (j + 1) * cap] = pieces[j][...]
    for b in range(bricks):
        merged[b * rows : (b + 1) * rows] = stacked[b]
    base = ids[0] * bricks
    for f in range(1, frames):
        for b in range(bricks):
            q = (f - 1) * bricks + b
            weight = merge_num[f - 1, base + b].astype(jnp.float32) * 0.25
            piece = slots[req_tab[q]].astype(jnp.float32)
            at = f * per_frame + b * rows
            merged[at : at + rows] = (
                stacked[f * bricks + b].astype(jnp.float32) + weight * piece
            ).astype(jnp.bfloat16)
    normed = normalise(merged[...], gain_a[...])
    queries = matmul(normed, w_q[...]).astype(jnp.bfloat16)
    keys = matmul(normed, w_k[...]).astype(jnp.bfloat16)
    vals = matmul(normed, w_v[...]).astype(jnp.bfloat16)

    def frame_of(x, f):
        return x[f * per_frame : (f + 1) * per_frame]

    lanes = 128
    head_of = lax.broadcasted_iota(jnp.int32, (width, lanes), 0) // HD
    gather_heads = (head_of == lax.broadcasted_iota(jnp.int32, (width, lanes), 1)).astype(
        jnp.bfloat16
    )
    head_to = lax.broadcasted_iota(jnp.int32, (lanes, width), 1) // HD
    spread_heads = (head_to == lax.broadcasted_iota(jnp.int32, (lanes, width), 0)).astype(
        jnp.bfloat16
    )
    for f in range(frames):
        query = frame_of(queries, f).astype(jnp.float32)
        scores = []
        for g in range(f + 1):
            product = query * frame_of(keys, g).astype(jnp.float32)
            high = product.astype(jnp.bfloat16)
            low = (product - high.astype(jnp.float32)).astype(jnp.bfloat16)
            scores.append(
                (matmul(high, gather_heads) + matmul(low, gather_heads)) * (1.0 / HD**0.5)
            )
        top = functools.reduce(jnp.maximum, scores)
        exps = [jnp.exp(s - top) for s in scores]
        total = functools.reduce(jnp.add, exps)
        context = None
        for g in range(f + 1):
            prob = (exps[g] / total).astype(jnp.bfloat16)
            term = matmul(prob, spread_heads) * frame_of(vals, g).astype(jnp.float32)
            context = term if context is None else context + term
        hidden[f * per_frame : (f + 1) * per_frame] = context.astype(jnp.bfloat16)
    mid = (merged[...].astype(jnp.float32) + matmul(hidden[...], w_o[...])).astype(jnp.bfloat16)
    normed2 = normalise(mid, gain_m[...])
    total = mid.astype(jnp.float32)
    depth = w_in.shape[1]
    step = min(BLOCK_FF, depth)
    for at in range(0, depth, step):
        part = jax.nn.gelu(matmul(normed2, w_in[:, at : at + step])).astype(jnp.bfloat16)
        total = total + matmul(part, w_back[at : at + step])
    result[...] = total.astype(jnp.bfloat16).reshape(result.shape)
    mine = ids[1]
    for k in range(frames):
        outs[k][...] = result[pl.ds((mine ^ k) * bricks, bricks)]


def run_block(ids, req_tab, merge_num, stacked, pieces, weights, frames, cap):
    spaces = len(pieces)
    total, rows, width = stacked.shape
    bricks = total // frames
    dtype = stacked.dtype
    return pl.pallas_call(
        functools.partial(block_kernel, frames, bricks, cap, spaces, width // HD),
        out_shape=(jax.ShapeDtypeStruct((bricks, rows, width), dtype),) * frames,
        in_specs=[spec(SMEM)] * 3 + [spec(VMEM)] * (1 + spaces + len(weights)),
        out_specs=(spec(VMEM),) * frames,
        scratch_shapes=[
            VMEM((spaces * cap, rows, width), dtype),
            VMEM((total * rows, width), dtype),
            VMEM((total * rows, width), dtype),
            VMEM((total, rows, width), dtype),
        ],
        compiler_params=pltpu.CompilerParams(vmem_limit_bytes=32 << 20),
        cost_estimate=pl.CostEstimate(
            flops=6_400_000_000, bytes_accessed=8 << 20, transcendentals=1 << 20
        ),
        name="block",
    )(ids, req_tab, merge_num, stacked, *pieces, *weights)


def assemble_kernel(count, mine_at, *refs):
    ids = refs[0]
    parts = refs[1 : 1 + count]
    out, sems = refs[1 + count :]
    copies = [
        pltpu.make_async_copy(parts[i], out.at[:, mine_at(i, ids[1])], sems.at[i])
        for i in range(count)
    ]
    for copy in copies:
        copy.start()
    for copy in copies:
        copy.wait()


def assemble(ids, parts, frames):
    count = len(parts)
    bricks, rows, width = parts[0].shape

    def mine_at(i, mine):
        return i // frames * frames + (mine ^ (i % frames))

    return pl.pallas_call(
        functools.partial(assemble_kernel, count, mine_at),
        out_shape=jax.ShapeDtypeStruct((bricks, count, rows, width), parts[0].dtype),
        in_specs=[spec(SMEM)] + [spec(VMEM)] * count,
        out_specs=spec(pl.ANY),
        scratch_shapes=[pltpu.SemaphoreType.DMA((count,))],
        compiler_params=pltpu.CompilerParams(vmem_limit_bytes=4 << 20),
        name="assemble",
    )(ids, *parts)


def local(tokens, src_brick, merge_num, gain_attn, w_q, w_k, w_v, w_out, gain_mlp, w_in, w_back):
    frames = lax.axis_size("frame")
    spaces = lax.axis_size("space")
    _, bricks, tall, width = tokens.shape
    cap = max(2, (frames - 1) * bricks // spaces + 1)
    chunks = max(1, tall // frames // ROW_TILE)
    rows = tall // frames // chunks
    mine = lax.axis_index("frame")
    ids = jnp.stack([lax.axis_index("space"), mine]).astype(jnp.int32)
    cut = tokens.reshape(bricks, chunks * frames, rows, width)
    weights = (gain_attn[None], w_q, w_k, w_v, w_out, gain_mlp[None], w_in, w_back)
    send_tab, req_tab = plan_tables(ids, src_brick, cap, bricks, spaces)

    arrived = []
    for c in range(chunks):
        parts = [
            lax.dynamic_index_in_dim(cut, c * frames + (mine ^ k), 1, keepdims=False)
            for k in range(frames)
        ]
        if arrived:
            held = lax.optimization_barrier((tuple(parts), tuple(arrived[-1])))
            parts, arrived[-1] = list(held[0]), list(held[1])
        arrived.append(
            [parts[0]] + [exchange(parts[k], "frame", k) for k in range(1, frames)]
        )
    back = []
    for c in range(chunks):
        stacked, *slots = select(ids, send_tab, arrived[c], cap, spaces)
        pieces = [slots[0]] + [exchange(slots[j], "space", j) for j in range(1, spaces)]
        done = run_block(ids, req_tab, merge_num, stacked, pieces, weights, frames, cap)
        back += [done[0]] + [exchange(done[k], "frame", k) for k in range(1, frames)]
    out = assemble(ids, back, frames)
    return out.reshape(1, bricks, tall, width)


def solution(mesh):
    tokens = P("frame", ("groups", "space"), None, None)
    tables = P(None, "groups")
    in_specs = (tokens, tables, tables) + (P(),) * 8
    return jax.shard_map(local, mesh=mesh, in_specs=in_specs, out_specs=tokens, check_vma=False)
```

time: 148 us -> 75.7 us (0.51)
  matrix products: 30.1 us -> 0 us
  blocking collectives: 28.2 us -> 0 us
  local copies, waits for them, and re-layouts: 37 us -> 9.81 us
  Pallas kernels: 0 us -> 19.6 us
  waiting for transfers between devices: 35.9 us -> 22.3 us
  starting transfers between devices: 10.5 us -> 22.9 us
  other arithmetic: 5.3 us -> 0.59 us
    all_to_all x2 -> x0, waiting for transfers between devices: 35.9 us -> none  [the longest x1 24.1 us: local(): lax.all_to_all(tokens, 'frame', split_axis=2, concat_axis=0, tiled=True)]
    dot_general x7 -> x0, matrix products: 30.1 us -> none  [the longest x1 7.12 us: temporal_block(): jnp.dot(hidden, w_back, preferred_element_type=jnp.float32)]
    all_to_all x1 -> x0, blocking collectives: 28.2 us -> none  [local(): lax.all_to_all(result, 'frame', split_axis=0, concat_axis=2, tiled=True)]
    ppermute x0 -> x18, starting transfers between devices: none -> 22.9 us  [exchange(): return lax.ppermute(values, axis, [(i, i ^ step) for i in range(size)])]
    ppermute x0 -> x18, waiting for transfers between devices: none -> 22.3 us  [exchange(): return lax.ppermute(values, axis, [(i, i ^ step) for i in range(size)])]
    pallas_call x0 -> x6, Pallas kernels: none -> 19.6 us  [the longest x2 13.7 us: run_block(): pl.pallas_call(functools.partial(block_kernel, frames, bricks, cap, space...]
    convert_element_type x5 -> x0, local copies, waits for them, and re-layouts: 12.8 us -> none  [the longest x1 4.26 us: temporal_block(): (weights_exp / jnp.sum(weights_exp, axis=1, keepdims=True)).astype(jnp.bf...]
    all_to_all x2 -> x0, starting transfers between devices: 10.5 us -> none  [the longest x1 6.32 us: local(): lax.all_to_all(tokens, 'frame', split_axis=2, concat_axis=0, tiled=True)]
  transfers between devices with their start and end apart: 2 -> 18, of which waited for: 2 -> 7; matrix products, arithmetic and copies ran while one was open for 2% -> 1% of each run, Pallas kernels for 0% -> 24%
where the time goes in v1:
time: 75.7 us; the launch traced here: 75.3 us
  starting transfers between devices  22.9 us (30%)
  waiting for transfers between devices  22.3 us (29%)
  Pallas kernels  19.6 us (26%)
  local copies, waits for them, and re-layouts  9.81 us (13%)
    ppermute x18, starting transfers between devices, exchange(): return lax.ppermute(values, axis, [(i, i ^ step) for i in range(size)])  22.9 us
    ppermute x18, waiting for transfers between devices, exchange(): return lax.ppermute(values, axis, [(i, i ^ step) for i in range(size)])  22.3 us
    pallas_call x2, Pallas kernels, run_block(): pl.pallas_call(functools.partial(block_kernel, frames, bricks, cap, space...  13.7 us
    unnamed x32, local copies, waits for them, and re-layouts  8.3 us
    pallas_call x1, Pallas kernels, plan_tables(): pl.pallas_call(functools.partial(table_kernel, cap, bricks, spaces), out_...  3.09 us
    pallas_call x1, Pallas kernels, assemble(): pl.pallas_call(functools.partial(assemble_kernel, count, mine_at), out_sh...  1.57 us
  transfers between devices with their start and end apart: 18, of which 7 were waited for; matrix products, arithmetic and copies ran while one was open for 1% of the time, Pallas kernels for 24%

profile of v1, /device:TPU:0, one launch (start us, length us, event | category | flops | bytes accessed | tf_op | source)
XLA Modules:
  0.0 75.3 jit_solution(14455829606636196046)
XLA Ops:
  0.0 0.0 copy-start.3
  0.0 0.0 copy-start.12
  0.0 1.5 %dynamic-slice_bitcast_fusion = (bf16[8,16,512]{2,1,0:T(8,128)(2,1)S(1)}, bf16[8,16,512]{2,1,0:T(8,128)(2,1)S(1)}, bf16[8,16,512]{2,1,0:T(8,128)(2,1)S(1)}, bf16...) fusion(bf16[8,8,16,512]{3,2,1,0:T(8,128)(2,1)} %bitcast.42, ...), kind=kLoop, calls=%fused_computation | loop fusion | bytes 2097184 | tf_op jit(solution)/shard_map/jit(dynamic_index_in_dim)/squeeze | solution.py:255
  1.5 5.2 %collective-permute-start.2 = (bf16[8,16,512]{2,1,0:T(8,128)(2,1)S(1)}, bf16[8,16,512]{2,1,0:T(8,128)(2,1)S(1)}, u32[]{:S(2)}, u32[]{:S(2)}) collective-permute-start(bf16[8,16,512]{2,1,0:T(8,128)(2,1)S(1)} %get-tuple-element.61), channel_id=1, source_target_pairs={{0,3},{1,2},{2,1},{3,0},{4,7},{5,6},{6,5},{7,4},{8,11},{9,10},{10,... | collective-permute-start | bytes 393224 | tf_op jit(solution)/shard_map/ppermute | solution.py:24
  6.7 0.0 collective-permute-start.1
  6.7 0.6 collective-permute-start
  7.3 3.8 %collective-permute-done.2.refs_5_ = bf16[8,16,512]{2,1,0:T(8,128)(2,1)S(1)} collective-permute-done((bf16[8,16,512]{2,1,0:T(8,128)(2,1)S(1)}, bf16[8,16,512]{2,1,0:T(8,128)(2,1)S(1)}, u32[]{:S(2)}, u32[]{:S(2)}) %collective-permute-start.2) | collective-permute-done | bytes 131104 | tf_op jit(solution)/shard_map/ppermute | solution.py:24
  11.1 6.6 %collective-permute-done.1.refs_4_ = bf16[8,16,512]{2,1,0:T(8,128)(2,1)S(1)} collective-permute-done((bf16[8,16,512]{2,1,0:T(8,128)(2,1)S(1)}, bf16[8,16,512]{2,1,0:T(8,128)(2,1)S(1)}, u32[]{:S(2)}, u32[]{:S(2)}) %collective-permute-start.1) | collective-permute-done | bytes 131104 | tf_op jit(solution)/shard_map/ppermute | solution.py:24
  17.8 0.0 collective-permute-done.refs_3_
  17.8 0.0 collective-permute-start.9
  17.8 3.0 %collective-permute-start.10 = (bf16[8,16,512]{2,1,0:T(8,128)(2,1)S(1)}, bf16[8,16,512]{2,1,0:T(8,128)(2,1)S(1)}, u32[]{:S(2)}, u32[]{:S(2)}) collective-permute-start(bf16[8,16,512]{2,1,0:T(8,128)(2,1)S(1)} %get-tuple-element.50), channel_id=1, source_target_pairs={{0,2},{1,3},{2,0},{3,1},{4,6},{5,7},{6,4},{7,5},{8,10},{9,11},{10,... | collective-permute-start | bytes 393224 | tf_op jit(solution)/shard_map/ppermute | solution.py:24
  20.8 1.3 %collective-permute-start.11 = (bf16[8,16,512]{2,1,0:T(8,128)(2,1)S(1)}, bf16[8,16,512]{2,1,0:T(8,128)(2,1)S(1)}, u32[]{:S(2)}, u32[]{:S(2)}) collective-permute-start(bf16[8,16,512]{2,1,0:T(8,128)(2,1)S(1)} %get-tuple-element.51), channel_id=1, source_target_pairs={{0,3},{1,2},{2,1},{3,0},{4,7},{5,6},{6,5},{7,4},{8,11},{9,10},{10,... | collective-permute-start | bytes 393224 | tf_op jit(solution)/shard_map/ppermute | solution.py:24
  22.1 0.6 pad_add_fusion.ids.refs_0_
  22.7 3.1 %plan.1 = (s32[29]{0:T(128)}, s32[24]{0:T(128)}) custom-call(s32[2]{0:T(128)} %pad_add_fusion.ids.refs_0_, s32[3,32]{1,0:T(4,128)} %src.1), custom_call_target="tpu_custom_call" | custom-call | tf_op jit(solution)/shard_map/plan/pallas_call | solution.py:58
  25.8 0.0 copy-start
  25.8 0.6 copy-done
  26.4 0.7 copy-done.2
  27.1 0.6 select.2
  27.7 0.1 collective-permute-start.3
  27.8 1.6 %collective-permute-start.4 = (bf16[7,16,512]{2,1,0:T(8,128)(2,1)S(1)}, bf16[7,16,512]{2,1,0:T(8,128)(2,1)S(1)}, u32[]{:S(2)}, u32[]{:S(2)}) collective-permute-start(bf16[7,16,512]{2,1,0:T(8,128)(2,1)S(1)} %get-tuple-element.42), channel_id=1, source_target_pairs={{0,8},{4,12},{8,0},{12,4},{1,9},{5,13},{9,1},{13,5},{2,10},{6,14},... | collective-permute-start | bytes 344072 | tf_op jit(solution)/shard_map/ppermute | solution.py:24
  29.4 0.0 collective-permute-done.9.refs_3_
  29.4 0.3 collective-permute-start.5
  29.7 0.6 collective-permute-done.10.refs_4_
  30.3 0.0 collective-permute-done.11.refs_5_
  30.3 0.6 select.3
  30.9 0.1 collective-permute-start.12
  31.0 1.6 %collective-permute-start.13 = (bf16[7,16,512]{2,1,0:T(8,128)(2,1)S(1)}, bf16[7,16,512]{2,1,0:T(8,128)(2,1)S(1)}, u32[]{:S(2)}, u32[]{:S(2)}) collective-permute-start(bf16[7,16,512]{2,1,0:T(8,128)(2,1)S(1)} %get-tuple-element.55), channel_id=1, source_target_pairs={{0,8},{4,12},{8,0},{12,4},{1,9},{5,13},{9,1},{13,5},{2,10},{6,14},... | collective-permute-start | bytes 344072 | tf_op jit(solution)/shard_map/ppermute | solution.py:24
  32.6 0.0 collective-permute-done.3.refs_5_
  32.6 0.3 collective-permute-start.14
  32.8 1.0 %collective-permute-done.4.refs_6_ = bf16[7,16,512]{2,1,0:T(8,128)(2,1)S(1)} collective-permute-done((bf16[7,16,512]{2,1,0:T(8,128)(2,1)S(1)}, bf16[7,16,512]{2,1,0:T(8,128)(2,1)S(1)}, u32[]{:S(2)}, u32[]{:S(2)}) %collective-permute-start.4) | collective-permute-done | bytes 114720 | tf_op jit(solution)/shard_map/ppermute | solution.py:24
  33.8 1.6 %collective-permute-done.5.refs_7_ = bf16[7,16,512]{2,1,0:T(8,128)(2,1)S(1)} collective-permute-done((bf16[7,16,512]{2,1,0:T(8,128)(2,1)S(1)}, bf16[7,16,512]{2,1,0:T(8,128)(2,1)S(1)}, u32[]{:S(2)}, u32[]{:S(2)}) %collective-permute-start.5) | collective-permute-done | bytes 114720 | tf_op jit(solution)/shard_map/ppermute | solution.py:24
  35.4 0.0 copy-done.3
  35.4 0.0 copy-done.12
  35.4 0.0 copy-done.14
  35.4 0.0 copy-done.13
  35.4 0.0 copy-start.1
  35.4 0.6 copy-done.1
  36.0 1.6 %copy-done.4 = bf16[2048,512]{1,0:T(8,128)(2,1)S(1)} copy-done((bf16[2048,512]{1,0:T(8,128)(2,1)S(1)}, bf16[2048,512]{1,0:T(8,128)(2,1)}, u32[]{:S(2)}) %copy-start.4) | copy-done | bytes 2097176
  37.6 1.0 %copy-done.5 = bf16[512,512]{1,0:T(8,128)(2,1)S(1)} copy-done((bf16[512,512]{1,0:T(8,128)(2,1)S(1)}, bf16[512,512]{1,0:T(8,128)(2,1)}, u32[]{:S(2)}) %copy-start.5) | copy-done | bytes 524312
  38.6 1.0 %copy-done.7 = bf16[512,512]{1,0:T(8,128)(2,1)S(1)} copy-done((bf16[512,512]{1,0:T(8,128)(2,1)S(1)}, bf16[512,512]{1,0:T(8,128)(2,1)}, u32[]{:S(2)}) %copy-start.7) | copy-done | bytes 524312
  39.7 1.0 %copy-done.9 = bf16[512,512]{1,0:T(8,128)(2,1)S(1)} copy-done((bf16[512,512]{1,0:T(8,128)(2,1)S(1)}, bf16[512,512]{1,0:T(8,128)(2,1)}, u32[]{:S(2)}) %copy-start.9) | copy-done | bytes 524312
  40.7 1.0 %copy-done.11 = bf16[512,512]{1,0:T(8,128)(2,1)S(1)} copy-done((bf16[512,512]{1,0:T(8,128)(2,1)S(1)}, bf16[512,512]{1,0:T(8,128)(2,1)}, u32[]{:S(2)}) %copy-start.11) | copy-done | bytes 524312
  41.8 0.7 copy-done.15
  42.4 6.8 %block.2 = (bf16[8,16,512]{2,1,0:T(8,128)(2,1)S(1)}, bf16[8,16,512]{2,1,0:T(8,128)(2,1)S(1)}, bf16[8,16,512]{2,1,0:T(8,128)(2,1)S(1)}, bf16[8,16,512]{2,1,0:T(8,128)(2,1)S(1)}) custom-call(s32[2]{0:T(128)S(1)} %copy-done.1, s32[24]{0:T(128)S(1)} %copy-done.15, s32[3,32]{1,0:T(4,128)S(1)} %copy-done.12, bf16[32,16,512]{2,1,0:T(8,128)(2,1)S(1)} %get-tuple-element.39.refs_3_, ...), custom_call_target="tpu_custom_call" | custom-call | flops 6400000000 | bytes 8388608 | tf_op jit(solution)/shard_map/block/pallas_call | solution.py:188
  49.3 0.1 collective-permute-start.6
  49.3 3.0 %collective-permute-start.7 = (bf16[8,16,512]{2,1,0:T(8,128)(2,1)S(1)}, bf16[8,16,512]{2,1,0:T(8,128)(2,1)S(1)}, u32[]{:S(2)}, u32[]{:S(2)}) collective-permute-start(bf16[8,16,512]{2,1,0:T(8,128)(2,1)S(1)} %get-tuple-element.46), channel_id=1, source_target_pairs={{0,2},{1,3},{2,0},{3,1},{4,6},{5,7},{6,4},{7,5},{8,10},{9,11},{10,... | collective-permute-start | bytes 393224 | tf_op jit(solution)/shard_map/ppermute | solution.py:24
  52.4 0.0 collective-permute-done.12.refs_5_
  52.4 1.4 %collective-permute-start.8 = (bf16[8,16,512]{2,1,0:T(8,128)(2,1)S(1)}, bf16[8,16,512]{2,1,0:T(8,128)(2,1)S(1)}, u32[]{:S(2)}, u32[]{:S(2)}) collective-permute-start(bf16[8,16,512]{2,1,0:T(8,128)(2,1)S(1)} %get-tuple-element.47), channel_id=1, source_target_pairs={{0,3},{1,2},{2,1},{3,0},{4,7},{5,6},{6,5},{7,4},{8,11},{9,10},{10,... | collective-permute-start | bytes 393224 | tf_op jit(solution)/shard_map/ppermute | solution.py:24
  53.7 0.0 collective-permute-done.13.refs_6_
  53.7 0.0 collective-permute-done.14.refs_7_
  53.7 0.0 copy-done.6
  53.7 0.0 copy-done.8
  53.7 0.0 copy-done.10
  53.7 6.9 %block.3 = (bf16[8,16,512]{2,1,0:T(8,128)(2,1)S(1)}, bf16[8,16,512]{2,1,0:T(8,128)(2,1)S(1)}, bf16[8,16,512]{2,1,0:T(8,128)(2,1)S(1)}, bf16[8,16,512]{2,1,0:T(8,128)(2,1)S(1)}) custom-call(s32[2]{0:T(128)S(1)} %copy-done.1, s32[24]{0:T(128)S(1)} %copy-done.15, s32[3,32]{1,0:T(4,128)S(1)} %copy-done.12, bf16[32,16,512]{2,1,0:T(8,128)(2,1)S(1)} %get-tuple-element.52.refs_3_, ...), custom_call_target="tpu_custom_call" | custom-call | flops 6400000000 | bytes 8388608 | tf_op jit(solution)/shard_map/block/pallas_call | solution.py:188
  60.6 0.1 collective-permute-start.15
  60.7 3.0 %collective-permute-start.16 = (bf16[8,16,512]{2,1,0:T(8,128)(2,1)S(1)}, bf16[8,16,512]{2,1,0:T(8,128)(2,1)S(1)}, u32[]{:S(2)}, u32[]{:S(2)}) collective-permute-start(bf16[8,16,512]{2,1,0:T(8,128)(2,1)S(1)} %get-tuple-element.59), channel_id=1, source_target_pairs={{0,2},{1,3},{2,0},{3,1},{4,6},{5,7},{6,4},{7,5},{8,10},{9,11},{10,... | collective-permute-start | bytes 393224 | tf_op jit(solution)/shard_map/ppermute | solution.py:24
  63.7 0.0 collective-permute-done.6.refs_2_
  63.7 1.4 %collective-permute-start.17 = (bf16[8,16,512]{2,1,0:T(8,128)(2,1)S(1)}, bf16[8,16,512]{2,1,0:T(8,128)(2,1)S(1)}, u32[]{:S(2)}, u32[]{:S(2)}) collective-permute-start(bf16[8,16,512]{2,1,0:T(8,128)(2,1)S(1)} %get-tuple-element.60), channel_id=1, source_target_pairs={{0,3},{1,2},{2,1},{3,0},{4,7},{5,6},{6,5},{7,4},{8,11},{9,10},{10,... | collective-permute-start | bytes 393224 | tf_op jit(solution)/shard_map/ppermute | solution.py:24
  65.1 0.0 collective-permute-done.7.refs_3_
  65.1 0.0 collective-permute-done.8.refs_4_
  65.1 2.8 %collective-permute-done.15.refs_6_ = bf16[8,16,512]{2,1,0:T(8,128)(2,1)S(1)} collective-permute-done((bf16[8,16,512]{2,1,0:T(8,128)(2,1)S(1)}, bf16[8,16,512]{2,1,0:T(8,128)(2,1)S(1)}, u32[]{:S(2)}, u32[]{:S(2)}) %collective-permute-start.15) | collective-permute-done | bytes 131104 | tf_op jit(solution)/shard_map/ppermute | solution.py:24
  67.9 5.9 %collective-permute-done.16.refs_7_ = bf16[8,16,512]{2,1,0:T(8,128)(2,1)S(1)} collective-permute-done((bf16[8,16,512]{2,1,0:T(8,128)(2,1)S(1)}, bf16[8,16,512]{2,1,0:T(8,128)(2,1)S(1)}, u32[]{:S(2)}, u32[]{:S(2)}) %collective-permute-start.16) | collective-permute-done | bytes 131104 | tf_op jit(solution)/shard_map/ppermute | solution.py:24
  73.8 0.0 collective-permute-done.17.refs_8_
  73.8 1.6 %assemble.1 = bf16[8,8,16,512]{3,2,1,0:T(8,128)(2,1)} custom-call(s32[2]{0:T(128)S(1)} %copy-done.1, bf16[8,16,512]{2,1,0:T(8,128)(2,1)S(1)} %get-tuple-element.44.refs_1_, bf16[8,16,512]{2,1,0:T(8,128)(2,1)S(1)} %collective-permute-done.6.refs_2_, bf16[8,16,512]{2,1,0:T(8,128)(2,1)S(1)} %collective-permute-done.7.refs_3_, ...), custom_call_target="tpu_custom_call" | custom-call | tf_op jit(solution)/shard_map/assemble/pallas_call | solution.py:228
  (12 shorter events, 0.0 us)
Async XLA Ops:
  0.0 35.4 %copy-start.3 = (bf16[512,2048]{1,0:T(8,128)(2,1)S(1)}, bf16[512,2048]{1,0:T(8,128)(2,1)}, u32[]{:S(2)}) copy-start(bf16[512,2048]{1,0:T(8,128)(2,1)} %refs_14_.3) | copy-start | bytes 6291460
  0.0 35.4 %copy-start.12 = (s32[3,32]{1,0:T(4,128)S(1)}, s32[3,32]{1,0:T(4,128)}, u32[]{:S(2)}) copy-start(s32[3,32]{1,0:T(4,128)} %refs_2_.3) | copy-start | bytes 1156
  0.0 35.4 %copy-start.14 = (f32[512]{0:T(512)S(1)}, f32[512]{0:T(512)}, u32[]{:S(2)}) copy-start(f32[512]{0:T(512)} %param.19) | copy-start | bytes 6148
  0.0 35.4 %copy-start.13 = (f32[512]{0:T(512)S(1)}, f32[512]{0:T(512)}, u32[]{:S(2)}) copy-start(f32[512]{0:T(512)} %param.14) | copy-start | bytes 6148
  1.5 9.6 %collective-permute-start.2 = (bf16[8,16,512]{2,1,0:T(8,128)(2,1)S(1)}, bf16[8,16,512]{2,1,0:T(8,128)(2,1)S(1)}, u32[]{:S(2)}, u32[]{:S(2)}) collective-permute-start(bf16[8,16,512]{2,1,0:T(8,128)(2,1)S(1)} %get-tuple-element.61), channel_id=1, source_target_pairs={{0,3},{1,2},{2,1},{3,0},{4,7},{5,6},{6,5},{7,4},{8,11},{9,10},{10,... | collective-permute-start | bytes 393224 | tf_op jit(solution)/shard_map/ppermute | solution.py:24
  6.7 11.1 %collective-permute-start.1 = (bf16[8,16,512]{2,1,0:T(8,128)(2,1)S(1)}, bf16[8,16,512]{2,1,0:T(8,128)(2,1)S(1)}, u32[]{:S(2)}, u32[]{:S(2)}) collective-permute-start(bf16[8,16,512]{2,1,0:T(8,128)(2,1)S(1)} %get-tuple-element.62), channel_id=1, source_target_pairs={{0,2},{1,3},{2,0},{3,1},{4,6},{5,7},{6,4},{7,5},{8,10},{9,11},{10,... | collective-permute-start | bytes 393224 | tf_op jit(solution)/shard_map/ppermute | solution.py:24
  6.7 11.1 %collective-permute-start = (bf16[8,16,512]{2,1,0:T(8,128)(2,1)S(1)}, bf16[8,16,512]{2,1,0:T(8,128)(2,1)S(1)}, u32[]{:S(2)}, u32[]{:S(2)}) collective-permute-start(bf16[8,16,512]{2,1,0:T(8,128)(2,1)S(1)} %get-tuple-element.63), channel_id=1, source_target_pairs={{0,1},{1,0},{2,3},{3,2},{4,5},{5,4},{6,7},{7,6},{8,9},{9,8},{10,11... | collective-permute-start | bytes 393224 | tf_op jit(solution)/shard_map/ppermute | solution.py:24
  17.8 11.6 %collective-permute-start.9 = (bf16[8,16,512]{2,1,0:T(8,128)(2,1)S(1)}, bf16[8,16,512]{2,1,0:T(8,128)(2,1)S(1)}, u32[]{:S(2)}, u32[]{:S(2)}) collective-permute-start(bf16[8,16,512]{2,1,0:T(8,128)(2,1)S(1)} %get-tuple-element.49), channel_id=1, source_target_pairs={{0,1},{1,0},{2,3},{3,2},{4,5},{5,4},{6,7},{7,6},{8,9},{9,8},{10,11... | collective-permute-start | bytes 393224 | tf_op jit(solution)/shard_map/ppermute | solution.py:24
  17.8 12.5 %collective-permute-start.10 = (bf16[8,16,512]{2,1,0:T(8,128)(2,1)S(1)}, bf16[8,16,512]{2,1,0:T(8,128)(2,1)S(1)}, u32[]{:S(2)}, u32[]{:S(2)}) collective-permute-start(bf16[8,16,512]{2,1,0:T(8,128)(2,1)S(1)} %get-tuple-element.50), channel_id=1, source_target_pairs={{0,2},{1,3},{2,0},{3,1},{4,6},{5,7},{6,4},{7,5},{8,10},{9,11},{10,... | collective-permute-start | bytes 393224 | tf_op jit(solution)/shard_map/ppermute | solution.py:24
  20.8 9.5 %collective-permute-start.11 = (bf16[8,16,512]{2,1,0:T(8,128)(2,1)S(1)}, bf16[8,16,512]{2,1,0:T(8,128)(2,1)S(1)}, u32[]{:S(2)}, u32[]{:S(2)}) collective-permute-start(bf16[8,16,512]{2,1,0:T(8,128)(2,1)S(1)} %get-tuple-element.51), channel_id=1, source_target_pairs={{0,3},{1,2},{2,1},{3,0},{4,7},{5,6},{6,5},{7,4},{8,11},{9,10},{10,... | collective-permute-start | bytes 393224 | tf_op jit(solution)/shard_map/ppermute | solution.py:24
  25.8 0.6 copy-start
  26.4 0.7 copy-start.2
  27.7 4.8 %collective-permute-start.3 = (bf16[7,16,512]{2,1,0:T(8,128)(2,1)S(1)}, bf16[7,16,512]{2,1,0:T(8,128)(2,1)S(1)}, u32[]{:S(2)}, u32[]{:S(2)}) collective-permute-start(bf16[7,16,512]{2,1,0:T(8,128)(2,1)S(1)} %get-tuple-element.41), channel_id=1, source_target_pairs={{0,4},{4,0},{8,12},{12,8},{1,5},{5,1},{9,13},{13,9},{2,6},{6,2},{1... | collective-permute-start | bytes 344072 | tf_op jit(solution)/shard_map/ppermute | solution.py:24
  27.8 6.0 %collective-permute-start.4 = (bf16[7,16,512]{2,1,0:T(8,128)(2,1)S(1)}, bf16[7,16,512]{2,1,0:T(8,128)(2,1)S(1)}, u32[]{:S(2)}, u32[]{:S(2)}) collective-permute-start(bf16[7,16,512]{2,1,0:T(8,128)(2,1)S(1)} %get-tuple-element.42), channel_id=1, source_target_pairs={{0,8},{4,12},{8,0},{12,4},{1,9},{5,13},{9,1},{13,5},{2,10},{6,14},... | collective-permute-start | bytes 344072 | tf_op jit(solution)/shard_map/ppermute | solution.py:24
  29.4 6.0 %collective-permute-start.5 = (bf16[7,16,512]{2,1,0:T(8,128)(2,1)S(1)}, bf16[7,16,512]{2,1,0:T(8,128)(2,1)S(1)}, u32[]{:S(2)}, u32[]{:S(2)}) collective-permute-start(bf16[7,16,512]{2,1,0:T(8,128)(2,1)S(1)} %get-tuple-element.43), channel_id=1, source_target_pairs={{0,12},{4,8},{8,4},{12,0},{1,13},{5,9},{9,5},{13,1},{2,14},{6,10},... | collective-permute-start | bytes 344072 | tf_op jit(solution)/shard_map/ppermute | solution.py:24
  30.9 21.4 %collective-permute-start.12 = (bf16[7,16,512]{2,1,0:T(8,128)(2,1)S(1)}, bf16[7,16,512]{2,1,0:T(8,128)(2,1)S(1)}, u32[]{:S(2)}, u32[]{:S(2)}) collective-permute-start(bf16[7,16,512]{2,1,0:T(8,128)(2,1)S(1)} %get-tuple-element.54), channel_id=1, source_target_pairs={{0,4},{4,0},{8,12},{12,8},{1,5},{5,1},{9,13},{13,9},{2,6},{6,2},{1... | collective-permute-start | bytes 344072 | tf_op jit(solution)/shard_map/ppermute | solution.py:24
  31.0 22.7 %collective-permute-start.13 = (bf16[7,16,512]{2,1,0:T(8,128)(2,1)S(1)}, bf16[7,16,512]{2,1,0:T(8,128)(2,1)S(1)}, u32[]{:S(2)}, u32[]{:S(2)}) collective-permute-start(bf16[7,16,512]{2,1,0:T(8,128)(2,1)S(1)} %get-tuple-element.55), channel_id=1, source_target_pairs={{0,8},{4,12},{8,0},{12,4},{1,9},{5,13},{9,1},{13,5},{2,10},{6,14},... | collective-permute-start | bytes 344072 | tf_op jit(solution)/shard_map/ppermute | solution.py:24
  32.6 21.1 %collective-permute-start.14 = (bf16[7,16,512]{2,1,0:T(8,128)(2,1)S(1)}, bf16[7,16,512]{2,1,0:T(8,128)(2,1)S(1)}, u32[]{:S(2)}, u32[]{:S(2)}) collective-permute-start(bf16[7,16,512]{2,1,0:T(8,128)(2,1)S(1)} %get-tuple-element.56), channel_id=1, source_target_pairs={{0,12},{4,8},{8,4},{12,0},{1,13},{5,9},{9,5},{13,1},{2,14},{6,10},... | collective-permute-start | bytes 344072 | tf_op jit(solution)/shard_map/ppermute | solution.py:24
  35.4 0.6 copy-start.1
  36.0 1.6 %copy-start.4 = (bf16[2048,512]{1,0:T(8,128)(2,1)S(1)}, bf16[2048,512]{1,0:T(8,128)(2,1)}, u32[]{:S(2)}) copy-start(bf16[2048,512]{1,0:T(8,128)(2,1)} %refs_15_.3) | copy-start | bytes 6291460
  37.6 1.0 %copy-start.5 = (bf16[512,512]{1,0:T(8,128)(2,1)S(1)}, bf16[512,512]{1,0:T(8,128)(2,1)}, u32[]{:S(2)}) copy-start(bf16[512,512]{1,0:T(8,128)(2,1)} %refs_9_.3) | copy-start | bytes 1572868
  38.6 1.0 %copy-start.7 = (bf16[512,512]{1,0:T(8,128)(2,1)S(1)}, bf16[512,512]{1,0:T(8,128)(2,1)}, u32[]{:S(2)}) copy-start(bf16[512,512]{1,0:T(8,128)(2,1)} %refs_10_.3) | copy-start | bytes 1572868
  39.7 1.0 %copy-start.9 = (bf16[512,512]{1,0:T(8,128)(2,1)S(1)}, bf16[512,512]{1,0:T(8,128)(2,1)}, u32[]{:S(2)}) copy-start(bf16[512,512]{1,0:T(8,128)(2,1)} %refs_11_.3) | copy-start | bytes 1572868
  40.7 1.0 %copy-start.11 = (bf16[512,512]{1,0:T(8,128)(2,1)S(1)}, bf16[512,512]{1,0:T(8,128)(2,1)}, u32[]{:S(2)}) copy-start(bf16[512,512]{1,0:T(8,128)(2,1)} %refs_12_.3) | copy-start | bytes 1572868
  41.8 0.7 copy-start.15
  42.4 11.3 %copy-start.6 = (bf16[512,512]{1,0:T(8,128)(2,1)S(1)}, bf16[512,512]{1,0:T(8,128)(2,1)}, u32[]{:S(2)}) copy-start(bf16[512,512]{1,0:T(8,128)(2,1)} %refs_9_.3) | copy-start | bytes 1572868
  42.4 11.3 %copy-start.8 = (bf16[512,512]{1,0:T(8,128)(2,1)S(1)}, bf16[512,512]{1,0:T(8,128)(2,1)}, u32[]{:S(2)}) copy-start(bf16[512,512]{1,0:T(8,128)(2,1)} %refs_10_.3) | copy-start | bytes 1572868
  42.4 11.3 %copy-start.10 = (bf16[512,512]{1,0:T(8,128)(2,1)S(1)}, bf16[512,512]{1,0:T(8,128)(2,1)}, u32[]{:S(2)}) copy-start(bf16[512,512]{1,0:T(8,128)(2,1)} %refs_11_.3) | copy-start | bytes 1572868
  49.3 14.5 %collective-permute-start.6 = (bf16[8,16,512]{2,1,0:T(8,128)(2,1)S(1)}, bf16[8,16,512]{2,1,0:T(8,128)(2,1)S(1)}, u32[]{:S(2)}, u32[]{:S(2)}) collective-permute-start(bf16[8,16,512]{2,1,0:T(8,128)(2,1)S(1)} %get-tuple-element.45), channel_id=1, source_target_pairs={{0,1},{1,0},{2,3},{3,2},{4,5},{5,4},{6,7},{7,6},{8,9},{9,8},{10,11... | collective-permute-start | bytes 393224 | tf_op jit(solution)/shard_map/ppermute | solution.py:24
  49.3 15.7 %collective-permute-start.7 = (bf16[8,16,512]{2,1,0:T(8,128)(2,1)S(1)}, bf16[8,16,512]{2,1,0:T(8,128)(2,1)S(1)}, u32[]{:S(2)}, u32[]{:S(2)}) collective-permute-start(bf16[8,16,512]{2,1,0:T(8,128)(2,1)S(1)} %get-tuple-element.46), channel_id=1, source_target_pairs={{0,2},{1,3},{2,0},{3,1},{4,6},{5,7},{6,4},{7,5},{8,10},{9,11},{10,... | collective-permute-start | bytes 393224 | tf_op jit(solution)/shard_map/ppermute | solution.py:24
  52.4 12.7 %collective-permute-start.8 = (bf16[8,16,512]{2,1,0:T(8,128)(2,1)S(1)}, bf16[8,16,512]{2,1,0:T(8,128)(2,1)S(1)}, u32[]{:S(2)}, u32[]{:S(2)}) collective-permute-start(bf16[8,16,512]{2,1,0:T(8,128)(2,1)S(1)} %get-tuple-element.47), channel_id=1, source_target_pairs={{0,3},{1,2},{2,1},{3,0},{4,7},{5,6},{6,5},{7,4},{8,11},{9,10},{10,... | collective-permute-start | bytes 393224 | tf_op jit(solution)/shard_map/ppermute | solution.py:24
  60.6 7.3 %collective-permute-start.15 = (bf16[8,16,512]{2,1,0:T(8,128)(2,1)S(1)}, bf16[8,16,512]{2,1,0:T(8,128)(2,1)S(1)}, u32[]{:S(2)}, u32[]{:S(2)}) collective-permute-start(bf16[8,16,512]{2,1,0:T(8,128)(2,1)S(1)} %get-tuple-element.58), channel_id=1, source_target_pairs={{0,1},{1,0},{2,3},{3,2},{4,5},{5,4},{6,7},{7,6},{8,9},{9,8},{10,11... | collective-permute-start | bytes 393224 | tf_op jit(solution)/shard_map/ppermute | solution.py:24
  60.7 13.1 %collective-permute-start.16 = (bf16[8,16,512]{2,1,0:T(8,128)(2,1)S(1)}, bf16[8,16,512]{2,1,0:T(8,128)(2,1)S(1)}, u32[]{:S(2)}, u32[]{:S(2)}) collective-permute-start(bf16[8,16,512]{2,1,0:T(8,128)(2,1)S(1)} %get-tuple-element.59), channel_id=1, source_target_pairs={{0,2},{1,3},{2,0},{3,1},{4,6},{5,7},{6,4},{7,5},{8,10},{9,11},{10,... | collective-permute-start | bytes 393224 | tf_op jit(solution)/shard_map/ppermute | solution.py:24
  63.7 10.0 %collective-permute-start.17 = (bf16[8,16,512]{2,1,0:T(8,128)(2,1)S(1)}, bf16[8,16,512]{2,1,0:T(8,128)(2,1)S(1)}, u32[]{:S(2)}, u32[]{:S(2)}) collective-permute-start(bf16[8,16,512]{2,1,0:T(8,128)(2,1)S(1)} %get-tuple-element.60), channel_id=1, source_target_pairs={{0,3},{1,2},{2,1},{3,0},{4,7},{5,6},{6,5},{7,4},{8,11},{9,10},{10,... | collective-permute-start | bytes 393224 | tf_op jit(solution)/shard_map/ppermute | solution.py:24

commit v2 on v1

v2 whole, which is shorter than its diff:
```python
import functools

import jax
import jax.numpy as jnp
from jax import lax
from jax.experimental import pallas as pl
from jax.experimental.pallas import tpu as pltpu
from jax.sharding import PartitionSpec as P

HD = 64
ROW_TILE = 16
BLOCK_FF = 512

VMEM = pltpu.VMEM
SMEM = pltpu.SMEM


def spec(space):
    return pl.BlockSpec(memory_space=space)


def exchange(values, axis, step):
    size = lax.axis_size(axis)
    return lax.ppermute(values, axis, [(i, i ^ step) for i in range(size)])


def pinned(values, space):
    return [pltpu.with_memory_space_constraint(v, space) for v in values]


class Layout:
    def __init__(self, frames, bricks, spaces, cap):
        self.frames, self.bricks, self.spaces, self.cap = frames, bricks, spaces, cap
        self.requests = (frames - 1) * bricks
        self.send = 2
        self.take = self.send + spaces * cap + 1
        self.weight = self.take + self.requests
        self.size = self.weight + self.requests


def prepare_kernel(lay, ids, src, merge_num, *refs):
    count = refs[-2]
    sems = refs[-1]
    half = (len(refs) - 3) // 2
    stored, table, loaded = refs[:half], refs[half], refs[half + 1 : -2]
    loads = [
        pltpu.make_async_copy(stored[i], loaded[i], sems.at[i]) for i in range(half)
    ]
    for load in loads:
        load.start()
    bricks, cap = lay.bricks, lay.cap
    me = ids[0]
    table[0] = me
    table[1] = ids[1]
    for owner in range(lay.spaces):
        count[owner] = 0

    def one_request(q, carry):
        frame, brick = lax.div(q, bricks), me * bricks + lax.rem(q, bricks)
        owner = lax.div(src[frame, brick], bricks)
        rank = count[owner]
        table[lay.take + q] = (owner ^ me) * cap + rank
        table[lay.weight + q] = merge_num[frame, brick]
        count[owner] = rank + 1
        return carry

    lax.fori_loop(0, lay.requests, one_request, 0)

    for j in range(lay.spaces):
        target = me ^ j

        def one_send(q, filled, target=target, j=j):
            frame = lax.div(q, bricks)
            source = src[frame, target * bricks + lax.rem(q, bricks)]
            owner = lax.div(source, bricks)
            table[lay.send + j * cap + filled] = frame * bricks + lax.rem(source, bricks)
            return filled + (owner == me).astype(jnp.int32)

        lax.fori_loop(0, lay.requests, one_send, 0)
    for load in loads:
        load.wait()


def prepare(lay, ids, src_brick, merge_num, weights):
    return pl.pallas_call(
        functools.partial(prepare_kernel, lay),
        out_shape=(pltpu.SMEM((lay.size,), jnp.int32),)
        + tuple(pltpu.VMEM(w.shape, w.dtype) for w in weights),
        in_specs=[spec(SMEM)] * 3 + [spec(pltpu.HBM)] * len(weights),
        out_specs=(spec(SMEM),) + (spec(VMEM),) * len(weights),
        scratch_shapes=[
            SMEM((lay.spaces,), jnp.int32),
            pltpu.SemaphoreType.DMA((len(weights),)),
        ],
        compiler_params=pltpu.CompilerParams(vmem_limit_bytes=1 << 20),
        name="prepare",
    )(ids, src_brick, merge_num, *pinned(weights, pltpu.HBM))


def select_kernel(lay, *refs):
    frames = lay.frames
    table = refs[0]
    parts = refs[1 : 1 + frames]
    stacked = refs[1 + frames]
    outs = refs[2 + frames :]
    mine = table[1]
    for k in range(frames):
        stacked[pl.ds((mine ^ k) * lay.bricks, lay.bricks)] = parts[k][...]
    for j in list(range(1, lay.spaces)) + [0]:
        for m in range(lay.cap):
            outs[j][m] = stacked[table[lay.send + j * lay.cap + m]]


def select(lay, table, parts):
    bricks, rows, width = parts[0].shape
    dtype = parts[0].dtype
    return pl.pallas_call(
        functools.partial(select_kernel, lay),
        out_shape=(jax.ShapeDtypeStruct((lay.frames * bricks, rows, width), dtype),)
        + (jax.ShapeDtypeStruct((lay.cap, rows, width), dtype),) * lay.spaces,
        in_specs=[spec(SMEM)] + [spec(VMEM)] * lay.frames,
        out_specs=(spec(VMEM),) * (1 + lay.spaces),
        compiler_params=pltpu.CompilerParams(vmem_limit_bytes=4 << 20),
        name="select",
    )(*pinned([table], SMEM), *parts)


def normalise(values, gain):
    wide = values.astype(jnp.float32)
    mean_sq = jnp.mean(wide * wide, axis=-1, keepdims=True)
    return (wide * lax.rsqrt(mean_sq + 1e-06) * gain).astype(jnp.bfloat16)


def matmul(a, b):
    return jnp.dot(a, b, preferred_element_type=jnp.float32)


def block_kernel(lay, *refs):
    frames, bricks, cap, spaces = lay.frames, lay.bricks, lay.cap, lay.spaces
    table, stacked = refs[:2]
    pieces = refs[2 : 2 + spaces]
    gain_a, gain_m, w_q, w_k, w_v, w_o, w_in, w_back = refs[2 + spaces : 10 + spaces]
    outs = refs[10 + spaces : 10 + spaces + frames]
    slots, merged, hidden, result = refs[10 + spaces + frames :]
    rows, width = stacked.shape[1:]
    per_frame = bricks * rows
    for j in range(spaces):
        slots[j * cap : (j + 1) * cap] = pieces[j][...]
    for b in range(bricks):
        merged[b * rows : (b + 1) * rows] = stacked[b]
    for f in range(1, frames):
        for b in range(bricks):
            q = (f - 1) * bricks + b
            weight = table[lay.weight + q].astype(jnp.float32) * 0.25
            piece = slots[table[lay.take + q]].astype(jnp.float32)
            at = f * per_frame + b * rows
            merged[at : at + rows] = (
                stacked[f * bricks + b].astype(jnp.float32) + weight * piece
            ).astype(jnp.bfloat16)
    normed = normalise(merged[...], gain_a[...])
    queries = matmul(normed, w_q[...]).astype(jnp.bfloat16)
    keys = matmul(normed, w_k[...]).astype(jnp.bfloat16)
    vals = matmul(normed, w_v[...]).astype(jnp.bfloat16)

    def frame_of(x, f):
        return x[f * per_frame : (f + 1) * per_frame]

    lanes = 128
    head_of = lax.broadcasted_iota(jnp.int32, (width, lanes), 0) // HD
    gather_heads = (head_of == lax.broadcasted_iota(jnp.int32, (width, lanes), 1)).astype(
        jnp.bfloat16
    )
    head_to = lax.broadcasted_iota(jnp.int32, (lanes, width), 1) // HD
    spread_heads = (head_to == lax.broadcasted_iota(jnp.int32, (lanes, width), 0)).astype(
        jnp.bfloat16
    )
    for f in range(frames):
        query = frame_of(queries, f).astype(jnp.float32)
        scores = []
        for g in range(f + 1):
            product = query * frame_of(keys, g).astype(jnp.float32)
            high = product.astype(jnp.bfloat16)
            low = (product - high.astype(jnp.float32)).astype(jnp.bfloat16)
            scores.append(
                (matmul(high, gather_heads) + matmul(low, gather_heads)) * (1.0 / HD**0.5)
            )
        top = functools.reduce(jnp.maximum, scores)
        exps = [jnp.exp(s - top) for s in scores]
        total = functools.reduce(jnp.add, exps)
        context = None
        for g in range(f + 1):
            prob = (exps[g] / total).astype(jnp.bfloat16)
            term = matmul(prob, spread_heads) * frame_of(vals, g).astype(jnp.float32)
            context = term if context is None else context + term
        hidden[f * per_frame : (f + 1) * per_frame] = context.astype(jnp.bfloat16)
    mid = (merged[...].astype(jnp.float32) + matmul(hidden[...], w_o[...])).astype(jnp.bfloat16)
    normed2 = normalise(mid, gain_m[...])
    total = mid.astype(jnp.float32)
    depth = w_in.shape[1]
    step = min(BLOCK_FF, depth)
    for at in range(0, depth, step):
        part = jax.nn.gelu(matmul(normed2, w_in[:, at : at + step])).astype(jnp.bfloat16)
        total = total + matmul(part, w_back[at : at + step])
    result[...] = total.astype(jnp.bfloat16).reshape(result.shape)
    mine = table[1]
    for k in range(frames):
        outs[k][...] = result[pl.ds((mine ^ k) * bricks, bricks)]


def run_block(lay, table, stacked, pieces, gains, weights):
    total, rows, width = stacked.shape
    dtype = stacked.dtype
    return pl.pallas_call(
        functools.partial(block_kernel, lay),
        out_shape=(jax.ShapeDtypeStruct((lay.bricks, rows, width), dtype),) * lay.frames,
        in_specs=[spec(SMEM)]
        + [spec(VMEM)] * (1 + lay.spaces + len(gains) + len(weights)),
        out_specs=(spec(VMEM),) * lay.frames,
        scratch_shapes=[
            VMEM((lay.spaces * lay.cap, rows, width), dtype),
            VMEM((total * rows, width), dtype),
            VMEM((total * rows, width), dtype),
            VMEM((total, rows, width), dtype),
        ],
        compiler_params=pltpu.CompilerParams(vmem_limit_bytes=20 << 20),
        name="block",
    )(*pinned([table], SMEM), stacked, *pieces, *gains, *pinned(weights, VMEM))


def assemble_kernel(count, mine_at, *refs):
    table = refs[0]
    parts = refs[1 : 1 + count]
    out, sems = refs[1 + count :]
    copies = [
        pltpu.make_async_copy(parts[i], out.at[:, mine_at(i, table[1])], sems.at[i])
        for i in range(count)
    ]
    for copy in copies:
        copy.start()
    for copy in copies:
        copy.wait()


def assemble(table, parts, frames):
    count = len(parts)
    bricks, rows, width = parts[0].shape

    def mine_at(i, mine):
        return i // frames * frames + (mine ^ (i % frames))

    return pl.pallas_call(
        functools.partial(assemble_kernel, count, mine_at),
        out_shape=jax.ShapeDtypeStruct((bricks, count, rows, width), parts[0].dtype),
        in_specs=[spec(SMEM)] + [spec(VMEM)] * count,
        out_specs=spec(pl.ANY),
        scratch_shapes=[pltpu.SemaphoreType.DMA((count,))],
        compiler_params=pltpu.CompilerParams(vmem_limit_bytes=4 << 20),
        name="assemble",
    )(*pinned([table], SMEM), *parts)


def local(tokens, src_brick, merge_num, gain_attn, w_q, w_k, w_v, w_out, gain_mlp, w_in, w_back):
    frames = lax.axis_size("frame")
    spaces = lax.axis_size("space")
    _, bricks, tall, width = tokens.shape
    cap = max(2, (frames - 1) * bricks // spaces + 1)
    chunks = max(1, tall // frames // ROW_TILE)
    rows = tall // frames // chunks
    mine = lax.axis_index("frame")
    ids = jnp.stack([lax.axis_index("space"), mine]).astype(jnp.int32)
    cut = tokens.reshape(bricks, chunks * frames, rows, width)
    lay = Layout(frames, bricks, spaces, cap)
    gains = (gain_attn[None], gain_mlp[None])
    weights = (w_q, w_k, w_v, w_out, w_in, w_back)

    def across(parts, axis):
        return [exchange(part, axis, k) for k, part in enumerate(parts, 1)]

    parts = [
        [
            lax.dynamic_index_in_dim(cut, c * frames + (mine ^ k), 1, keepdims=False)
            for k in range(frames)
        ]
        for c in range(chunks)
    ]
    (src_brick, merge_num), parts = lax.optimization_barrier(((src_brick, merge_num), parts))
    arrived = [across(parts[0][1:], "frame")]
    table, *weights = prepare(lay, ids, src_brick, merge_num, weights)
    for c in range(1, chunks):
        leaving, table, arrived[-1][0] = lax.optimization_barrier(
            (parts[c][1:], table, arrived[-1][0])
        )
        arrived.append(across(leaving, "frame"))
    back = []
    for c in range(chunks):
        stacked, *slots = select(lay, table, [parts[c][0]] + arrived[c])
        pieces = [slots[0]] + across(slots[1:], "space")
        done = run_block(lay, table, stacked, pieces, gains, weights)
        if c + 1 < chunks:
            arrived[c + 1], done = lax.optimization_barrier((arrived[c + 1], done))
        back += [done[0]] + across(done[1:], "frame")
    out = assemble(table, back, frames)
    return out.reshape(1, bricks, tall, width)


def solution(mesh):
    tokens = P("frame", ("groups", "space"), None, None)
    tables = P(None, "groups")
    in_specs = (tokens, tables, tables) + (P(),) * 8
    return jax.shard_map(local, mesh=mesh, in_specs=in_specs, out_specs=tokens, check_vma=False)
```

time: 75.7 us -> 65.2 us (0.86)
  local copies, waits for them, and re-layouts: 9.81 us -> 1.43 us
  Pallas kernels: 19.6 us -> 17.1 us
  waiting for transfers between devices: 22.3 us -> 23.7 us
    unnamed x32 -> x8, local copies, waits for them, and re-layouts: 8.3 us -> 0.01 us
    pallas_call x5, Pallas kernels: 18 us -> 16.1 us  [the longest x2 12.4 us: run_block(): pl.pallas_call(functools.partial(block_kernel, lay), out_shape=(jax.Shape...]
    ppermute x18, waiting for transfers between devices: 22.3 us -> 23.7 us  [exchange(): return lax.ppermute(values, axis, [(i, i ^ step) for i in range(size)])]
  transfers between devices with their start and end apart: 18 -> 18, of which waited for: 7 -> 7; matrix products, arithmetic and copies ran while one was open for 1% -> 0% of each run, Pallas kernels for 24% -> 25%
where the time goes in v2:
time: 65.2 us; the launch traced here: 65 us
  waiting for transfers between devices  23.7 us (36%)
  starting transfers between devices  22.6 us (35%)
  Pallas kernels  17.1 us (26%)
  local copies, waits for them, and re-layouts  1.43 us (2%)
    ppermute x18, waiting for transfers between devices, exchange(): return lax.ppermute(values, axis, [(i, i ^ step) for i in range(size)])  23.7 us
    ppermute x18, starting transfers between devices, exchange(): return lax.ppermute(values, axis, [(i, i ^ step) for i in range(size)])  22.6 us
    pallas_call x2, Pallas kernels, run_block(): pl.pallas_call(functools.partial(block_kernel, lay), out_shape=(jax.Shape...  12.4 us
    pallas_call x1, Pallas kernels, prepare(): pl.pallas_call(functools.partial(prepare_kernel, lay), out_shape=(pltpu.S...  3.54 us
    squeeze x1, local copies, waits for them, and re-layouts, local(): lax.dynamic_index_in_dim(cut, c * frames + (mine ^ k), 1, keepdims=False)  1.41 us
  transfers between devices with their start and end apart: 18, of which 7 were waited for; matrix products, arithmetic and copies ran while one was open for 0% of the time, Pallas kernels for 25%

profile of v2, /device:TPU:0, one launch (start us, length us, event | category | flops | bytes accessed | tf_op | source)
XLA Modules:
  0.0 65.0 jit_solution(7943223556918860835)
XLA Ops:
  0.0 0.0 copy-start.3
  0.0 0.0 copy-start.2
  0.0 1.4 %dynamic-slice_bitcast_fusion = (bf16[8,16,512]{2,1,0:T(8,128)(2,1)S(1)}, bf16[8,16,512]{2,1,0:T(8,128)(2,1)S(1)}, bf16[8,16,512]{2,1,0:T(8,128)(2,1)S(1)}, bf16...) fusion(bf16[8,8,16,512]{3,2,1,0:T(8,128)(2,1)} %bitcast.42, ...), kind=kLoop, calls=%fused_computation | loop fusion | bytes 2097184 | tf_op jit(solution)/shard_map/jit(dynamic_index_in_dim)/squeeze | solution.py:281
  1.4 3.1 %collective-permute-start = (bf16[8,16,512]{2,1,0:T(8,128)(2,1)S(1)}, bf16[8,16,512]{2,1,0:T(8,128)(2,1)S(1)}, u32[]{:S(2)}, u32[]{:S(2)}) collective-permute-start(bf16[8,16,512]{2,1,0:T(8,128)(2,1)S(1)} %get-tuple-element.58), channel_id=1, source_target_pairs={{0,1},{1,0},{2,3},{3,2},{4,5},{5,4},{6,7},{7,6},{8,9},{9,8},{10,11... | collective-permute-start | bytes 393224 | tf_op jit(solution)/shard_map/ppermute | solution.py:24
  4.5 2.6 %collective-permute-start.4 = (bf16[8,16,512]{2,1,0:T(8,128)(2,1)S(1)}, bf16[8,16,512]{2,1,0:T(8,128)(2,1)S(1)}, u32[]{:S(2)}, u32[]{:S(2)}) collective-permute-start(bf16[8,16,512]{2,1,0:T(8,128)(2,1)S(1)} %get-tuple-element.65), channel_id=1, source_target_pairs={{0,2},{1,3},{2,0},{3,1},{4,6},{5,7},{6,4},{7,5},{8,10},{9,11},{10,... | collective-permute-start | bytes 393224 | tf_op jit(solution)/shard_map/ppermute | solution.py:24
  7.1 0.0 collective-permute-start.5
  7.1 0.1 pad_add_fusion.ids
  7.2 0.0 copy-done.3
  7.2 0.0 copy-done.2
  7.2 0.0 copy-start
  7.2 0.0 copy-start.1
  7.2 3.5 %prepare.1 = (s32[79]{0:T(128)S(4)}, bf16[512,512]{1,0:T(8,128)(2,1)S(1)}, bf16[512,512]{1,0:T(8,128)(2,1)S(1)}, bf16[512,512]{1,0:T(8,128)(2,1)S(1)}, bf16[512,...) custom-call(s32[2]{0:T(128)S(1)} %pad_add_fusion.ids, s32[3,32]{1,0:T(4,128)S(1)} %copy-done.2, ...), custom_call_target="tpu_custom_call" | custom-call | tf_op jit(solution)/shard_map/prepare/pallas_call | solution.py:85
  10.7 0.0 collective-permute-done.refs_2_
  10.8 6.7 %collective-permute-done.4.refs_3_ = bf16[8,16,512]{2,1,0:T(8,128)(2,1)S(1)} collective-permute-done((bf16[8,16,512]{2,1,0:T(8,128)(2,1)S(1)}, bf16[8,16,512]{2,1,0:T(8,128)(2,1)S(1)}, u32[]{:S(2)}, u32[]{:S(2)}) %collective-permute-start.4) | collective-permute-done | bytes 131104 | tf_op jit(solution)/shard_map/ppermute | solution.py:24
  17.4 0.0 collective-permute-done.5.refs_4_
  17.4 0.1 select.2
  17.5 0.1 collective-permute-start.6
  17.6 2.0 %collective-permute-start.1 = (bf16[8,16,512]{2,1,0:T(8,128)(2,1)S(1)}, bf16[8,16,512]{2,1,0:T(8,128)(2,1)S(1)}, u32[]{:S(2)}, u32[]{:S(2)}) collective-permute-start(bf16[8,16,512]{2,1,0:T(8,128)(2,1)S(1)} %get-tuple-element.60), channel_id=1, source_target_pairs={{0,1},{1,0},{2,3},{3,2},{4,5},{5,4},{6,7},{7,6},{8,9},{9,8},{10,11... | collective-permute-start | bytes 393224 | tf_op jit(solution)/shard_map/ppermute | solution.py:24
  19.6 1.1 %collective-permute-start.2 = (bf16[8,16,512]{2,1,0:T(8,128)(2,1)S(1)}, bf16[8,16,512]{2,1,0:T(8,128)(2,1)S(1)}, u32[]{:S(2)}, u32[]{:S(2)}) collective-permute-start(bf16[8,16,512]{2,1,0:T(8,128)(2,1)S(1)} %get-tuple-element.61), channel_id=1, source_target_pairs={{0,2},{1,3},{2,0},{3,1},{4,6},{5,7},{6,4},{7,5},{8,10},{9,11},{10,... | collective-permute-start | bytes 393224 | tf_op jit(solution)/shard_map/ppermute | solution.py:24
  20.7 1.4 %collective-permute-start.3 = (bf16[8,16,512]{2,1,0:T(8,128)(2,1)S(1)}, bf16[8,16,512]{2,1,0:T(8,128)(2,1)S(1)}, u32[]{:S(2)}, u32[]{:S(2)}) collective-permute-start(bf16[8,16,512]{2,1,0:T(8,128)(2,1)S(1)} %get-tuple-element.62), channel_id=1, source_target_pairs={{0,3},{1,2},{2,1},{3,0},{4,7},{5,6},{6,5},{7,4},{8,11},{9,10},{10,... | collective-permute-start | bytes 393224 | tf_op jit(solution)/shard_map/ppermute | solution.py:24
  22.1 1.5 %collective-permute-start.7 = (bf16[7,16,512]{2,1,0:T(8,128)(2,1)S(1)}, bf16[7,16,512]{2,1,0:T(8,128)(2,1)S(1)}, u32[]{:S(2)}, u32[]{:S(2)}) collective-permute-start(bf16[7,16,512]{2,1,0:T(8,128)(2,1)S(1)} %get-tuple-element.70), channel_id=1, source_target_pairs={{0,8},{4,12},{8,0},{12,4},{1,9},{5,13},{9,1},{13,5},{2,10},{6,14},... | collective-permute-start | bytes 344072 | tf_op jit(solution)/shard_map/ppermute | solution.py:24
  23.6 0.0 collective-permute-done.6.refs_3_
  23.6 0.0 collective-permute-start.8
  23.6 3.8 %collective-permute-done.7.refs_4_ = bf16[7,16,512]{2,1,0:T(8,128)(2,1)S(1)} collective-permute-done((bf16[7,16,512]{2,1,0:T(8,128)(2,1)S(1)}, bf16[7,16,512]{2,1,0:T(8,128)(2,1)S(1)}, u32[]{:S(2)}, u32[]{:S(2)}) %collective-permute-start.7) | collective-permute-done | bytes 114720 | tf_op jit(solution)/shard_map/ppermute | solution.py:24
  27.5 1.6 %collective-permute-done.8.refs_5_ = bf16[7,16,512]{2,1,0:T(8,128)(2,1)S(1)} collective-permute-done((bf16[7,16,512]{2,1,0:T(8,128)(2,1)S(1)}, bf16[7,16,512]{2,1,0:T(8,128)(2,1)S(1)}, u32[]{:S(2)}, u32[]{:S(2)}) %collective-permute-start.8) | collective-permute-done | bytes 114720 | tf_op jit(solution)/shard_map/ppermute | solution.py:24
  29.1 0.0 copy-done
  29.1 0.0 copy-done.1
  29.1 6.2 %block.2 = (bf16[8,16,512]{2,1,0:T(8,128)(2,1)S(1)}, bf16[8,16,512]{2,1,0:T(8,128)(2,1)S(1)}, bf16[8,16,512]{2,1,0:T(8,128)(2,1)S(1)}, bf16[8,16,512]{2,1,0:T(8,128)(2,1)S(1)}) custom-call(s32[79]{0:T(128)S(4)} %get-tuple-element.59.refs_0_, bf16[32,16,512]{2,1,0:T(8,128)(2,1)S(1)} %get-tuple-element.67.refs_1_, ...), custom_call_target="tpu_custom_call" | custom-call | tf_op jit(solution)/shard_map/block/pallas_call | solution.py:213
  35.3 0.0 collective-permute-done.1.refs_2_
  35.3 0.0 collective-permute-done.2.refs_3_
  35.3 0.0 collective-permute-done.3.refs_4_
  35.3 1.1 %collective-permute-start.9 = (bf16[8,16,512]{2,1,0:T(8,128)(2,1)S(1)}, bf16[8,16,512]{2,1,0:T(8,128)(2,1)S(1)}, u32[]{:S(2)}, u32[]{:S(2)}) collective-permute-start(bf16[8,16,512]{2,1,0:T(8,128)(2,1)S(1)} %get-tuple-element.83), channel_id=1, source_target_pairs={{0,1},{1,0},{2,3},{3,2},{4,5},{5,4},{6,7},{7,6},{8,9},{9,8},{10,11... | collective-permute-start | bytes 393224 | tf_op jit(solution)/shard_map/ppermute | solution.py:24
  36.4 0.1 select.3
  36.5 0.1 collective-permute-start.12
  36.6 1.3 %collective-permute-start.13 = (bf16[7,16,512]{2,1,0:T(8,128)(2,1)S(1)}, bf16[7,16,512]{2,1,0:T(8,128)(2,1)S(1)}, u32[]{:S(2)}, u32[]{:S(2)}) collective-permute-start(bf16[7,16,512]{2,1,0:T(8,128)(2,1)S(1)} %get-tuple-element.93), channel_id=1, source_target_pairs={{0,8},{4,12},{8,0},{12,4},{1,9},{5,13},{9,1},{13,5},{2,10},{6,14},... | collective-permute-start | bytes 344072 | tf_op jit(solution)/shard_map/ppermute | solution.py:24
  37.8 0.6 collective-permute-start.14
  38.4 2.0 %collective-permute-start.10 = (bf16[8,16,512]{2,1,0:T(8,128)(2,1)S(1)}, bf16[8,16,512]{2,1,0:T(8,128)(2,1)S(1)}, u32[]{:S(2)}, u32[]{:S(2)}) collective-permute-start(bf16[8,16,512]{2,1,0:T(8,128)(2,1)S(1)} %get-tuple-element.84), channel_id=1, source_target_pairs={{0,2},{1,3},{2,0},{3,1},{4,6},{5,7},{6,4},{7,5},{8,10},{9,11},{10,... | collective-permute-start | bytes 393224 | tf_op jit(solution)/shard_map/ppermute | solution.py:24
  40.4 0.0 collective-permute-done.12.refs_3_
  40.4 1.4 %collective-permute-start.11 = (bf16[8,16,512]{2,1,0:T(8,128)(2,1)S(1)}, bf16[8,16,512]{2,1,0:T(8,128)(2,1)S(1)}, u32[]{:S(2)}, u32[]{:S(2)}) collective-permute-start(bf16[8,16,512]{2,1,0:T(8,128)(2,1)S(1)} %get-tuple-element.85), channel_id=1, source_target_pairs={{0,3},{1,2},{2,1},{3,0},{4,7},{5,6},{6,5},{7,4},{8,11},{9,10},{10,... | collective-permute-start | bytes 393224 | tf_op jit(solution)/shard_map/ppermute | solution.py:24
  41.8 0.8 %collective-permute-done.13.refs_4_ = bf16[7,16,512]{2,1,0:T(8,128)(2,1)S(1)} collective-permute-done((bf16[7,16,512]{2,1,0:T(8,128)(2,1)S(1)}, bf16[7,16,512]{2,1,0:T(8,128)(2,1)S(1)}, u32[]{:S(2)}, u32[]{:S(2)}) %collective-permute-start.13) | collective-permute-done | bytes 114720 | tf_op jit(solution)/shard_map/ppermute | solution.py:24
  42.6 1.6 %collective-permute-done.14.refs_5_ = bf16[7,16,512]{2,1,0:T(8,128)(2,1)S(1)} collective-permute-done((bf16[7,16,512]{2,1,0:T(8,128)(2,1)S(1)}, bf16[7,16,512]{2,1,0:T(8,128)(2,1)S(1)}, u32[]{:S(2)}, u32[]{:S(2)}) %collective-permute-start.14) | collective-permute-done | bytes 114720 | tf_op jit(solution)/shard_map/ppermute | solution.py:24
  44.1 6.2 %block.3 = (bf16[8,16,512]{2,1,0:T(8,128)(2,1)S(1)}, bf16[8,16,512]{2,1,0:T(8,128)(2,1)S(1)}, bf16[8,16,512]{2,1,0:T(8,128)(2,1)S(1)}, bf16[8,16,512]{2,1,0:T(8,128)(2,1)S(1)}) custom-call(s32[79]{0:T(128)S(4)} %get-tuple-element.59.refs_0_, bf16[32,16,512]{2,1,0:T(8,128)(2,1)S(1)} %get-tuple-element.90.refs_1_, ...), custom_call_target="tpu_custom_call" | custom-call | tf_op jit(solution)/shard_map/block/pallas_call | solution.py:213
  50.4 0.8 %collective-permute-start.15 = (bf16[8,16,512]{2,1,0:T(8,128)(2,1)S(1)}, bf16[8,16,512]{2,1,0:T(8,128)(2,1)S(1)}, u32[]{:S(2)}, u32[]{:S(2)}) collective-permute-start(bf16[8,16,512]{2,1,0:T(8,128)(2,1)S(1)} %get-tuple-element.96), channel_id=1, source_target_pairs={{0,1},{1,0},{2,3},{3,2},{4,5},{5,4},{6,7},{7,6},{8,9},{9,8},{10,11... | collective-permute-start | bytes 393224 | tf_op jit(solution)/shard_map/ppermute | solution.py:24
  51.2 2.3 %collective-permute-start.16 = (bf16[8,16,512]{2,1,0:T(8,128)(2,1)S(1)}, bf16[8,16,512]{2,1,0:T(8,128)(2,1)S(1)}, u32[]{:S(2)}, u32[]{:S(2)}) collective-permute-start(bf16[8,16,512]{2,1,0:T(8,128)(2,1)S(1)} %get-tuple-element.97), channel_id=1, source_target_pairs={{0,2},{1,3},{2,0},{3,1},{4,6},{5,7},{6,4},{7,5},{8,10},{9,11},{10,... | collective-permute-start | bytes 393224 | tf_op jit(solution)/shard_map/ppermute | solution.py:24
  53.5 0.0 collective-permute-done.9.refs_2_
  53.5 1.3 %collective-permute-start.17 = (bf16[8,16,512]{2,1,0:T(8,128)(2,1)S(1)}, bf16[8,16,512]{2,1,0:T(8,128)(2,1)S(1)}, u32[]{:S(2)}, u32[]{:S(2)}) collective-permute-start(bf16[8,16,512]{2,1,0:T(8,128)(2,1)S(1)} %get-tuple-element.98), channel_id=1, source_target_pairs={{0,3},{1,2},{2,1},{3,0},{4,7},{5,6},{6,5},{7,4},{8,11},{9,10},{10,... | collective-permute-start | bytes 393224 | tf_op jit(solution)/shard_map/ppermute | solution.py:24
  54.8 0.0 collective-permute-done.10.refs_3_
  54.8 0.0 collective-permute-done.11.refs_4_
  54.8 4.1 %collective-permute-done.15.refs_6_ = bf16[8,16,512]{2,1,0:T(8,128)(2,1)S(1)} collective-permute-done((bf16[8,16,512]{2,1,0:T(8,128)(2,1)S(1)}, bf16[8,16,512]{2,1,0:T(8,128)(2,1)S(1)}, u32[]{:S(2)}, u32[]{:S(2)}) %collective-permute-start.15) | collective-permute-done | bytes 131104 | tf_op jit(solution)/shard_map/ppermute | solution.py:24
  59.0 5.1 %collective-permute-done.16.refs_7_ = bf16[8,16,512]{2,1,0:T(8,128)(2,1)S(1)} collective-permute-done((bf16[8,16,512]{2,1,0:T(8,128)(2,1)S(1)}, bf16[8,16,512]{2,1,0:T(8,128)(2,1)S(1)}, u32[]{:S(2)}, u32[]{:S(2)}) %collective-permute-start.16) | collective-permute-done | bytes 131104 | tf_op jit(solution)/shard_map/ppermute | solution.py:24
  64.0 0.0 collective-permute-done.17.refs_8_
  64.0 1.0 %assemble.1 = bf16[8,8,16,512]{3,2,1,0:T(8,128)(2,1)} custom-call(s32[79]{0:T(128)S(4)} %get-tuple-element.59.refs_0_, bf16[8,16,512]{2,1,0:T(8,128)(2,1)S(1)} %get-tuple-element.82.refs_1_, bf16[8,16,512]{2,1,0:T(8,128)(2,1)S(1)} %collective-permute-done.9.refs_2_, bf16[8,16,512]{2,1,0:T(8,128)(2,1)S(1)} %collective-permute-done.10.refs_3_, ...), custom_call_target="tpu_custom_call" | custom-call | tf_op jit(solution)/shard_map/assemble/pallas_call | solution.py:251
Async XLA Ops:
  0.0 7.2 %copy-start.3 = (s32[3,32]{1,0:T(4,128)S(1)}, s32[3,32]{1,0:T(4,128)}, u32[]{:S(2)}) copy-start(s32[3,32]{1,0:T(4,128)} %merge_num) | copy-start | bytes 1156
  0.0 7.2 %copy-start.2 = (s32[3,32]{1,0:T(4,128)S(1)}, s32[3,32]{1,0:T(4,128)}, u32[]{:S(2)}) copy-start(s32[3,32]{1,0:T(4,128)} %src) | copy-start | bytes 1156
  1.4 9.3 %collective-permute-start = (bf16[8,16,512]{2,1,0:T(8,128)(2,1)S(1)}, bf16[8,16,512]{2,1,0:T(8,128)(2,1)S(1)}, u32[]{:S(2)}, u32[]{:S(2)}) collective-permute-start(bf16[8,16,512]{2,1,0:T(8,128)(2,1)S(1)} %get-tuple-element.58), channel_id=1, source_target_pairs={{0,1},{1,0},{2,3},{3,2},{4,5},{5,4},{6,7},{7,6},{8,9},{9,8},{10,11... | collective-permute-start | bytes 393224 | tf_op jit(solution)/shard_map/ppermute | solution.py:24
  4.5 12.9 %collective-permute-start.4 = (bf16[8,16,512]{2,1,0:T(8,128)(2,1)S(1)}, bf16[8,16,512]{2,1,0:T(8,128)(2,1)S(1)}, u32[]{:S(2)}, u32[]{:S(2)}) collective-permute-start(bf16[8,16,512]{2,1,0:T(8,128)(2,1)S(1)} %get-tuple-element.65), channel_id=1, source_target_pairs={{0,2},{1,3},{2,0},{3,1},{4,6},{5,7},{6,4},{7,5},{8,10},{9,11},{10,... | collective-permute-start | bytes 393224 | tf_op jit(solution)/shard_map/ppermute | solution.py:24
  7.1 10.3 %collective-permute-start.5 = (bf16[8,16,512]{2,1,0:T(8,128)(2,1)S(1)}, bf16[8,16,512]{2,1,0:T(8,128)(2,1)S(1)}, u32[]{:S(2)}, u32[]{:S(2)}) collective-permute-start(bf16[8,16,512]{2,1,0:T(8,128)(2,1)S(1)} %get-tuple-element.66), channel_id=1, source_target_pairs={{0,3},{1,2},{2,1},{3,0},{4,7},{5,6},{6,5},{7,4},{8,11},{9,10},{10,... | collective-permute-start | bytes 393224 | tf_op jit(solution)/shard_map/ppermute | solution.py:24
  7.2 21.9 %copy-start = (f32[512]{0:T(512)S(1)}, f32[512]{0:T(512)}, u32[]{:S(2)}) copy-start(f32[512]{0:T(512)} %param.14) | copy-start | bytes 6148
  7.2 21.9 %copy-start.1 = (f32[512]{0:T(512)S(1)}, f32[512]{0:T(512)}, u32[]{:S(2)}) copy-start(f32[512]{0:T(512)} %param.19) | copy-start | bytes 6148
  17.5 6.1 %collective-permute-start.6 = (bf16[7,16,512]{2,1,0:T(8,128)(2,1)S(1)}, bf16[7,16,512]{2,1,0:T(8,128)(2,1)S(1)}, u32[]{:S(2)}, u32[]{:S(2)}) collective-permute-start(bf16[7,16,512]{2,1,0:T(8,128)(2,1)S(1)} %get-tuple-element.69), channel_id=1, source_target_pairs={{0,4},{4,0},{8,12},{12,8},{1,5},{5,1},{9,13},{13,9},{2,6},{6,2},{1... | collective-permute-start | bytes 344072 | tf_op jit(solution)/shard_map/ppermute | solution.py:24
  17.6 17.7 %collective-permute-start.1 = (bf16[8,16,512]{2,1,0:T(8,128)(2,1)S(1)}, bf16[8,16,512]{2,1,0:T(8,128)(2,1)S(1)}, u32[]{:S(2)}, u32[]{:S(2)}) collective-permute-start(bf16[8,16,512]{2,1,0:T(8,128)(2,1)S(1)} %get-tuple-element.60), channel_id=1, source_target_pairs={{0,1},{1,0},{2,3},{3,2},{4,5},{5,4},{6,7},{7,6},{8,9},{9,8},{10,11... | collective-permute-start | bytes 393224 | tf_op jit(solution)/shard_map/ppermute | solution.py:24
  19.6 15.7 %collective-permute-start.2 = (bf16[8,16,512]{2,1,0:T(8,128)(2,1)S(1)}, bf16[8,16,512]{2,1,0:T(8,128)(2,1)S(1)}, u32[]{:S(2)}, u32[]{:S(2)}) collective-permute-start(bf16[8,16,512]{2,1,0:T(8,128)(2,1)S(1)} %get-tuple-element.61), channel_id=1, source_target_pairs={{0,2},{1,3},{2,0},{3,1},{4,6},{5,7},{6,4},{7,5},{8,10},{9,11},{10,... | collective-permute-start | bytes 393224 | tf_op jit(solution)/shard_map/ppermute | solution.py:24
  20.7 14.6 %collective-permute-start.3 = (bf16[8,16,512]{2,1,0:T(8,128)(2,1)S(1)}, bf16[8,16,512]{2,1,0:T(8,128)(2,1)S(1)}, u32[]{:S(2)}, u32[]{:S(2)}) collective-permute-start(bf16[8,16,512]{2,1,0:T(8,128)(2,1)S(1)} %get-tuple-element.62), channel_id=1, source_target_pairs={{0,3},{1,2},{2,1},{3,0},{4,7},{5,6},{6,5},{7,4},{8,11},{9,10},{10,... | collective-permute-start | bytes 393224 | tf_op jit(solution)/shard_map/ppermute | solution.py:24
  22.1 5.4 %collective-permute-start.7 = (bf16[7,16,512]{2,1,0:T(8,128)(2,1)S(1)}, bf16[7,16,512]{2,1,0:T(8,128)(2,1)S(1)}, u32[]{:S(2)}, u32[]{:S(2)}) collective-permute-start(bf16[7,16,512]{2,1,0:T(8,128)(2,1)S(1)} %get-tuple-element.70), channel_id=1, source_target_pairs={{0,8},{4,12},{8,0},{12,4},{1,9},{5,13},{9,1},{13,5},{2,10},{6,14},... | collective-permute-start | bytes 344072 | tf_op jit(solution)/shard_map/ppermute | solution.py:24
  23.6 5.4 %collective-permute-start.8 = (bf16[7,16,512]{2,1,0:T(8,128)(2,1)S(1)}, bf16[7,16,512]{2,1,0:T(8,128)(2,1)S(1)}, u32[]{:S(2)}, u32[]{:S(2)}) collective-permute-start(bf16[7,16,512]{2,1,0:T(8,128)(2,1)S(1)} %get-tuple-element.71), channel_id=1, source_target_pairs={{0,12},{4,8},{8,4},{12,0},{1,13},{5,9},{9,5},{13,1},{2,14},{6,10},... | collective-permute-start | bytes 344072 | tf_op jit(solution)/shard_map/ppermute | solution.py:24
  35.3 18.1 %collective-permute-start.9 = (bf16[8,16,512]{2,1,0:T(8,128)(2,1)S(1)}, bf16[8,16,512]{2,1,0:T(8,128)(2,1)S(1)}, u32[]{:S(2)}, u32[]{:S(2)}) collective-permute-start(bf16[8,16,512]{2,1,0:T(8,128)(2,1)S(1)} %get-tuple-element.83), channel_id=1, source_target_pairs={{0,1},{1,0},{2,3},{3,2},{4,5},{5,4},{6,7},{7,6},{8,9},{9,8},{10,11... | collective-permute-start | bytes 393224 | tf_op jit(solution)/shard_map/ppermute | solution.py:24
  36.5 3.9 %collective-permute-start.12 = (bf16[7,16,512]{2,1,0:T(8,128)(2,1)S(1)}, bf16[7,16,512]{2,1,0:T(8,128)(2,1)S(1)}, u32[]{:S(2)}, u32[]{:S(2)}) collective-permute-start(bf16[7,16,512]{2,1,0:T(8,128)(2,1)S(1)} %get-tuple-element.92), channel_id=1, source_target_pairs={{0,4},{4,0},{8,12},{12,8},{1,5},{5,1},{9,13},{13,9},{2,6},{6,2},{1... | collective-permute-start | bytes 344072 | tf_op jit(solution)/shard_map/ppermute | solution.py:24
  36.6 6.0 %collective-permute-start.13 = (bf16[7,16,512]{2,1,0:T(8,128)(2,1)S(1)}, bf16[7,16,512]{2,1,0:T(8,128)(2,1)S(1)}, u32[]{:S(2)}, u32[]{:S(2)}) collective-permute-start(bf16[7,16,512]{2,1,0:T(8,128)(2,1)S(1)} %get-tuple-element.93), channel_id=1, source_target_pairs={{0,8},{4,12},{8,0},{12,4},{1,9},{5,13},{9,1},{13,5},{2,10},{6,14},... | collective-permute-start | bytes 344072 | tf_op jit(solution)/shard_map/ppermute | solution.py:24
  37.8 6.3 %collective-permute-start.14 = (bf16[7,16,512]{2,1,0:T(8,128)(2,1)S(1)}, bf16[7,16,512]{2,1,0:T(8,128)(2,1)S(1)}, u32[]{:S(2)}, u32[]{:S(2)}) collective-permute-start(bf16[7,16,512]{2,1,0:T(8,128)(2,1)S(1)} %get-tuple-element.94), channel_id=1, source_target_pairs={{0,12},{4,8},{8,4},{12,0},{1,13},{5,9},{9,5},{13,1},{2,14},{6,10},... | collective-permute-start | bytes 344072 | tf_op jit(solution)/shard_map/ppermute | solution.py:24
  38.4 16.4 %collective-permute-start.10 = (bf16[8,16,512]{2,1,0:T(8,128)(2,1)S(1)}, bf16[8,16,512]{2,1,0:T(8,128)(2,1)S(1)}, u32[]{:S(2)}, u32[]{:S(2)}) collective-permute-start(bf16[8,16,512]{2,1,0:T(8,128)(2,1)S(1)} %get-tuple-element.84), channel_id=1, source_target_pairs={{0,2},{1,3},{2,0},{3,1},{4,6},{5,7},{6,4},{7,5},{8,10},{9,11},{10,... | collective-permute-start | bytes 393224 | tf_op jit(solution)/shard_map/ppermute | solution.py:24
  40.4 14.4 %collective-permute-start.11 = (bf16[8,16,512]{2,1,0:T(8,128)(2,1)S(1)}, bf16[8,16,512]{2,1,0:T(8,128)(2,1)S(1)}, u32[]{:S(2)}, u32[]{:S(2)}) collective-permute-start(bf16[8,16,512]{2,1,0:T(8,128)(2,1)S(1)} %get-tuple-element.85), channel_id=1, source_target_pairs={{0,3},{1,2},{2,1},{3,0},{4,7},{5,6},{6,5},{7,4},{8,11},{9,10},{10,... | collective-permute-start | bytes 393224 | tf_op jit(solution)/shard_map/ppermute | solution.py:24
  50.4 8.6 %collective-permute-start.15 = (bf16[8,16,512]{2,1,0:T(8,128)(2,1)S(1)}, bf16[8,16,512]{2,1,0:T(8,128)(2,1)S(1)}, u32[]{:S(2)}, u32[]{:S(2)}) collective-permute-start(bf16[8,16,512]{2,1,0:T(8,128)(2,1)S(1)} %get-tuple-element.96), channel_id=1, source_target_pairs={{0,1},{1,0},{2,3},{3,2},{4,5},{5,4},{6,7},{7,6},{8,9},{9,8},{10,11... | collective-permute-start | bytes 393224 | tf_op jit(solution)/shard_map/ppermute | solution.py:24
  51.2 12.8 %collective-permute-start.16 = (bf16[8,16,512]{2,1,0:T(8,128)(2,1)S(1)}, bf16[8,16,512]{2,1,0:T(8,128)(2,1)S(1)}, u32[]{:S(2)}, u32[]{:S(2)}) collective-permute-start(bf16[8,16,512]{2,1,0:T(8,128)(2,1)S(1)} %get-tuple-element.97), channel_id=1, source_target_pairs={{0,2},{1,3},{2,0},{3,1},{4,6},{5,7},{6,4},{7,5},{8,10},{9,11},{10,... | collective-permute-start | bytes 393224 | tf_op jit(solution)/shard_map/ppermute | solution.py:24
  53.5 10.6 %collective-permute-start.17 = (bf16[8,16,512]{2,1,0:T(8,128)(2,1)S(1)}, bf16[8,16,512]{2,1,0:T(8,128)(2,1)S(1)}, u32[]{:S(2)}, u32[]{:S(2)}) collective-permute-start(bf16[8,16,512]{2,1,0:T(8,128)(2,1)S(1)} %get-tuple-element.98), channel_id=1, source_target_pairs={{0,3},{1,2},{2,1},{3,0},{4,7},{5,6},{6,5},{7,4},{8,11},{9,10},{10,... | collective-permute-start | bytes 393224 | tf_op jit(solution)/shard_map/ppermute | solution.py:24

commit v3 on v2

--- a/solution.py
+++ b/solution.py
@@ -10,6 +10,7 @@
 HD = 64
 ROW_TILE = 16
 BLOCK_FF = 512
+TURNED = 3
 
 VMEM = pltpu.VMEM
 SMEM = pltpu.SMEM
@@ -39,12 +40,14 @@
 
 
 def prepare_kernel(lay, ids, src, merge_num, *refs):
-    count = refs[-2]
-    sems = refs[-1]
-    half = (len(refs) - 3) // 2
-    stored, table, loaded = refs[:half], refs[half], refs[half + 1 : -2]
+    held, count, sems = refs[-3:]
+    half = (len(refs) - 4) // 2
+    stored, table, loaded = refs[:half], refs[half], refs[half + 1 : -3]
     loads = [
-        pltpu.make_async_copy(stored[i], loaded[i], sems.at[i]) for i in range(half)
+        pltpu.make_async_copy(
+            stored[i], held.at[i] if i < TURNED else loaded[i], sems.at[i]
+        )
+        for i in range(half)
     ]
     for load in loads:
         load.start()
@@ -66,6 +69,10 @@
 
     lax.fori_loop(0, lay.requests, one_request, 0)
 
+    for i in range(TURNED):
+        loads[i].wait()
+        loaded[i][...] = held[i].T
+
     for j in range(lay.spaces):
         target = me ^ j
 
@@ -77,7 +84,7 @@
             return filled + (owner == me).astype(jnp.int32)
 
         lax.fori_loop(0, lay.requests, one_send, 0)
-    for load in loads:
+    for load in loads[TURNED:]:
         load.wait()
 
 
@@ -89,10 +96,11 @@
         in_specs=[spec(SMEM)] * 3 + [spec(pltpu.HBM)] * len(weights),
         out_specs=(spec(SMEM),) + (spec(VMEM),) * len(weights),
         scratch_shapes=[
+            VMEM((TURNED,) + weights[0].shape, weights[0].dtype),
             SMEM((lay.spaces,), jnp.int32),
             pltpu.SemaphoreType.DMA((len(weights),)),
         ],
-        compiler_params=pltpu.CompilerParams(vmem_limit_bytes=1 << 20),
+        compiler_params=pltpu.CompilerParams(vmem_limit_bytes=6 << 20),
         name="prepare",
     )(ids, src_brick, merge_num, *pinned(weights, pltpu.HBM))
 
@@ -121,6 +129,7 @@
         in_specs=[spec(SMEM)] + [spec(VMEM)] * lay.frames,
         out_specs=(spec(VMEM),) * (1 + lay.spaces),
         compiler_params=pltpu.CompilerParams(vmem_limit_bytes=4 << 20),
+        cost_estimate=pl.CostEstimate(flops=1, bytes_accessed=0, transcendentals=0),
         name="select",
     )(*pinned([table], SMEM), *parts)
 
@@ -129,6 +138,13 @@
     wide = values.astype(jnp.float32)
     mean_sq = jnp.mean(wide * wide, axis=-1, keepdims=True)
     return (wide * lax.rsqrt(mean_sq + 1e-06) * gain).astype(jnp.bfloat16)
+
+
+def project_turned(turned, values):
+    out = lax.dot_general(
+        turned, values, (((1,), (1,)), ((), ())), preferred_element_type=jnp.float32
+    )
+    return out.astype(jnp.bfloat16)
 
 
 def matmul(a, b):
@@ -158,41 +174,29 @@
                 stacked[f * bricks + b].astype(jnp.float32) + weight * piece
             ).astype(jnp.bfloat16)
     normed = normalise(merged[...], gain_a[...])
-    queries = matmul(normed, w_q[...]).astype(jnp.bfloat16)
-    keys = matmul(normed, w_k[...]).astype(jnp.bfloat16)
-    vals = matmul(normed, w_v[...]).astype(jnp.bfloat16)
-
-    def frame_of(x, f):
-        return x[f * per_frame : (f + 1) * per_frame]
-
-    lanes = 128
-    head_of = lax.broadcasted_iota(jnp.int32, (width, lanes), 0) // HD
-    gather_heads = (head_of == lax.broadcasted_iota(jnp.int32, (width, lanes), 1)).astype(
-        jnp.bfloat16
-    )
-    head_to = lax.broadcasted_iota(jnp.int32, (lanes, width), 1) // HD
-    spread_heads = (head_to == lax.broadcasted_iota(jnp.int32, (lanes, width), 0)).astype(
-        jnp.bfloat16
-    )
+    queries = project_turned(w_q[...], normed)
+    keys = project_turned(w_k[...], normed)
+    vals = project_turned(w_v[...], normed)
+
+    def heads_of(x, f):
+        part = x[:, f * per_frame : (f + 1) * per_frame].astype(jnp.float32)
+        return part.reshape(width // HD, HD, per_frame)
+
     for f in range(frames):
-        query = frame_of(queries, f).astype(jnp.float32)
-        scores = []
-        for g in range(f + 1):
-            product = query * frame_of(keys, g).astype(jnp.float32)
-            high = product.astype(jnp.bfloat16)
-            low = (product - high.astype(jnp.float32)).astype(jnp.bfloat16)
-            scores.append(
-                (matmul(high, gather_heads) + matmul(low, gather_heads)) * (1.0 / HD**0.5)
-            )
+        query = heads_of(queries, f) * (1.0 / HD**0.5)
+        scores = [
+            jnp.sum(query * heads_of(keys, g), axis=1, keepdims=True) for g in range(f + 1)
+        ]
         top = functools.reduce(jnp.maximum, scores)
         exps = [jnp.exp(s - top) for s in scores]
         total = functools.reduce(jnp.add, exps)
         context = None
         for g in range(f + 1):
-            prob = (exps[g] / total).astype(jnp.bfloat16)
-            term = matmul(prob, spread_heads) * frame_of(vals, g).astype(jnp.float32)
+            prob = (exps[g] / total).astype(jnp.bfloat16).astype(jnp.float32)
+            term = prob * heads_of(vals, g)
             context = term if context is None else context + term
-        hidden[f * per_frame : (f + 1) * per_frame] = context.astype(jnp.bfloat16)
+        context = context.reshape(width, per_frame).astype(jnp.bfloat16)
+        hidden[f * per_frame : (f + 1) * per_frame] = context.T
     mid = (merged[...].astype(jnp.float32) + matmul(hidden[...], w_o[...])).astype(jnp.bfloat16)
     normed2 = normalise(mid, gain_m[...])
     total = mid.astype(jnp.float32)
@@ -223,6 +227,7 @@
             VMEM((total, rows, width), dtype),
         ],
         compiler_params=pltpu.CompilerParams(vmem_limit_bytes=20 << 20),
+        cost_estimate=pl.CostEstimate(flops=10000000000, bytes_accessed=0, transcendentals=0),
         name="block",
     )(*pinned([table], SMEM), stacked, *pieces, *gains, *pinned(weights, VMEM))
 
@@ -295,11 +300,16 @@
     for c in range(chunks):
         stacked, *slots = select(lay, table, [parts[c][0]] + arrived[c])
         pieces = [slots[0]] + across(slots[1:], "space")
+        if c + 1 < chunks:
+            pieces, arrived[c + 1][0] = lax.optimization_barrier((pieces, arrived[c + 1][0]))
+        if c > 0:
+            pieces, back[-1][3] = lax.optimization_barrier((pieces, back[-1][3]))
         done = run_block(lay, table, stacked, pieces, gains, weights)
         if c + 1 < chunks:
-            arrived[c + 1], done = lax.optimization_barrier((arrived[c + 1], done))
-        back += [done[0]] + across(done[1:], "frame")
-    out = assemble(table, back, frames)
+            arrived[c + 1], _ = lax.optimization_barrier((arrived[c + 1], done))
+        returned = across(done[1:], "frame")
+        back.append([done[0]] + returned)
+    out = assemble(table, sum(back, []), frames)
     return out.reshape(1, bricks, tall, width)
 
 

time: 65.2 us -> 62.3 us (0.956)
  waiting for transfers between devices: 23.7 us -> 19.3 us
  starting transfers between devices: 22.6 us -> 26.5 us
  Pallas kernels: 17.1 us -> 14.7 us
    ppermute x18, waiting for transfers between devices: 23.7 us -> 19.3 us  [exchange(): return lax.ppermute(values, axis, [(i, i ^ step) for i in range(size)])]
    ppermute x18, starting transfers between devices: 22.6 us -> 26.5 us  [exchange(): return lax.ppermute(values, axis, [(i, i ^ step) for i in range(size)])]
    pallas_call x2, Pallas kernels: 12.4 us -> 9.82 us  [run_block(): pl.pallas_call(functools.partial(block_kernel, lay), out_shape=(jax.Shape...]
  transfers between devices with their start and end apart: 18 -> 18, of which waited for: 7 -> 6; matrix products, arithmetic and copies ran while one was open for 0% -> 0% of each run, Pallas kernels for 25% -> 22%
where the time goes in v3:
time: 62.3 us; the launch traced here: 62.1 us
  starting transfers between devices  26.5 us (43%)
  waiting for transfers between devices  19.3 us (31%)
  Pallas kernels  14.7 us (24%)
  local copies, waits for them, and re-layouts  1.43 us (2%)
    ppermute x18, starting transfers between devices, exchange(): return lax.ppermute(values, axis, [(i, i ^ step) for i in range(size)])  26.5 us
    ppermute x18, waiting for transfers between devices, exchange(): return lax.ppermute(values, axis, [(i, i ^ step) for i in range(size)])  19.3 us
    pallas_call x2, Pallas kernels, run_block(): pl.pallas_call(functools.partial(block_kernel, lay), out_shape=(jax.Shape...  9.82 us
    pallas_call x1, Pallas kernels, prepare(): pl.pallas_call(functools.partial(prepare_kernel, lay), out_shape=(pltpu.S...  3.74 us
    squeeze x1, local copies, waits for them, and re-layouts, local(): lax.dynamic_index_in_dim(cut, c * frames + (mine ^ k), 1, keepdims=False)  1.41 us
  transfers between devices with their start and end apart: 18, of which 6 were waited for; matrix products, arithmetic and copies ran while one was open for 0% of the time, Pallas kernels for 22%

profile of v3, /device:TPU:0, one launch (start us, length us, event | category | flops | bytes accessed | tf_op | source)
XLA Modules:
  0.0 62.1 jit_solution(10669952405232417645)
XLA Ops:
  0.0 0.0 copy-start.1
  0.0 0.0 copy-start
  0.0 1.4 %dynamic-slice_bitcast_fusion = (bf16[8,16,512]{2,1,0:T(8,128)(2,1)S(1)}, bf16[8,16,512]{2,1,0:T(8,128)(2,1)S(1)}, bf16[8,16,512]{2,1,0:T(8,128)(2,1)S(1)}, bf16...) fusion(bf16[8,8,16,512]{3,2,1,0:T(8,128)(2,1)} %bitcast.42, ...), kind=kLoop, calls=%fused_computation | loop fusion | bytes 2097184 | tf_op jit(solution)/shard_map/jit(dynamic_index_in_dim)/squeeze | solution.py:286
  1.4 3.1 %collective-permute-start = (bf16[8,16,512]{2,1,0:T(8,128)(2,1)S(1)}, bf16[8,16,512]{2,1,0:T(8,128)(2,1)S(1)}, u32[]{:S(2)}, u32[]{:S(2)}) collective-permute-start(bf16[8,16,512]{2,1,0:T(8,128)(2,1)S(1)} %get-tuple-element.64), channel_id=1, source_target_pairs={{0,1},{1,0},{2,3},{3,2},{4,5},{5,4},{6,7},{7,6},{8,9},{9,8},{10,11... | collective-permute-start | bytes 393224 | tf_op jit(solution)/shard_map/ppermute | solution.py:25
  4.5 2.6 %collective-permute-start.1 = (bf16[8,16,512]{2,1,0:T(8,128)(2,1)S(1)}, bf16[8,16,512]{2,1,0:T(8,128)(2,1)S(1)}, u32[]{:S(2)}, u32[]{:S(2)}) collective-permute-start(bf16[8,16,512]{2,1,0:T(8,128)(2,1)S(1)} %get-tuple-element.68), channel_id=1, source_target_pairs={{0,2},{1,3},{2,0},{3,1},{4,6},{5,7},{6,4},{7,5},{8,10},{9,11},{10,... | collective-permute-start | bytes 393224 | tf_op jit(solution)/shard_map/ppermute | solution.py:25
  7.1 0.0 collective-permute-start.2
  7.1 0.1 pad_add_fusion.ids
  7.2 0.0 copy-done.1
  7.2 0.0 copy-done
  7.2 0.0 copy-start.2
  7.2 0.0 copy-start.3
  7.2 3.7 %prepare.1 = (s32[79]{0:T(128)S(4)}, bf16[512,512]{1,0:T(8,128)(2,1)S(1)}, bf16[512,512]{1,0:T(8,128)(2,1)S(1)}, bf16[512,512]{1,0:T(8,128)(2,1)S(1)}, bf16[512,...) custom-call(s32[2]{0:T(128)S(1)} %pad_add_fusion.ids, s32[3,32]{1,0:T(4,128)S(1)} %copy-done, ...), custom_call_target="tpu_custom_call" | custom-call | tf_op jit(solution)/shard_map/prepare/pallas_call | solution.py:92
  11.0 0.0 collective-permute-done.refs_2_
  11.0 1.0 %collective-permute-start.6 = (bf16[8,16,512]{2,1,0:T(8,128)(2,1)S(1)}, bf16[8,16,512]{2,1,0:T(8,128)(2,1)S(1)}, u32[]{:S(2)}, u32[]{:S(2)}) collective-permute-start(bf16[8,16,512]{2,1,0:T(8,128)(2,1)S(1)} %get-tuple-element.75), channel_id=1, source_target_pairs={{0,1},{1,0},{2,3},{3,2},{4,5},{5,4},{6,7},{7,6},{8,9},{9,8},{10,11... | collective-permute-start | bytes 393224 | tf_op jit(solution)/shard_map/ppermute | solution.py:25
  11.9 5.5 %collective-permute-done.1.refs_3_ = bf16[8,16,512]{2,1,0:T(8,128)(2,1)S(1)} collective-permute-done((bf16[8,16,512]{2,1,0:T(8,128)(2,1)S(1)}, bf16[8,16,512]{2,1,0:T(8,128)(2,1)S(1)}, u32[]{:S(2)}, u32[]{:S(2)}) %collective-permute-start.1) | collective-permute-done | bytes 131104 | tf_op jit(solution)/shard_map/ppermute | solution.py:25
  17.4 0.0 collective-permute-done.2.refs_4_
  17.4 0.1 select.2
  17.5 0.1 collective-permute-start.3
  17.6 1.6 %collective-permute-start.4 = (bf16[7,16,512]{2,1,0:T(8,128)(2,1)S(1)}, bf16[7,16,512]{2,1,0:T(8,128)(2,1)S(1)}, u32[]{:S(2)}, u32[]{:S(2)}) collective-permute-start(bf16[7,16,512]{2,1,0:T(8,128)(2,1)S(1)} %get-tuple-element.73), channel_id=1, source_target_pairs={{0,8},{4,12},{8,0},{12,4},{1,9},{5,13},{9,1},{13,5},{2,10},{6,14},... | collective-permute-start | bytes 344072 | tf_op jit(solution)/shard_map/ppermute | solution.py:25
  19.2 0.3 collective-permute-start.5
  19.5 3.0 %collective-permute-start.9 = (bf16[8,16,512]{2,1,0:T(8,128)(2,1)S(1)}, bf16[8,16,512]{2,1,0:T(8,128)(2,1)S(1)}, u32[]{:S(2)}, u32[]{:S(2)}) collective-permute-start(bf16[8,16,512]{2,1,0:T(8,128)(2,1)S(1)} %get-tuple-element.91), channel_id=1, source_target_pairs={{0,2},{1,3},{2,0},{3,1},{4,6},{5,7},{6,4},{7,5},{8,10},{9,11},{10,... | collective-permute-start | bytes 393224 | tf_op jit(solution)/shard_map/ppermute | solution.py:25
  22.4 0.0 collective-permute-done.3.refs_3_
  22.4 1.4 %collective-permute-start.10 = (bf16[8,16,512]{2,1,0:T(8,128)(2,1)S(1)}, bf16[8,16,512]{2,1,0:T(8,128)(2,1)S(1)}, u32[]{:S(2)}, u32[]{:S(2)}) collective-permute-start(bf16[8,16,512]{2,1,0:T(8,128)(2,1)S(1)} %get-tuple-element.92), channel_id=1, source_target_pairs={{0,3},{1,2},{2,1},{3,0},{4,7},{5,6},{6,5},{7,4},{8,11},{9,10},{10,... | collective-permute-start | bytes 393224 | tf_op jit(solution)/shard_map/ppermute | solution.py:25
  23.8 0.0 collective-permute-done.4.refs_4_
  23.8 1.4 %collective-permute-done.5.refs_5_ = bf16[7,16,512]{2,1,0:T(8,128)(2,1)S(1)} collective-permute-done((bf16[7,16,512]{2,1,0:T(8,128)(2,1)S(1)}, bf16[7,16,512]{2,1,0:T(8,128)(2,1)S(1)}, u32[]{:S(2)}, u32[]{:S(2)}) %collective-permute-start.5) | collective-permute-done | bytes 114720 | tf_op jit(solution)/shard_map/ppermute | solution.py:25
  25.2 0.0 collective-permute-done.6.refs_2_
  25.2 0.0 copy-done.2
  25.2 0.0 copy-done.3
  25.2 4.9 %block.2 = (bf16[8,16,512]{2,1,0:T(8,128)(2,1)S(1)}, bf16[8,16,512]{2,1,0:T(8,128)(2,1)S(1)}, bf16[8,16,512]{2,1,0:T(8,128)(2,1)S(1)}, bf16[8,16,512]{2,1,0:T(8,128)(2,1)S(1)}) custom-call(s32[79]{0:T(128)S(4)} %get-tuple-element.65.refs_0_, bf16[32,16,512]{2,1,0:T(8,128)(2,1)S(1)} %get-tuple-element.70.refs_1_, ...), custom_call_target="tpu_custom_call" | custom-call | flops 10000000000 | tf_op jit(solution)/shard_map/block/pallas_call | solution.py:217
  30.1 2.4 %collective-permute-start.14 = (bf16[8,16,512]{2,1,0:T(8,128)(2,1)S(1)}, bf16[8,16,512]{2,1,0:T(8,128)(2,1)S(1)}, u32[]{:S(2)}, u32[]{:S(2)}) collective-permute-start(bf16[8,16,512]{2,1,0:T(8,128)(2,1)S(1)} %get-tuple-element.93), channel_id=1, source_target_pairs={{0,3},{1,2},{2,1},{3,0},{4,7},{5,6},{6,5},{7,4},{8,11},{9,10},{10,... | collective-permute-start | bytes 393224 | tf_op jit(solution)/shard_map/ppermute | solution.py:25
  32.5 0.0 collective-permute-done.9.refs_3_
  32.5 0.0 collective-permute-done.10.refs_4_
  32.5 0.1 select.3
  32.5 0.4 collective-permute-start.11
  32.9 1.5 %collective-permute-start.12 = (bf16[7,16,512]{2,1,0:T(8,128)(2,1)S(1)}, bf16[7,16,512]{2,1,0:T(8,128)(2,1)S(1)}, u32[]{:S(2)}, u32[]{:S(2)}) collective-permute-start(bf16[7,16,512]{2,1,0:T(8,128)(2,1)S(1)} %get-tuple-element.99), channel_id=1, source_target_pairs={{0,8},{4,12},{8,0},{12,4},{1,9},{5,13},{9,1},{13,5},{2,10},{6,14},... | collective-permute-start | bytes 344072 | tf_op jit(solution)/shard_map/ppermute | solution.py:25
  34.4 0.0 collective-permute-start.13
  34.5 3.0 %collective-permute-start.7 = (bf16[8,16,512]{2,1,0:T(8,128)(2,1)S(1)}, bf16[8,16,512]{2,1,0:T(8,128)(2,1)S(1)}, u32[]{:S(2)}, u32[]{:S(2)}) collective-permute-start(bf16[8,16,512]{2,1,0:T(8,128)(2,1)S(1)} %get-tuple-element.87), channel_id=1, source_target_pairs={{0,1},{1,0},{2,3},{3,2},{4,5},{5,4},{6,7},{7,6},{8,9},{9,8},{10,11... | collective-permute-start | bytes 393224 | tf_op jit(solution)/shard_map/ppermute | solution.py:25
  37.5 0.0 collective-permute-done.11.refs_3_
  37.5 0.4 collective-permute-start.8
  38.0 0.9 %collective-permute-done.12.refs_4_ = bf16[7,16,512]{2,1,0:T(8,128)(2,1)S(1)} collective-permute-done((bf16[7,16,512]{2,1,0:T(8,128)(2,1)S(1)}, bf16[7,16,512]{2,1,0:T(8,128)(2,1)S(1)}, u32[]{:S(2)}, u32[]{:S(2)}) %collective-permute-start.12) | collective-permute-done | bytes 114720 | tf_op jit(solution)/shard_map/ppermute | solution.py:25
  38.9 1.0 %collective-permute-done.13.refs_5_ = bf16[7,16,512]{2,1,0:T(8,128)(2,1)S(1)} collective-permute-done((bf16[7,16,512]{2,1,0:T(8,128)(2,1)S(1)}, bf16[7,16,512]{2,1,0:T(8,128)(2,1)S(1)}, u32[]{:S(2)}, u32[]{:S(2)}) %collective-permute-start.13) | collective-permute-done | bytes 114720 | tf_op jit(solution)/shard_map/ppermute | solution.py:25
  39.9 0.0 collective-permute-done.14.refs_4_
  39.9 4.9 %block.3 = (bf16[8,16,512]{2,1,0:T(8,128)(2,1)S(1)}, bf16[8,16,512]{2,1,0:T(8,128)(2,1)S(1)}, bf16[8,16,512]{2,1,0:T(8,128)(2,1)S(1)}, bf16[8,16,512]{2,1,0:T(8,128)(2,1)S(1)}) custom-call(s32[79]{0:T(128)S(4)} %get-tuple-element.65.refs_0_, bf16[32,16,512]{2,1,0:T(8,128)(2,1)S(1)} %get-tuple-element.102.refs_1_, ...), custom_call_target="tpu_custom_call" | custom-call | flops 10000000000 | tf_op jit(solution)/shard_map/block/pallas_call | solution.py:217
  44.8 3.4 %collective-permute-start.15 = (bf16[8,16,512]{2,1,0:T(8,128)(2,1)S(1)}, bf16[8,16,512]{2,1,0:T(8,128)(2,1)S(1)}, u32[]{:S(2)}, u32[]{:S(2)}) collective-permute-start(bf16[8,16,512]{2,1,0:T(8,128)(2,1)S(1)} %get-tuple-element.108), channel_id=1, source_target_pairs={{0,1},{1,0},{2,3},{3,2},{4,5},{5,4},{6,7},{7,6},{8,9},{9,8},{10,11... | collective-permute-start | bytes 393224 | tf_op jit(solution)/shard_map/ppermute | solution.py:25
  48.2 0.5 collective-permute-start.16
  48.7 1.9 %collective-permute-start.17 = (bf16[8,16,512]{2,1,0:T(8,128)(2,1)S(1)}, bf16[8,16,512]{2,1,0:T(8,128)(2,1)S(1)}, u32[]{:S(2)}, u32[]{:S(2)}) collective-permute-start(bf16[8,16,512]{2,1,0:T(8,128)(2,1)S(1)} %get-tuple-element.110), channel_id=1, source_target_pairs={{0,3},{1,2},{2,1},{3,0},{4,7},{5,6},{6,5},{7,4},{8,11},{9,10},{10,... | collective-permute-start | bytes 393224 | tf_op jit(solution)/shard_map/ppermute | solution.py:25
  50.6 0.0 collective-permute-done.7.refs_2_
  50.6 0.0 collective-permute-done.8.refs_3_
  50.6 3.9 %collective-permute-done.15.refs_6_ = bf16[8,16,512]{2,1,0:T(8,128)(2,1)S(1)} collective-permute-done((bf16[8,16,512]{2,1,0:T(8,128)(2,1)S(1)}, bf16[8,16,512]{2,1,0:T(8,128)(2,1)S(1)}, u32[]{:S(2)}, u32[]{:S(2)}) %collective-permute-start.15) | collective-permute-done | bytes 131104 | tf_op jit(solution)/shard_map/ppermute | solution.py:25
  54.6 6.5 %collective-permute-done.16.refs_7_ = bf16[8,16,512]{2,1,0:T(8,128)(2,1)S(1)} collective-permute-done((bf16[8,16,512]{2,1,0:T(8,128)(2,1)S(1)}, bf16[8,16,512]{2,1,0:T(8,128)(2,1)S(1)}, u32[]{:S(2)}, u32[]{:S(2)}) %collective-permute-start.16) | collective-permute-done | bytes 131104 | tf_op jit(solution)/shard_map/ppermute | solution.py:25
  61.1 0.0 collective-permute-done.17.refs_8_
  61.1 1.0 %assemble.1 = bf16[8,8,16,512]{3,2,1,0:T(8,128)(2,1)} custom-call(s32[79]{0:T(128)S(4)} %get-tuple-element.65.refs_0_, bf16[8,16,512]{2,1,0:T(8,128)(2,1)S(1)} %get-tuple-element.86.refs_1_, bf16[8,16,512]{2,1,0:T(8,128)(2,1)S(1)} %collective-permute-done.7.refs_2_, bf16[8,16,512]{2,1,0:T(8,128)(2,1)S(1)} %collective-permute-done.8.refs_3_, ...), custom_call_target="tpu_custom_call" | custom-call | tf_op jit(solution)/shard_map/assemble/pallas_call | solution.py:256
Async XLA Ops:
  0.0 7.2 %copy-start.1 = (s32[3,32]{1,0:T(4,128)S(1)}, s32[3,32]{1,0:T(4,128)}, u32[]{:S(2)}) copy-start(s32[3,32]{1,0:T(4,128)} %merge_num) | copy-start | bytes 1156
  0.0 7.2 %copy-start = (s32[3,32]{1,0:T(4,128)S(1)}, s32[3,32]{1,0:T(4,128)}, u32[]{:S(2)}) copy-start(s32[3,32]{1,0:T(4,128)} %src) | copy-start | bytes 1156
  1.4 9.5 %collective-permute-start = (bf16[8,16,512]{2,1,0:T(8,128)(2,1)S(1)}, bf16[8,16,512]{2,1,0:T(8,128)(2,1)S(1)}, u32[]{:S(2)}, u32[]{:S(2)}) collective-permute-start(bf16[8,16,512]{2,1,0:T(8,128)(2,1)S(1)} %get-tuple-element.64), channel_id=1, source_target_pairs={{0,1},{1,0},{2,3},{3,2},{4,5},{5,4},{6,7},{7,6},{8,9},{9,8},{10,11... | collective-permute-start | bytes 393224 | tf_op jit(solution)/shard_map/ppermute | solution.py:25
  4.5 12.9 %collective-permute-start.1 = (bf16[8,16,512]{2,1,0:T(8,128)(2,1)S(1)}, bf16[8,16,512]{2,1,0:T(8,128)(2,1)S(1)}, u32[]{:S(2)}, u32[]{:S(2)}) collective-permute-start(bf16[8,16,512]{2,1,0:T(8,128)(2,1)S(1)} %get-tuple-element.68), channel_id=1, source_target_pairs={{0,2},{1,3},{2,0},{3,1},{4,6},{5,7},{6,4},{7,5},{8,10},{9,11},{10,... | collective-permute-start | bytes 393224 | tf_op jit(solution)/shard_map/ppermute | solution.py:25
  7.1 10.3 %collective-permute-start.2 = (bf16[8,16,512]{2,1,0:T(8,128)(2,1)S(1)}, bf16[8,16,512]{2,1,0:T(8,128)(2,1)S(1)}, u32[]{:S(2)}, u32[]{:S(2)}) collective-permute-start(bf16[8,16,512]{2,1,0:T(8,128)(2,1)S(1)} %get-tuple-element.69), channel_id=1, source_target_pairs={{0,3},{1,2},{2,1},{3,0},{4,7},{5,6},{6,5},{7,4},{8,11},{9,10},{10,... | collective-permute-start | bytes 393224 | tf_op jit(solution)/shard_map/ppermute | solution.py:25
  7.2 18.0 %copy-start.2 = (f32[512]{0:T(512)S(1)}, f32[512]{0:T(512)}, u32[]{:S(2)}) copy-start(f32[512]{0:T(512)} %param.14) | copy-start | bytes 6148
  7.2 18.0 %copy-start.3 = (f32[512]{0:T(512)S(1)}, f32[512]{0:T(512)}, u32[]{:S(2)}) copy-start(f32[512]{0:T(512)} %param.19) | copy-start | bytes 6148
  11.0 14.2 %collective-permute-start.6 = (bf16[8,16,512]{2,1,0:T(8,128)(2,1)S(1)}, bf16[8,16,512]{2,1,0:T(8,128)(2,1)S(1)}, u32[]{:S(2)}, u32[]{:S(2)}) collective-permute-start(bf16[8,16,512]{2,1,0:T(8,128)(2,1)S(1)} %get-tuple-element.75), channel_id=1, source_target_pairs={{0,1},{1,0},{2,3},{3,2},{4,5},{5,4},{6,7},{7,6},{8,9},{9,8},{10,11... | collective-permute-start | bytes 393224 | tf_op jit(solution)/shard_map/ppermute | solution.py:25
  17.5 4.9 %collective-permute-start.3 = (bf16[7,16,512]{2,1,0:T(8,128)(2,1)S(1)}, bf16[7,16,512]{2,1,0:T(8,128)(2,1)S(1)}, u32[]{:S(2)}, u32[]{:S(2)}) collective-permute-start(bf16[7,16,512]{2,1,0:T(8,128)(2,1)S(1)} %get-tuple-element.72), channel_id=1, source_target_pairs={{0,4},{4,0},{8,12},{12,8},{1,5},{5,1},{9,13},{13,9},{2,6},{6,2},{1... | collective-permute-start | bytes 344072 | tf_op jit(solution)/shard_map/ppermute | solution.py:25
  17.6 6.2 %collective-permute-start.4 = (bf16[7,16,512]{2,1,0:T(8,128)(2,1)S(1)}, bf16[7,16,512]{2,1,0:T(8,128)(2,1)S(1)}, u32[]{:S(2)}, u32[]{:S(2)}) collective-permute-start(bf16[7,16,512]{2,1,0:T(8,128)(2,1)S(1)} %get-tuple-element.73), channel_id=1, source_target_pairs={{0,8},{4,12},{8,0},{12,4},{1,9},{5,13},{9,1},{13,5},{2,10},{6,14},... | collective-permute-start | bytes 344072 | tf_op jit(solution)/shard_map/ppermute | solution.py:25
  19.2 6.0 %collective-permute-start.5 = (bf16[7,16,512]{2,1,0:T(8,128)(2,1)S(1)}, bf16[7,16,512]{2,1,0:T(8,128)(2,1)S(1)}, u32[]{:S(2)}, u32[]{:S(2)}) collective-permute-start(bf16[7,16,512]{2,1,0:T(8,128)(2,1)S(1)} %get-tuple-element.74), channel_id=1, source_target_pairs={{0,12},{4,8},{8,4},{12,0},{1,13},{5,9},{9,5},{13,1},{2,14},{6,10},... | collective-permute-start | bytes 344072 | tf_op jit(solution)/shard_map/ppermute | solution.py:25
  19.5 13.0 %collective-permute-start.9 = (bf16[8,16,512]{2,1,0:T(8,128)(2,1)S(1)}, bf16[8,16,512]{2,1,0:T(8,128)(2,1)S(1)}, u32[]{:S(2)}, u32[]{:S(2)}) collective-permute-start(bf16[8,16,512]{2,1,0:T(8,128)(2,1)S(1)} %get-tuple-element.91), channel_id=1, source_target_pairs={{0,2},{1,3},{2,0},{3,1},{4,6},{5,7},{6,4},{7,5},{8,10},{9,11},{10,... | collective-permute-start | bytes 393224 | tf_op jit(solution)/shard_map/ppermute | solution.py:25
  22.4 10.0 %collective-permute-start.10 = (bf16[8,16,512]{2,1,0:T(8,128)(2,1)S(1)}, bf16[8,16,512]{2,1,0:T(8,128)(2,1)S(1)}, u32[]{:S(2)}, u32[]{:S(2)}) collective-permute-start(bf16[8,16,512]{2,1,0:T(8,128)(2,1)S(1)} %get-tuple-element.92), channel_id=1, source_target_pairs={{0,3},{1,2},{2,1},{3,0},{4,7},{5,6},{6,5},{7,4},{8,11},{9,10},{10,... | collective-permute-start | bytes 393224 | tf_op jit(solution)/shard_map/ppermute | solution.py:25
  30.1 9.8 %collective-permute-start.14 = (bf16[8,16,512]{2,1,0:T(8,128)(2,1)S(1)}, bf16[8,16,512]{2,1,0:T(8,128)(2,1)S(1)}, u32[]{:S(2)}, u32[]{:S(2)}) collective-permute-start(bf16[8,16,512]{2,1,0:T(8,128)(2,1)S(1)} %get-tuple-element.93), channel_id=1, source_target_pairs={{0,3},{1,2},{2,1},{3,0},{4,7},{5,6},{6,5},{7,4},{8,11},{9,10},{10,... | collective-permute-start | bytes 393224 | tf_op jit(solution)/shard_map/ppermute | solution.py:25
  32.5 5.0 %collective-permute-start.11 = (bf16[7,16,512]{2,1,0:T(8,128)(2,1)S(1)}, bf16[7,16,512]{2,1,0:T(8,128)(2,1)S(1)}, u32[]{:S(2)}, u32[]{:S(2)}) collective-permute-start(bf16[7,16,512]{2,1,0:T(8,128)(2,1)S(1)} %get-tuple-element.98), channel_id=1, source_target_pairs={{0,4},{4,0},{8,12},{12,8},{1,5},{5,1},{9,13},{13,9},{2,6},{6,2},{1... | collective-permute-start | bytes 344072 | tf_op jit(solution)/shard_map/ppermute | solution.py:25
  32.9 6.0 %collective-permute-start.12 = (bf16[7,16,512]{2,1,0:T(8,128)(2,1)S(1)}, bf16[7,16,512]{2,1,0:T(8,128)(2,1)S(1)}, u32[]{:S(2)}, u32[]{:S(2)}) collective-permute-start(bf16[7,16,512]{2,1,0:T(8,128)(2,1)S(1)} %get-tuple-element.99), channel_id=1, source_target_pairs={{0,8},{4,12},{8,0},{12,4},{1,9},{5,13},{9,1},{13,5},{2,10},{6,14},... | collective-permute-start | bytes 344072 | tf_op jit(solution)/shard_map/ppermute | solution.py:25
  34.4 5.5 %collective-permute-start.13 = (bf16[7,16,512]{2,1,0:T(8,128)(2,1)S(1)}, bf16[7,16,512]{2,1,0:T(8,128)(2,1)S(1)}, u32[]{:S(2)}, u32[]{:S(2)}) collective-permute-start(bf16[7,16,512]{2,1,0:T(8,128)(2,1)S(1)} %get-tuple-element.100), channel_id=1, source_target_pairs={{0,12},{4,8},{8,4},{12,0},{1,13},{5,9},{9,5},{13,1},{2,14},{6,10},... | collective-permute-start | bytes 344072 | tf_op jit(solution)/shard_map/ppermute | solution.py:25
  34.5 16.2 %collective-permute-start.7 = (bf16[8,16,512]{2,1,0:T(8,128)(2,1)S(1)}, bf16[8,16,512]{2,1,0:T(8,128)(2,1)S(1)}, u32[]{:S(2)}, u32[]{:S(2)}) collective-permute-start(bf16[8,16,512]{2,1,0:T(8,128)(2,1)S(1)} %get-tuple-element.87), channel_id=1, source_target_pairs={{0,1},{1,0},{2,3},{3,2},{4,5},{5,4},{6,7},{7,6},{8,9},{9,8},{10,11... | collective-permute-start | bytes 393224 | tf_op jit(solution)/shard_map/ppermute | solution.py:25
  37.5 13.1 %collective-permute-start.8 = (bf16[8,16,512]{2,1,0:T(8,128)(2,1)S(1)}, bf16[8,16,512]{2,1,0:T(8,128)(2,1)S(1)}, u32[]{:S(2)}, u32[]{:S(2)}) collective-permute-start(bf16[8,16,512]{2,1,0:T(8,128)(2,1)S(1)} %get-tuple-element.88), channel_id=1, source_target_pairs={{0,2},{1,3},{2,0},{3,1},{4,6},{5,7},{6,4},{7,5},{8,10},{9,11},{10,... | collective-permute-start | bytes 393224 | tf_op jit(solution)/shard_map/ppermute | solution.py:25
  44.8 9.7 %collective-permute-start.15 = (bf16[8,16,512]{2,1,0:T(8,128)(2,1)S(1)}, bf16[8,16,512]{2,1,0:T(8,128)(2,1)S(1)}, u32[]{:S(2)}, u32[]{:S(2)}) collective-permute-start(bf16[8,16,512]{2,1,0:T(8,128)(2,1)S(1)} %get-tuple-element.108), channel_id=1, source_target_pairs={{0,1},{1,0},{2,3},{3,2},{4,5},{5,4},{6,7},{7,6},{8,9},{9,8},{10,11... | collective-permute-start | bytes 393224 | tf_op jit(solution)/shard_map/ppermute | solution.py:25
  48.2 12.9 %collective-permute-start.16 = (bf16[8,16,512]{2,1,0:T(8,128)(2,1)S(1)}, bf16[8,16,512]{2,1,0:T(8,128)(2,1)S(1)}, u32[]{:S(2)}, u32[]{:S(2)}) collective-permute-start(bf16[8,16,512]{2,1,0:T(8,128)(2,1)S(1)} %get-tuple-element.109), channel_id=1, source_target_pairs={{0,2},{1,3},{2,0},{3,1},{4,6},{5,7},{6,4},{7,5},{8,10},{9,11},{10,... | collective-permute-start | bytes 393224 | tf_op jit(solution)/shard_map/ppermute | solution.py:25
  48.7 12.4 %collective-permute-start.17 = (bf16[8,16,512]{2,1,0:T(8,128)(2,1)S(1)}, bf16[8,16,512]{2,1,0:T(8,128)(2,1)S(1)}, u32[]{:S(2)}, u32[]{:S(2)}) collective-permute-start(bf16[8,16,512]{2,1,0:T(8,128)(2,1)S(1)} %get-tuple-element.110), channel_id=1, source_target_pairs={{0,3},{1,2},{2,1},{3,0},{4,7},{5,6},{6,5},{7,4},{8,11},{9,10},{10,... | collective-permute-start | bytes 393224 | tf_op jit(solution)/shard_map/ppermute | solution.py:25

commit v4 on v3

--- a/solution.py
+++ b/solution.py
@@ -9,7 +9,7 @@
 
 HD = 64
 ROW_TILE = 16
-BLOCK_FF = 512
+BLOCK_FF = 256
 TURNED = 3
 
 VMEM = pltpu.VMEM
@@ -58,6 +58,12 @@
     for owner in range(lay.spaces):
         count[owner] = 0
 
+    def clear(i, carry):
+        table[lay.send + i] = 0
+        return carry
+
+    lax.fori_loop(0, lay.spaces * cap + 1, clear, 0)
+
     def one_request(q, carry):
         frame, brick = lax.div(q, bricks), me * bricks + lax.rem(q, bricks)
         owner = lax.div(src[frame, brick], bricks)
@@ -105,10 +111,14 @@
     )(ids, src_brick, merge_num, *pinned(weights, pltpu.HBM))
 
 
+def far_first(count):
+    return [*range(2, count), *range(1, min(2, count)), 0]
+
+
 def select_kernel(lay, *refs):
     frames = lay.frames
     table = refs[0]
-    parts = refs[1 : 1 + frames]
+    parts = dict(zip(far_first(frames), refs[1 : 1 + frames]))
     stacked = refs[1 + frames]
     outs = refs[2 + frames :]
     mine = table[1]
@@ -145,6 +155,12 @@
         turned, values, (((1,), (1,)), ((), ())), preferred_element_type=jnp.float32
     )
     return out.astype(jnp.bfloat16)
+
+
+def gelu(x):
+    scale = (2.0 / 3.141592653589793) ** 0.5
+    half = 0.5 * x
+    return half + half * jnp.tanh(x * (scale + (scale * 0.044715) * (x * x)))
 
 
 def matmul(a, b):
@@ -203,7 +219,7 @@
     depth = w_in.shape[1]
     step = min(BLOCK_FF, depth)
     for at in range(0, depth, step):
-        part = jax.nn.gelu(matmul(normed2, w_in[:, at : at + step])).astype(jnp.bfloat16)
+        part = gelu(matmul(normed2, w_in[:, at : at + step])).astype(jnp.bfloat16)
         total = total + matmul(part, w_back[at : at + step])
     result[...] = total.astype(jnp.bfloat16).reshape(result.shape)
     mine = table[1]
@@ -232,13 +248,16 @@
     )(*pinned([table], SMEM), stacked, *pieces, *gains, *pinned(weights, VMEM))
 
 
-def assemble_kernel(count, mine_at, *refs):
+def assemble_kernel(steps, chunk, *refs):
+    count = len(steps)
     table = refs[0]
     parts = refs[1 : 1 + count]
-    out, sems = refs[1 + count :]
+    out, sems = refs[-2:]
     copies = [
-        pltpu.make_async_copy(parts[i], out.at[:, mine_at(i, table[1])], sems.at[i])
-        for i in range(count)
+        pltpu.make_async_copy(
+            parts[i], out.at[:, chunk * count + (table[1] ^ k)], sems.at[i]
+        )
+        for i, k in enumerate(steps)
     ]
     for copy in copies:
         copy.start()
@@ -246,22 +265,18 @@
         copy.wait()
 
 
-def assemble(table, parts, frames):
-    count = len(parts)
-    bricks, rows, width = parts[0].shape
-
-    def mine_at(i, mine):
-        return i // frames * frames + (mine ^ (i % frames))
-
+def assemble(table, parts, steps, chunk, shape, base):
+    count = len(steps)
     return pl.pallas_call(
-        functools.partial(assemble_kernel, count, mine_at),
-        out_shape=jax.ShapeDtypeStruct((bricks, count, rows, width), parts[0].dtype),
-        in_specs=[spec(SMEM)] + [spec(VMEM)] * count,
-        out_specs=spec(pl.ANY),
+        functools.partial(assemble_kernel, steps, chunk),
+        out_shape=jax.ShapeDtypeStruct(shape, parts[0].dtype),
+        in_specs=[spec(SMEM)] + [spec(VMEM)] * count + [spec(pltpu.HBM)] * len(base),
+        out_specs=spec(pltpu.HBM),
+        input_output_aliases={1 + count: 0} if base else {},
         scratch_shapes=[pltpu.SemaphoreType.DMA((count,))],
         compiler_params=pltpu.CompilerParams(vmem_limit_bytes=4 << 20),
         name="assemble",
-    )(*pinned([table], SMEM), *parts)
+    )(*pinned([table], SMEM), *parts, *base)
 
 
 def local(tokens, src_brick, merge_num, gain_attn, w_q, w_k, w_v, w_out, gain_mlp, w_in, w_back):
@@ -278,38 +293,44 @@
     gains = (gain_attn[None], gain_mlp[None])
     weights = (w_q, w_k, w_v, w_out, w_in, w_back)
 
-    def across(parts, axis):
-        return [exchange(part, axis, k) for k, part in enumerate(parts, 1)]
-
-    parts = [
-        [
-            lax.dynamic_index_in_dim(cut, c * frames + (mine ^ k), 1, keepdims=False)
-            for k in range(frames)
-        ]
-        for c in range(chunks)
-    ]
-    (src_brick, merge_num), parts = lax.optimization_barrier(((src_brick, merge_num), parts))
-    arrived = [across(parts[0][1:], "frame")]
+    steps = far_first(frames)
+
+    def across(parts, axis, keys):
+        return [exchange(part, axis, k) if k else part for k, part in zip(keys, parts)]
+
+    parts = []
+    for c in range(chunks):
+        parts.append(
+            [
+                lax.dynamic_index_in_dim(cut, c * frames + (mine ^ k), 1, keepdims=False)
+                for k in steps
+            ]
+        )
+        cut, parts[c] = lax.optimization_barrier((cut, parts[c]))
+    (src_brick, merge_num), parts[-1] = lax.optimization_barrier(
+        ((src_brick, merge_num), parts[-1])
+    )
+    arrived = [across(parts[0], "frame", steps)]
     table, *weights = prepare(lay, ids, src_brick, merge_num, weights)
     for c in range(1, chunks):
-        leaving, table, arrived[-1][0] = lax.optimization_barrier(
-            (parts[c][1:], table, arrived[-1][0])
+        parts[c], table, arrived[-1][0] = lax.optimization_barrier(
+            (parts[c], table, arrived[-1][0])
         )
-        arrived.append(across(leaving, "frame"))
+        arrived.append(across(parts[c], "frame", steps))
     back = []
+    stacked, *slots = select(lay, table, arrived[0])
     for c in range(chunks):
-        stacked, *slots = select(lay, table, [parts[c][0]] + arrived[c])
-        pieces = [slots[0]] + across(slots[1:], "space")
-        if c + 1 < chunks:
-            pieces, arrived[c + 1][0] = lax.optimization_barrier((pieces, arrived[c + 1][0]))
-        if c > 0:
-            pieces, back[-1][3] = lax.optimization_barrier((pieces, back[-1][3]))
+        pieces = across(slots, "space", range(spaces))
         done = run_block(lay, table, stacked, pieces, gains, weights)
         if c + 1 < chunks:
-            arrived[c + 1], _ = lax.optimization_barrier((arrived[c + 1], done))
-        returned = across(done[1:], "frame")
-        back.append([done[0]] + returned)
-    out = assemble(table, sum(back, []), frames)
+            arrived[c + 1], done = lax.optimization_barrier((arrived[c + 1], done))
+            stacked, *slots = select(lay, table, arrived[c + 1])
+            slots, done = lax.optimization_barrier((slots, done))
+        back.append(across([done[k] for k in steps], "frame", steps))
+    base = []
+    for c in range(chunks):
+        base = [assemble(table, back[c], steps, c, cut.shape, base)]
+    [out] = base
     return out.reshape(1, bricks, tall, width)
 
 

time: 62.3 us -> 60.8 us (0.976)
  starting transfers between devices: 26.5 us -> 23.1 us
  waiting for transfers between devices: 19.3 us -> 20.3 us
  local copies, waits for them, and re-layouts: 1.43 us -> 2.3 us
    ppermute x18, starting transfers between devices: 26.5 us -> 23.1 us  [exchange(): return lax.ppermute(values, axis, [(i, i ^ step) for i in range(size)])]
    ppermute x18, waiting for transfers between devices: 19.3 us -> 20.3 us  [exchange(): return lax.ppermute(values, axis, [(i, i ^ step) for i in range(size)])]
    squeeze x1 -> x2, local copies, waits for them, and re-layouts: 1.41 us -> 2.29 us  [local(): lax.dynamic_index_in_dim(cut, c * frames + (mine ^ k), 1, keepdims=False)]
    pallas_call x1 -> x2, Pallas kernels: 1.02 us -> 1.64 us  [assemble(): pl.pallas_call(functools.partial(assemble_kernel, steps, chunk), out_shap...]
  transfers between devices with their start and end apart: 18 -> 18, of which waited for: 6 -> 8; matrix products, arithmetic and copies ran while one was open for 0% -> 2% of each run, Pallas kernels for 22% -> 23%
where the time goes in v4:
time: 60.8 us; the launch traced here: 60.6 us
  starting transfers between devices  23.1 us (38%)
  waiting for transfers between devices  20.3 us (33%)
  Pallas kernels  14.8 us (24%)
  local copies, waits for them, and re-layouts  2.3 us (4%)
    ppermute x18, starting transfers between devices, exchange(): return lax.ppermute(values, axis, [(i, i ^ step) for i in range(size)])  23.1 us
    ppermute x18, waiting for transfers between devices, exchange(): return lax.ppermute(values, axis, [(i, i ^ step) for i in range(size)])  20.3 us
    pallas_call x2, Pallas kernels, run_block(): pl.pallas_call(functools.partial(block_kernel, lay), out_shape=(jax.Shape...  9.24 us
    pallas_call x1, Pallas kernels, prepare(): pl.pallas_call(functools.partial(prepare_kernel, lay), out_shape=(pltpu.S...  3.74 us
    squeeze x2, local copies, waits for them, and re-layouts, local(): lax.dynamic_index_in_dim(cut, c * frames + (mine ^ k), 1, keepdims=False)  2.29 us
    pallas_call x2, Pallas kernels, assemble(): pl.pallas_call(functools.partial(assemble_kernel, steps, chunk), out_shap...  1.64 us
  transfers between devices with their start and end apart: 18, of which 8 were waited for; matrix products, arithmetic and copies ran while one was open for 2% of the time, Pallas kernels for 23%

profile of v4, /device:TPU:0, one launch (start us, length us, event | category | flops | bytes accessed | tf_op | source)
XLA Modules:
  0.0 60.6 jit_solution(14990118227779000113)
XLA Ops:
  0.0 0.0 copy-start.1
  0.0 0.0 copy-start
  0.0 1.2 %dynamic-slice_bitcast_fusion.4 = (bf16[8,16,512]{2,1,0:T(8,128)(2,1)S(1)}, bf16[8,16,512]{2,1,0:T(8,128)(2,1)S(1)}, bf16[8,16,512]{2,1,0:T(8,128)(2,1)S(1)}, bf16[8,16,512]{2,1,0:T(8,128)(2,1)S(1)}) fusion(bf16[8,8,16,512]{3,2,1,0:T(8,128)(2,1)} %bitcast.34, s32[]{:T(128)S(6)} %select_n.28, s32[]{:T(128)S(6)} %select_n.27, s32[]{:T(128)S(6)} %select_n.26, ...), kind=kLoop, calls=%fused_computation.4 | loop fusion | bytes 1048592 | tf_op jit(solution)/shard_map/jit(dynamic_index_in_dim)/squeeze | solution.py:305
  1.2 4.1 %collective-permute-start = (bf16[8,16,512]{2,1,0:T(8,128)(2,1)S(1)}, bf16[8,16,512]{2,1,0:T(8,128)(2,1)S(1)}, u32[]{:S(2)}, u32[]{:S(2)}) collective-permute-start(bf16[8,16,512]{2,1,0:T(8,128)(2,1)S(1)} %get-tuple-element.79), channel_id=1, source_target_pairs={{0,2},{1,3},{2,0},{3,1},{4,6},{5,7},{6,4},{7,5},{8,10},{9,11},{10,... | collective-permute-start | bytes 393224 | tf_op jit(solution)/shard_map/ppermute | solution.py:25
  5.3 1.3 %collective-permute-start.4 = (bf16[8,16,512]{2,1,0:T(8,128)(2,1)S(1)}, bf16[8,16,512]{2,1,0:T(8,128)(2,1)S(1)}, u32[]{:S(2)}, u32[]{:S(2)}) collective-permute-start(bf16[8,16,512]{2,1,0:T(8,128)(2,1)S(1)} %get-tuple-element.86), channel_id=1, source_target_pairs={{0,3},{1,2},{2,1},{3,0},{4,7},{5,6},{6,5},{7,4},{8,11},{9,10},{10,... | collective-permute-start | bytes 393224 | tf_op jit(solution)/shard_map/ppermute | solution.py:25
  6.6 0.2 collective-permute-start.5
  6.8 1.1 %dynamic-slice_bitcast_fusion = (bf16[8,16,512]{2,1,0:T(8,128)(2,1)S(1)}, bf16[8,16,512]{2,1,0:T(8,128)(2,1)S(1)}, bf16[8,16,512]{2,1,0:T(8,128)(2,1)S(1)}, bf16[8,16,512]{2,1,0:T(8,128)(2,1)S(1)}) fusion(s32[]{:T(128)S(6)} %select_n.32, s32[]{:T(128)S(6)} %select_n.31, s32[]{:T(128)S(6)} %select_n.30, s32[]{:T(128)S(6)} %select_n.29, ...), kind=kLoop, calls=%fused_computation | loop fusion | bytes 1048592 | tf_op jit(solution)/shard_map/jit(dynamic_index_in_dim)/squeeze | solution.py:305
  8.0 0.1 pad_add_fusion.ids
  8.1 0.0 copy-done.1
  8.1 0.0 copy-done
  8.1 0.0 copy-start.2
  8.1 0.0 copy-start.3
  8.1 3.7 %prepare.1 = (s32[79]{0:T(128)S(4)}, bf16[512,512]{1,0:T(8,128)(2,1)S(1)}, bf16[512,512]{1,0:T(8,128)(2,1)S(1)}, bf16[512,512]{1,0:T(8,128)(2,1)S(1)}, bf16[512,...) custom-call(s32[2]{0:T(128)S(1)} %pad_add_fusion.ids, s32[3,32]{1,0:T(4,128)S(1)} %copy-done, ...), custom_call_target="tpu_custom_call" | custom-call | tf_op jit(solution)/shard_map/prepare/pallas_call | solution.py:98
  11.8 3.4 %collective-permute-done.refs_1_ = bf16[8,16,512]{2,1,0:T(8,128)(2,1)S(1)} collective-permute-done((bf16[8,16,512]{2,1,0:T(8,128)(2,1)S(1)}, bf16[8,16,512]{2,1,0:T(8,128)(2,1)S(1)}, u32[]{:S(2)}, u32[]{:S(2)}) %collective-permute-start) | collective-permute-done | bytes 131104 | tf_op jit(solution)/shard_map/ppermute | solution.py:25
  15.3 0.0 collective-permute-done.4.refs_2_
  15.3 0.5 collective-permute-done.5.refs_3_
  15.8 0.1 select.2
  15.8 0.1 collective-permute-start.6
  15.9 1.6 %collective-permute-start.7 = (bf16[7,16,512]{2,1,0:T(8,128)(2,1)S(1)}, bf16[7,16,512]{2,1,0:T(8,128)(2,1)S(1)}, u32[]{:S(2)}, u32[]{:S(2)}) collective-permute-start(bf16[7,16,512]{2,1,0:T(8,128)(2,1)S(1)} %get-tuple-element.92), channel_id=1, source_target_pairs={{0,8},{4,12},{8,0},{12,4},{1,9},{5,13},{9,1},{13,5},{2,10},{6,14},... | collective-permute-start | bytes 344072 | tf_op jit(solution)/shard_map/ppermute | solution.py:25
  17.6 0.2 collective-permute-start.8
  17.8 4.1 %collective-permute-start.1 = (bf16[8,16,512]{2,1,0:T(8,128)(2,1)S(1)}, bf16[8,16,512]{2,1,0:T(8,128)(2,1)S(1)}, u32[]{:S(2)}, u32[]{:S(2)}) collective-permute-start(bf16[8,16,512]{2,1,0:T(8,128)(2,1)S(1)} %get-tuple-element.81), channel_id=1, source_target_pairs={{0,2},{1,3},{2,0},{3,1},{4,6},{5,7},{6,4},{7,5},{8,10},{9,11},{10,... | collective-permute-start | bytes 393224 | tf_op jit(solution)/shard_map/ppermute | solution.py:25
  21.9 0.4 collective-permute-start.2
  22.3 0.0 collective-permute-done.6.refs_3_
  22.3 0.1 collective-permute-start.3
  22.5 0.0 collective-permute-done.7.refs_4_
  22.5 1.0 %collective-permute-done.8.refs_5_ = bf16[7,16,512]{2,1,0:T(8,128)(2,1)S(1)} collective-permute-done((bf16[7,16,512]{2,1,0:T(8,128)(2,1)S(1)}, bf16[7,16,512]{2,1,0:T(8,128)(2,1)S(1)}, u32[]{:S(2)}, u32[]{:S(2)}) %collective-permute-start.8) | collective-permute-done | bytes 114720 | tf_op jit(solution)/shard_map/ppermute | solution.py:25
  23.5 0.0 copy-done.2
  23.5 0.0 copy-done.3
  23.5 4.6 %block.2 = (bf16[8,16,512]{2,1,0:T(8,128)(2,1)S(1)}, bf16[8,16,512]{2,1,0:T(8,128)(2,1)S(1)}, bf16[8,16,512]{2,1,0:T(8,128)(2,1)S(1)}, bf16[8,16,512]{2,1,0:T(8,128)(2,1)S(1)}) custom-call(s32[79]{0:T(128)S(4)} %get-tuple-element.80.refs_0_, bf16[32,16,512]{2,1,0:T(8,128)(2,1)S(1)} %get-tuple-element.89.refs_1_, ...), custom_call_target="tpu_custom_call" | custom-call | flops 10000000000 | tf_op jit(solution)/shard_map/block/pallas_call | solution.py:233
  28.1 3.7 %collective-permute-done.1.refs_1_ = bf16[8,16,512]{2,1,0:T(8,128)(2,1)S(1)} collective-permute-done((bf16[8,16,512]{2,1,0:T(8,128)(2,1)S(1)}, bf16[8,16,512]{2,1,0:T(8,128)(2,1)S(1)}, u32[]{:S(2)}, u32[]{:S(2)}) %collective-permute-start.1) | collective-permute-done | bytes 131104 | tf_op jit(solution)/shard_map/ppermute | solution.py:25
  31.8 0.0 collective-permute-done.2.refs_2_
  31.8 1.1 %collective-permute-done.3.refs_3_ = bf16[8,16,512]{2,1,0:T(8,128)(2,1)S(1)} collective-permute-done((bf16[8,16,512]{2,1,0:T(8,128)(2,1)S(1)}, bf16[8,16,512]{2,1,0:T(8,128)(2,1)S(1)}, u32[]{:S(2)}, u32[]{:S(2)}) %collective-permute-start.3) | collective-permute-done | bytes 131104 | tf_op jit(solution)/shard_map/ppermute | solution.py:25
  32.9 0.1 select.3
  33.0 0.1 collective-permute-start.9
  33.0 1.6 %collective-permute-start.10 = (bf16[7,16,512]{2,1,0:T(8,128)(2,1)S(1)}, bf16[7,16,512]{2,1,0:T(8,128)(2,1)S(1)}, u32[]{:S(2)}, u32[]{:S(2)}) collective-permute-start(bf16[7,16,512]{2,1,0:T(8,128)(2,1)S(1)} %get-tuple-element.119), channel_id=1, source_target_pairs={{0,8},{4,12},{8,0},{12,4},{1,9},{5,13},{9,1},{13,5},{2,10},{6,14},... | collective-permute-start | bytes 344072 | tf_op jit(solution)/shard_map/ppermute | solution.py:25
  34.6 0.3 collective-permute-start.11
  34.9 2.6 %collective-permute-start.15 = (bf16[8,16,512]{2,1,0:T(8,128)(2,1)S(1)}, bf16[8,16,512]{2,1,0:T(8,128)(2,1)S(1)}, u32[]{:S(2)}, u32[]{:S(2)}) collective-permute-start(bf16[8,16,512]{2,1,0:T(8,128)(2,1)S(1)} %get-tuple-element.125), channel_id=1, source_target_pairs={{0,2},{1,3},{2,0},{3,1},{4,6},{5,7},{6,4},{7,5},{8,10},{9,11},{10,... | collective-permute-start | bytes 393224 | tf_op jit(solution)/shard_map/ppermute | solution.py:25
  37.6 1.8 %collective-permute-start.16 = (bf16[8,16,512]{2,1,0:T(8,128)(2,1)S(1)}, bf16[8,16,512]{2,1,0:T(8,128)(2,1)S(1)}, u32[]{:S(2)}, u32[]{:S(2)}) collective-permute-start(bf16[8,16,512]{2,1,0:T(8,128)(2,1)S(1)} %get-tuple-element.126), channel_id=1, source_target_pairs={{0,3},{1,2},{2,1},{3,0},{4,7},{5,6},{6,5},{7,4},{8,11},{9,10},{10,... | collective-permute-start | bytes 393224 | tf_op jit(solution)/shard_map/ppermute | solution.py:25
  39.3 0.0 collective-permute-done.9.refs_3_
  39.3 0.0 collective-permute-start.17
  39.3 0.0 collective-permute-done.10.refs_4_
  39.3 1.3 %collective-permute-done.11.refs_5_ = bf16[7,16,512]{2,1,0:T(8,128)(2,1)S(1)} collective-permute-done((bf16[7,16,512]{2,1,0:T(8,128)(2,1)S(1)}, bf16[7,16,512]{2,1,0:T(8,128)(2,1)S(1)}, u32[]{:S(2)}, u32[]{:S(2)}) %collective-permute-start.11) | collective-permute-done | bytes 114720 | tf_op jit(solution)/shard_map/ppermute | solution.py:25
  40.6 4.6 %block.3 = (bf16[8,16,512]{2,1,0:T(8,128)(2,1)S(1)}, bf16[8,16,512]{2,1,0:T(8,128)(2,1)S(1)}, bf16[8,16,512]{2,1,0:T(8,128)(2,1)S(1)}, bf16[8,16,512]{2,1,0:T(8,128)(2,1)S(1)}) custom-call(s32[79]{0:T(128)S(4)} %get-tuple-element.80.refs_0_, bf16[32,16,512]{2,1,0:T(8,128)(2,1)S(1)} %get-tuple-element.108.refs_1_, ...), custom_call_target="tpu_custom_call" | custom-call | flops 10000000000 | tf_op jit(solution)/shard_map/block/pallas_call | solution.py:233
  45.2 2.7 %collective-permute-start.12 = (bf16[8,16,512]{2,1,0:T(8,128)(2,1)S(1)}, bf16[8,16,512]{2,1,0:T(8,128)(2,1)S(1)}, u32[]{:S(2)}, u32[]{:S(2)}) collective-permute-start(bf16[8,16,512]{2,1,0:T(8,128)(2,1)S(1)} %get-tuple-element.121), channel_id=1, source_target_pairs={{0,2},{1,3},{2,0},{3,1},{4,6},{5,7},{6,4},{7,5},{8,10},{9,11},{10,... | collective-permute-start | bytes 393224 | tf_op jit(solution)/shard_map/ppermute | solution.py:25
  47.9 1.8 %collective-permute-start.13 = (bf16[8,16,512]{2,1,0:T(8,128)(2,1)S(1)}, bf16[8,16,512]{2,1,0:T(8,128)(2,1)S(1)}, u32[]{:S(2)}, u32[]{:S(2)}) collective-permute-start(bf16[8,16,512]{2,1,0:T(8,128)(2,1)S(1)} %get-tuple-element.122), channel_id=1, source_target_pairs={{0,3},{1,2},{2,1},{3,0},{4,7},{5,6},{6,5},{7,4},{8,11},{9,10},{10,... | collective-permute-start | bytes 393224 | tf_op jit(solution)/shard_map/ppermute | solution.py:25
  49.7 0.0 collective-permute-done.15.refs_1_
  49.7 0.0 collective-permute-start.14
  49.7 0.0 collective-permute-done.16.refs_2_
  49.7 0.0 collective-permute-done.17.refs_3_
  49.7 0.8 %assemble.2.refs_5_ = bf16[8,8,16,512]{3,2,1,0:T(8,128)(2,1)} custom-call(s32[79]{0:T(128)S(4)} %get-tuple-element.80.refs_0_, bf16[8,16,512]{2,1,0:T(8,128)(2,1)S(1)} %collective-permute-done.15.refs_1_, bf16[8,16,512]{2,1,0:T(8,128)(2,1)S(1)} %collective-permute-done.16.refs_2_, bf16[8,16,512]{2,1,0:T(8,128)(2,1)S(1)} %collective-permute-done.17.refs_3_, ...), custom_call_target="tpu_custom_call" | custom-call | tf_op jit(solution)/shard_map/assemble/pallas_call | solution.py:270
  50.6 8.5 %collective-permute-done.12.refs_1_ = bf16[8,16,512]{2,1,0:T(8,128)(2,1)S(1)} collective-permute-done((bf16[8,16,512]{2,1,0:T(8,128)(2,1)S(1)}, bf16[8,16,512]{2,1,0:T(8,128)(2,1)S(1)}, u32[]{:S(2)}, u32[]{:S(2)}) %collective-permute-start.12) | collective-permute-done | bytes 131104 | tf_op jit(solution)/shard_map/ppermute | solution.py:25
  59.1 0.0 collective-permute-done.13.refs_2_
  59.1 0.8 %collective-permute-done.14.refs_3_ = bf16[8,16,512]{2,1,0:T(8,128)(2,1)S(1)} collective-permute-done((bf16[8,16,512]{2,1,0:T(8,128)(2,1)S(1)}, bf16[8,16,512]{2,1,0:T(8,128)(2,1)S(1)}, u32[]{:S(2)}, u32[]{:S(2)}) %collective-permute-start.14) | collective-permute-done | bytes 131104 | tf_op jit(solution)/shard_map/ppermute | solution.py:25
  59.8 0.8 %assemble.3 = bf16[8,8,16,512]{3,2,1,0:T(8,128)(2,1)} custom-call(s32[79]{0:T(128)S(4)} %get-tuple-element.80.refs_0_, bf16[8,16,512]{2,1,0:T(8,128)(2,1)S(1)} %collective-permute-done.12.refs_1_, bf16[8,16,512]{2,1,0:T(8,128)(2,1)S(1)} %collective-permute-done.13.refs_2_, ...), custom_call_target="tpu_custom_call", output_to_operand_aliasing={{}: (5, {})} | custom-call | tf_op jit(solution)/shard_map/assemble/pallas_call | solution.py:270
Async XLA Ops:
  0.0 8.1 %copy-start.1 = (s32[3,32]{1,0:T(4,128)S(1)}, s32[3,32]{1,0:T(4,128)}, u32[]{:S(2)}) copy-start(s32[3,32]{1,0:T(4,128)} %merge_num) | copy-start | bytes 1156
  0.0 8.1 %copy-start = (s32[3,32]{1,0:T(4,128)S(1)}, s32[3,32]{1,0:T(4,128)}, u32[]{:S(2)}) copy-start(s32[3,32]{1,0:T(4,128)} %src) | copy-start | bytes 1156
  1.2 14.1 %collective-permute-start = (bf16[8,16,512]{2,1,0:T(8,128)(2,1)S(1)}, bf16[8,16,512]{2,1,0:T(8,128)(2,1)S(1)}, u32[]{:S(2)}, u32[]{:S(2)}) collective-permute-start(bf16[8,16,512]{2,1,0:T(8,128)(2,1)S(1)} %get-tuple-element.79), channel_id=1, source_target_pairs={{0,2},{1,3},{2,0},{3,1},{4,6},{5,7},{6,4},{7,5},{8,10},{9,11},{10,... | collective-permute-start | bytes 393224 | tf_op jit(solution)/shard_map/ppermute | solution.py:25
  5.3 10.0 %collective-permute-start.4 = (bf16[8,16,512]{2,1,0:T(8,128)(2,1)S(1)}, bf16[8,16,512]{2,1,0:T(8,128)(2,1)S(1)}, u32[]{:S(2)}, u32[]{:S(2)}) collective-permute-start(bf16[8,16,512]{2,1,0:T(8,128)(2,1)S(1)} %get-tuple-element.86), channel_id=1, source_target_pairs={{0,3},{1,2},{2,1},{3,0},{4,7},{5,6},{6,5},{7,4},{8,11},{9,10},{10,... | collective-permute-start | bytes 393224 | tf_op jit(solution)/shard_map/ppermute | solution.py:25
  6.6 9.2 %collective-permute-start.5 = (bf16[8,16,512]{2,1,0:T(8,128)(2,1)S(1)}, bf16[8,16,512]{2,1,0:T(8,128)(2,1)S(1)}, u32[]{:S(2)}, u32[]{:S(2)}) collective-permute-start(bf16[8,16,512]{2,1,0:T(8,128)(2,1)S(1)} %get-tuple-element.87), channel_id=1, source_target_pairs={{0,1},{1,0},{2,3},{3,2},{4,5},{5,4},{6,7},{7,6},{8,9},{9,8},{10,11... | collective-permute-start | bytes 393224 | tf_op jit(solution)/shard_map/ppermute | solution.py:25
  8.1 15.4 %copy-start.2 = (f32[512]{0:T(512)S(1)}, f32[512]{0:T(512)}, u32[]{:S(2)}) copy-start(f32[512]{0:T(512)} %param.14) | copy-start | bytes 6148
  8.1 15.4 %copy-start.3 = (f32[512]{0:T(512)S(1)}, f32[512]{0:T(512)}, u32[]{:S(2)}) copy-start(f32[512]{0:T(512)} %param.19) | copy-start | bytes 6148
  15.8 6.5 %collective-permute-start.6 = (bf16[7,16,512]{2,1,0:T(8,128)(2,1)S(1)}, bf16[7,16,512]{2,1,0:T(8,128)(2,1)S(1)}, u32[]{:S(2)}, u32[]{:S(2)}) collective-permute-start(bf16[7,16,512]{2,1,0:T(8,128)(2,1)S(1)} %get-tuple-element.91), channel_id=1, source_target_pairs={{0,4},{4,0},{8,12},{12,8},{1,5},{5,1},{9,13},{13,9},{2,6},{6,2},{1... | collective-permute-start | bytes 344072 | tf_op jit(solution)/shard_map/ppermute | solution.py:25
  15.9 6.5 %collective-permute-start.7 = (bf16[7,16,512]{2,1,0:T(8,128)(2,1)S(1)}, bf16[7,16,512]{2,1,0:T(8,128)(2,1)S(1)}, u32[]{:S(2)}, u32[]{:S(2)}) collective-permute-start(bf16[7,16,512]{2,1,0:T(8,128)(2,1)S(1)} %get-tuple-element.92), channel_id=1, source_target_pairs={{0,8},{4,12},{8,0},{12,4},{1,9},{5,13},{9,1},{13,5},{2,10},{6,14},... | collective-permute-start | bytes 344072 | tf_op jit(solution)/shard_map/ppermute | solution.py:25
  17.6 5.9 %collective-permute-start.8 = (bf16[7,16,512]{2,1,0:T(8,128)(2,1)S(1)}, bf16[7,16,512]{2,1,0:T(8,128)(2,1)S(1)}, u32[]{:S(2)}, u32[]{:S(2)}) collective-permute-start(bf16[7,16,512]{2,1,0:T(8,128)(2,1)S(1)} %get-tuple-element.93), channel_id=1, source_target_pairs={{0,12},{4,8},{8,4},{12,0},{1,13},{5,9},{9,5},{13,1},{2,14},{6,10},... | collective-permute-start | bytes 344072 | tf_op jit(solution)/shard_map/ppermute | solution.py:25
  17.8 14.0 %collective-permute-start.1 = (bf16[8,16,512]{2,1,0:T(8,128)(2,1)S(1)}, bf16[8,16,512]{2,1,0:T(8,128)(2,1)S(1)}, u32[]{:S(2)}, u32[]{:S(2)}) collective-permute-start(bf16[8,16,512]{2,1,0:T(8,128)(2,1)S(1)} %get-tuple-element.81), channel_id=1, source_target_pairs={{0,2},{1,3},{2,0},{3,1},{4,6},{5,7},{6,4},{7,5},{8,10},{9,11},{10,... | collective-permute-start | bytes 393224 | tf_op jit(solution)/shard_map/ppermute | solution.py:25
  21.9 9.9 %collective-permute-start.2 = (bf16[8,16,512]{2,1,0:T(8,128)(2,1)S(1)}, bf16[8,16,512]{2,1,0:T(8,128)(2,1)S(1)}, u32[]{:S(2)}, u32[]{:S(2)}) collective-permute-start(bf16[8,16,512]{2,1,0:T(8,128)(2,1)S(1)} %get-tuple-element.82), channel_id=1, source_target_pairs={{0,3},{1,2},{2,1},{3,0},{4,7},{5,6},{6,5},{7,4},{8,11},{9,10},{10,... | collective-permute-start | bytes 393224 | tf_op jit(solution)/shard_map/ppermute | solution.py:25
  22.3 10.5 %collective-permute-start.3 = (bf16[8,16,512]{2,1,0:T(8,128)(2,1)S(1)}, bf16[8,16,512]{2,1,0:T(8,128)(2,1)S(1)}, u32[]{:S(2)}, u32[]{:S(2)}) collective-permute-start(bf16[8,16,512]{2,1,0:T(8,128)(2,1)S(1)} %get-tuple-element.83), channel_id=1, source_target_pairs={{0,1},{1,0},{2,3},{3,2},{4,5},{5,4},{6,7},{7,6},{8,9},{9,8},{10,11... | collective-permute-start | bytes 393224 | tf_op jit(solution)/shard_map/ppermute | solution.py:25
  33.0 6.4 %collective-permute-start.9 = (bf16[7,16,512]{2,1,0:T(8,128)(2,1)S(1)}, bf16[7,16,512]{2,1,0:T(8,128)(2,1)S(1)}, u32[]{:S(2)}, u32[]{:S(2)}) collective-permute-start(bf16[7,16,512]{2,1,0:T(8,128)(2,1)S(1)} %get-tuple-element.118), channel_id=1, source_target_pairs={{0,4},{4,0},{8,12},{12,8},{1,5},{5,1},{9,13},{13,9},{2,6},{6,2},{1... | collective-permute-start | bytes 344072 | tf_op jit(solution)/shard_map/ppermute | solution.py:25
  33.0 6.3 %collective-permute-start.10 = (bf16[7,16,512]{2,1,0:T(8,128)(2,1)S(1)}, bf16[7,16,512]{2,1,0:T(8,128)(2,1)S(1)}, u32[]{:S(2)}, u32[]{:S(2)}) collective-permute-start(bf16[7,16,512]{2,1,0:T(8,128)(2,1)S(1)} %get-tuple-element.119), channel_id=1, source_target_pairs={{0,8},{4,12},{8,0},{12,4},{1,9},{5,13},{9,1},{13,5},{2,10},{6,14},... | collective-permute-start | bytes 344072 | tf_op jit(solution)/shard_map/ppermute | solution.py:25
  34.6 6.0 %collective-permute-start.11 = (bf16[7,16,512]{2,1,0:T(8,128)(2,1)S(1)}, bf16[7,16,512]{2,1,0:T(8,128)(2,1)S(1)}, u32[]{:S(2)}, u32[]{:S(2)}) collective-permute-start(bf16[7,16,512]{2,1,0:T(8,128)(2,1)S(1)} %get-tuple-element.120), channel_id=1, source_target_pairs={{0,12},{4,8},{8,4},{12,0},{1,13},{5,9},{9,5},{13,1},{2,14},{6,10},... | collective-permute-start | bytes 344072 | tf_op jit(solution)/shard_map/ppermute | solution.py:25
  34.9 14.8 %collective-permute-start.15 = (bf16[8,16,512]{2,1,0:T(8,128)(2,1)S(1)}, bf16[8,16,512]{2,1,0:T(8,128)(2,1)S(1)}, u32[]{:S(2)}, u32[]{:S(2)}) collective-permute-start(bf16[8,16,512]{2,1,0:T(8,128)(2,1)S(1)} %get-tuple-element.125), channel_id=1, source_target_pairs={{0,2},{1,3},{2,0},{3,1},{4,6},{5,7},{6,4},{7,5},{8,10},{9,11},{10,... | collective-permute-start | bytes 393224 | tf_op jit(solution)/shard_map/ppermute | solution.py:25
  37.6 12.2 %collective-permute-start.16 = (bf16[8,16,512]{2,1,0:T(8,128)(2,1)S(1)}, bf16[8,16,512]{2,1,0:T(8,128)(2,1)S(1)}, u32[]{:S(2)}, u32[]{:S(2)}) collective-permute-start(bf16[8,16,512]{2,1,0:T(8,128)(2,1)S(1)} %get-tuple-element.126), channel_id=1, source_target_pairs={{0,3},{1,2},{2,1},{3,0},{4,7},{5,6},{6,5},{7,4},{8,11},{9,10},{10,... | collective-permute-start | bytes 393224 | tf_op jit(solution)/shard_map/ppermute | solution.py:25
  39.3 10.4 %collective-permute-start.17 = (bf16[8,16,512]{2,1,0:T(8,128)(2,1)S(1)}, bf16[8,16,512]{2,1,0:T(8,128)(2,1)S(1)}, u32[]{:S(2)}, u32[]{:S(2)}) collective-permute-start(bf16[8,16,512]{2,1,0:T(8,128)(2,1)S(1)} %get-tuple-element.127), channel_id=1, source_target_pairs={{0,1},{1,0},{2,3},{3,2},{4,5},{5,4},{6,7},{7,6},{8,9},{9,8},{10,11... | collective-permute-start | bytes 393224 | tf_op jit(solution)/shard_map/ppermute | solution.py:25
  45.2 13.8 %collective-permute-start.12 = (bf16[8,16,512]{2,1,0:T(8,128)(2,1)S(1)}, bf16[8,16,512]{2,1,0:T(8,128)(2,1)S(1)}, u32[]{:S(2)}, u32[]{:S(2)}) collective-permute-start(bf16[8,16,512]{2,1,0:T(8,128)(2,1)S(1)} %get-tuple-element.121), channel_id=1, source_target_pairs={{0,2},{1,3},{2,0},{3,1},{4,6},{5,7},{6,4},{7,5},{8,10},{9,11},{10,... | collective-permute-start | bytes 393224 | tf_op jit(solution)/shard_map/ppermute | solution.py:25
  47.9 11.1 %collective-permute-start.13 = (bf16[8,16,512]{2,1,0:T(8,128)(2,1)S(1)}, bf16[8,16,512]{2,1,0:T(8,128)(2,1)S(1)}, u32[]{:S(2)}, u32[]{:S(2)}) collective-permute-start(bf16[8,16,512]{2,1,0:T(8,128)(2,1)S(1)} %get-tuple-element.122), channel_id=1, source_target_pairs={{0,3},{1,2},{2,1},{3,0},{4,7},{5,6},{6,5},{7,4},{8,11},{9,10},{10,... | collective-permute-start | bytes 393224 | tf_op jit(solution)/shard_map/ppermute | solution.py:25
  49.7 10.1 %collective-permute-start.14 = (bf16[8,16,512]{2,1,0:T(8,128)(2,1)S(1)}, bf16[8,16,512]{2,1,0:T(8,128)(2,1)S(1)}, u32[]{:S(2)}, u32[]{:S(2)}) collective-permute-start(bf16[8,16,512]{2,1,0:T(8,128)(2,1)S(1)} %get-tuple-element.123), channel_id=1, source_target_pairs={{0,1},{1,0},{2,3},{3,2},{4,5},{5,4},{6,7},{7,6},{8,9},{9,8},{10,11... | collective-permute-start | bytes 393224 | tf_op jit(solution)/shard_map/ppermute | solution.py:25

commit v5 on v4

--- a/solution.py
+++ b/solution.py
@@ -167,26 +167,61 @@
     return jnp.dot(a, b, preferred_element_type=jnp.float32)
 
 
+def finish(merged, context, gain, w_o, w_in, w_back):
+    mid = (merged.astype(jnp.float32) + matmul(context, w_o[...])).astype(jnp.bfloat16)
+    normed = normalise(mid, gain[...])
+    total = mid.astype(jnp.float32)
+    depth = w_in.shape[1]
+    step = min(BLOCK_FF, depth)
+    for at in range(0, depth, step):
+        part = gelu(matmul(normed, w_in[:, at : at + step])).astype(jnp.bfloat16)
+        total = total + matmul(part, w_back[at : at + step])
+    return total.astype(jnp.bfloat16)
+
+
+def first_kernel(lay, *refs):
+    stacked, gain_a, gain_m, w_q, w_k, w_v, w_o, w_in, w_back, key, val, out = refs
+    merged = stacked[: lay.bricks].reshape(-1, stacked.shape[2])
+    normed = normalise(merged, gain_a[...])
+    key[...] = project_turned(w_k[...], normed)
+    turned = project_turned(w_v[...], normed)
+    val[...] = turned
+    out[...] = finish(merged, turned.T, gain_m, w_o, w_in, w_back).reshape(out.shape)
+
+
+def run_first(lay, stacked, gains, weights):
+    _, rows, width = stacked.shape
+    dtype = stacked.dtype
+    heads = jax.ShapeDtypeStruct((width, lay.bricks * rows), dtype)
+    return pl.pallas_call(
+        functools.partial(first_kernel, lay),
+        out_shape=(heads, heads, jax.ShapeDtypeStruct((lay.bricks, rows, width), dtype)),
+        in_specs=[spec(VMEM)] * (1 + len(gains) + len(weights)),
+        out_specs=(spec(VMEM),) * 3,
+        compiler_params=pltpu.CompilerParams(vmem_limit_bytes=12 << 20),
+        cost_estimate=pl.CostEstimate(flops=10**9, bytes_accessed=0, transcendentals=0),
+        name="first",
+    )(stacked, *gains, *pinned(weights, VMEM))
+
+
 def block_kernel(lay, *refs):
     frames, bricks, cap, spaces = lay.frames, lay.bricks, lay.cap, lay.spaces
-    table, stacked = refs[:2]
-    pieces = refs[2 : 2 + spaces]
-    gain_a, gain_m, w_q, w_k, w_v, w_o, w_in, w_back = refs[2 + spaces : 10 + spaces]
-    outs = refs[10 + spaces : 10 + spaces + frames]
-    slots, merged, hidden, result = refs[10 + spaces + frames :]
+    table, stacked, key_0, val_0, out_0 = refs[:5]
+    refs = refs[5:]
+    pieces = refs[:spaces]
+    gain_a, gain_m, w_q, w_k, w_v, w_o, w_in, w_back = refs[spaces : 8 + spaces]
+    outs = refs[8 + spaces : 8 + spaces + frames]
+    slots, merged, hidden, result = refs[8 + spaces + frames :]
     rows, width = stacked.shape[1:]
     per_frame = bricks * rows
     for j in range(spaces):
         slots[j * cap : (j + 1) * cap] = pieces[j][...]
-    for b in range(bricks):
-        merged[b * rows : (b + 1) * rows] = stacked[b]
     for f in range(1, frames):
         for b in range(bricks):
             q = (f - 1) * bricks + b
             weight = table[lay.weight + q].astype(jnp.float32) * 0.25
             piece = slots[table[lay.take + q]].astype(jnp.float32)
-            at = f * per_frame + b * rows
-            merged[at : at + rows] = (
+            merged[q * rows : (q + 1) * rows] = (
                 stacked[f * bricks + b].astype(jnp.float32) + weight * piece
             ).astype(jnp.bfloat16)
     normed = normalise(merged[...], gain_a[...])
@@ -194,14 +229,18 @@
     keys = project_turned(w_k[...], normed)
     vals = project_turned(w_v[...], normed)
 
-    def heads_of(x, f):
-        part = x[:, f * per_frame : (f + 1) * per_frame].astype(jnp.float32)
-        return part.reshape(width // HD, HD, per_frame)
-
-    for f in range(frames):
-        query = heads_of(queries, f) * (1.0 / HD**0.5)
+    def heads_of(x):
+        return x.astype(jnp.float32).reshape(width // HD, HD, per_frame)
+
+    def later(x, f):
+        return heads_of(x[:, (f - 1) * per_frame : f * per_frame])
+
+    key_heads = [heads_of(key_0[...])] + [later(keys, f) for f in range(1, frames)]
+    val_heads = [heads_of(val_0[...])] + [later(vals, f) for f in range(1, frames)]
+    for f in range(1, frames):
+        query = later(queries, f) * (1.0 / HD**0.5)
         scores = [
-            jnp.sum(query * heads_of(keys, g), axis=1, keepdims=True) for g in range(f + 1)
+            jnp.sum(query * key_heads[g], axis=1, keepdims=True) for g in range(f + 1)
         ]
         top = functools.reduce(jnp.maximum, scores)
         exps = [jnp.exp(s - top) for s in scores]
@@ -209,43 +248,44 @@
         context = None
         for g in range(f + 1):
             prob = (exps[g] / total).astype(jnp.bfloat16).astype(jnp.float32)
-            term = prob * heads_of(vals, g)
+            term = prob * val_heads[g]
             context = term if context is None else context + term
         context = context.reshape(width, per_frame).astype(jnp.bfloat16)
-        hidden[f * per_frame : (f + 1) * per_frame] = context.T
-    mid = (merged[...].astype(jnp.float32) + matmul(hidden[...], w_o[...])).astype(jnp.bfloat16)
-    normed2 = normalise(mid, gain_m[...])
-    total = mid.astype(jnp.float32)
-    depth = w_in.shape[1]
-    step = min(BLOCK_FF, depth)
-    for at in range(0, depth, step):
-        part = gelu(matmul(normed2, w_in[:, at : at + step])).astype(jnp.bfloat16)
-        total = total + matmul(part, w_back[at : at + step])
-    result[...] = total.astype(jnp.bfloat16).reshape(result.shape)
+        hidden[(f - 1) * per_frame : f * per_frame] = context.T
+    done = finish(merged[...], hidden[...], gain_m, w_o, w_in, w_back)
+    result[:bricks] = out_0[...]
+    result[bricks:] = done.reshape(-1, rows, width)
     mine = table[1]
     for k in range(frames):
         outs[k][...] = result[pl.ds((mine ^ k) * bricks, bricks)]
 
 
-def run_block(lay, table, stacked, pieces, gains, weights):
+def run_block(lay, table, stacked, early, pieces, gains, weights):
     total, rows, width = stacked.shape
     dtype = stacked.dtype
     return pl.pallas_call(
         functools.partial(block_kernel, lay),
         out_shape=(jax.ShapeDtypeStruct((lay.bricks, rows, width), dtype),) * lay.frames,
         in_specs=[spec(SMEM)]
-        + [spec(VMEM)] * (1 + lay.spaces + len(gains) + len(weights)),
+        + [spec(VMEM)] * (4 + lay.spaces + len(gains) + len(weights)),
         out_specs=(spec(VMEM),) * lay.frames,
         scratch_shapes=[
             VMEM((lay.spaces * lay.cap, rows, width), dtype),
-            VMEM((total * rows, width), dtype),
-            VMEM((total * rows, width), dtype),
+            VMEM((lay.requests * rows, width), dtype),
+            VMEM((lay.requests * rows, width), dtype),
             VMEM((total, rows, width), dtype),
         ],
         compiler_params=pltpu.CompilerParams(vmem_limit_bytes=20 << 20),
-        cost_estimate=pl.CostEstimate(flops=10000000000, bytes_accessed=0, transcendentals=0),
+        cost_estimate=pl.CostEstimate(flops=10**10, bytes_accessed=0, transcendentals=0),
         name="block",
-    )(*pinned([table], SMEM), stacked, *pieces, *gains, *pinned(weights, VMEM))
+    )(
+        *pinned([table], SMEM),
+        stacked,
+        *early,
+        *pieces,
+        *gains,
+        *pinned(weights, VMEM),
+    )
 
 
 def assemble_kernel(steps, chunk, *refs):
@@ -321,11 +361,13 @@
     stacked, *slots = select(lay, table, arrived[0])
     for c in range(chunks):
         pieces = across(slots, "space", range(spaces))
-        done = run_block(lay, table, stacked, pieces, gains, weights)
+        if c > 0:
+            pieces, back[0][1] = lax.optimization_barrier((pieces, back[0][1]))
+        early = run_first(lay, stacked, gains, weights)
+        done = run_block(lay, table, stacked, early, pieces, gains, weights)
         if c + 1 < chunks:
-            arrived[c + 1], done = lax.optimization_barrier((arrived[c + 1], done))
+            arrived[c + 1][0], done = lax.optimization_barrier((arrived[c + 1][0], done))
             stacked, *slots = select(lay, table, arrived[c + 1])
-            slots, done = lax.optimization_barrier((slots, done))
         back.append(across([done[k] for k in steps], "frame", steps))
     base = []
     for c in range(chunks):

time: 60.8 us -> 60.4 us (level)
  waiting for transfers between devices: 20.3 us -> 18.6 us
  Pallas kernels: 14.8 us -> 16.3 us
    pallas_call x0 -> x2, Pallas kernels: none -> 3.35 us  [run_first(): pl.pallas_call(functools.partial(first_kernel, lay), out_shape=(heads, he...]
    pallas_call x2, Pallas kernels: 9.24 us -> 7.44 us  [run_block(): pl.pallas_call(functools.partial(block_kernel, lay), out_shape=(jax.Shape...]
    ppermute x18, waiting for transfers between devices: 20.3 us -> 18.6 us  [exchange(): return lax.ppermute(values, axis, [(i, i ^ step) for i in range(size)])]
  transfers between devices with their start and end apart: 18 -> 18, of which waited for: 8 -> 7; matrix products, arithmetic and copies ran while one was open for 2% -> 2% of each run, Pallas kernels for 23% -> 26%
where the time goes in v5:
time: 60.4 us; the launch traced here: 60.2 us
  starting transfers between devices  22.8 us (38%)
  waiting for transfers between devices  18.6 us (31%)
  Pallas kernels  16.3 us (27%)
  local copies, waits for them, and re-layouts  2.3 us (4%)
    ppermute x18, starting transfers between devices, exchange(): return lax.ppermute(values, axis, [(i, i ^ step) for i in range(size)])  22.8 us
    ppermute x18, waiting for transfers between devices, exchange(): return lax.ppermute(values, axis, [(i, i ^ step) for i in range(size)])  18.6 us
    pallas_call x2, Pallas kernels, run_block(): pl.pallas_call(functools.partial(block_kernel, lay), out_shape=(jax.Shape...  7.44 us
    pallas_call x1, Pallas kernels, prepare(): pl.pallas_call(functools.partial(prepare_kernel, lay), out_shape=(pltpu.S...  3.74 us
    pallas_call x2, Pallas kernels, run_first(): pl.pallas_call(functools.partial(first_kernel, lay), out_shape=(heads, he...  3.35 us
    squeeze x2, local copies, waits for them, and re-layouts, local(): lax.dynamic_index_in_dim(cut, c * frames + (mine ^ k), 1, keepdims=False)  2.29 us
    pallas_call x2, Pallas kernels, assemble(): pl.pallas_call(functools.partial(assemble_kernel, steps, chunk), out_shap...  1.64 us
  transfers between devices with their start and end apart: 18, of which 7 were waited for; matrix products, arithmetic and copies ran while one was open for 2% of the time, Pallas kernels for 26%

profile of v5, /device:TPU:0, one launch (start us, length us, event | category | flops | bytes accessed | tf_op | source)
XLA Modules:
  0.0 60.2 jit_solution(16031986692178909768)
XLA Ops:
  0.0 0.0 copy-start.3
  0.0 0.0 copy-start.2
  0.0 1.2 %dynamic-slice_bitcast_fusion.4 = (bf16[8,16,512]{2,1,0:T(8,128)(2,1)S(1)}, bf16[8,16,512]{2,1,0:T(8,128)(2,1)S(1)}, bf16[8,16,512]{2,1,0:T(8,128)(2,1)S(1)}, bf16[8,16,512]{2,1,0:T(8,128)(2,1)S(1)}) fusion(bf16[8,8,16,512]{3,2,1,0:T(8,128)(2,1)} %bitcast.38, s32[]{:T(128)S(6)} %select_n.28, s32[]{:T(128)S(6)} %select_n.27, s32[]{:T(128)S(6)} %select_n.26, ...), kind=kLoop, calls=%fused_computation.4 | loop fusion | bytes 1048592 | tf_op jit(solution)/shard_map/jit(dynamic_index_in_dim)/squeeze | solution.py:345
  1.2 4.1 %collective-permute-start = (bf16[8,16,512]{2,1,0:T(8,128)(2,1)S(1)}, bf16[8,16,512]{2,1,0:T(8,128)(2,1)S(1)}, u32[]{:S(2)}, u32[]{:S(2)}) collective-permute-start(bf16[8,16,512]{2,1,0:T(8,128)(2,1)S(1)} %get-tuple-element.79), channel_id=1, source_target_pairs={{0,2},{1,3},{2,0},{3,1},{4,6},{5,7},{6,4},{7,5},{8,10},{9,11},{10,... | collective-permute-start | bytes 393224 | tf_op jit(solution)/shard_map/ppermute | solution.py:25
  5.3 1.3 %collective-permute-start.2 = (bf16[8,16,512]{2,1,0:T(8,128)(2,1)S(1)}, bf16[8,16,512]{2,1,0:T(8,128)(2,1)S(1)}, u32[]{:S(2)}, u32[]{:S(2)}) collective-permute-start(bf16[8,16,512]{2,1,0:T(8,128)(2,1)S(1)} %get-tuple-element.83), channel_id=1, source_target_pairs={{0,3},{1,2},{2,1},{3,0},{4,7},{5,6},{6,5},{7,4},{8,11},{9,10},{10,... | collective-permute-start | bytes 393224 | tf_op jit(solution)/shard_map/ppermute | solution.py:25
  6.6 0.2 collective-permute-start.3
  6.8 1.1 %dynamic-slice_bitcast_fusion = (bf16[8,16,512]{2,1,0:T(8,128)(2,1)S(1)}, bf16[8,16,512]{2,1,0:T(8,128)(2,1)S(1)}, bf16[8,16,512]{2,1,0:T(8,128)(2,1)S(1)}, bf16[8,16,512]{2,1,0:T(8,128)(2,1)S(1)}) fusion(s32[]{:T(128)S(6)} %select_n.32, s32[]{:T(128)S(6)} %select_n.31, s32[]{:T(128)S(6)} %select_n.30, s32[]{:T(128)S(6)} %select_n.29, ...), kind=kLoop, calls=%fused_computation | loop fusion | bytes 1048592 | tf_op jit(solution)/shard_map/jit(dynamic_index_in_dim)/squeeze | solution.py:345
  8.0 0.1 pad_add_fusion.ids
  8.1 0.0 copy-done.3
  8.1 0.0 copy-done.2
  8.1 0.0 copy-start
  8.1 0.0 copy-start.1
  8.1 3.7 %prepare.1 = (s32[79]{0:T(128)S(4)}, bf16[512,512]{1,0:T(8,128)(2,1)S(1)}, bf16[512,512]{1,0:T(8,128)(2,1)S(1)}, bf16[512,512]{1,0:T(8,128)(2,1)S(1)}, bf16[512,...) custom-call(s32[2]{0:T(128)S(1)} %pad_add_fusion.ids, s32[3,32]{1,0:T(4,128)S(1)} %copy-done.2, ...), custom_call_target="tpu_custom_call" | custom-call | tf_op jit(solution)/shard_map/prepare/pallas_call | solution.py:98
  11.8 3.4 %collective-permute-done.refs_1_ = bf16[8,16,512]{2,1,0:T(8,128)(2,1)S(1)} collective-permute-done((bf16[8,16,512]{2,1,0:T(8,128)(2,1)S(1)}, bf16[8,16,512]{2,1,0:T(8,128)(2,1)S(1)}, u32[]{:S(2)}, u32[]{:S(2)}) %collective-permute-start) | collective-permute-done | bytes 131104 | tf_op jit(solution)/shard_map/ppermute | solution.py:25
  15.3 0.0 collective-permute-done.2.refs_2_
  15.3 0.5 collective-permute-done.3.refs_3_
  15.8 0.1 select.2
  15.8 0.1 collective-permute-start.4
  15.9 1.6 %collective-permute-start.5 = (bf16[7,16,512]{2,1,0:T(8,128)(2,1)S(1)}, bf16[7,16,512]{2,1,0:T(8,128)(2,1)S(1)}, u32[]{:S(2)}, u32[]{:S(2)}) collective-permute-start(bf16[7,16,512]{2,1,0:T(8,128)(2,1)S(1)} %get-tuple-element.98), channel_id=1, source_target_pairs={{0,8},{4,12},{8,0},{12,4},{1,9},{5,13},{9,1},{13,5},{2,10},{6,14},... | collective-permute-start | bytes 344072 | tf_op jit(solution)/shard_map/ppermute | solution.py:25
  17.6 0.2 collective-permute-start.6
  17.8 4.1 %collective-permute-start.1 = (bf16[8,16,512]{2,1,0:T(8,128)(2,1)S(1)}, bf16[8,16,512]{2,1,0:T(8,128)(2,1)S(1)}, u32[]{:S(2)}, u32[]{:S(2)}) collective-permute-start(bf16[8,16,512]{2,1,0:T(8,128)(2,1)S(1)} %get-tuple-element.81), channel_id=1, source_target_pairs={{0,2},{1,3},{2,0},{3,1},{4,6},{5,7},{6,4},{7,5},{8,10},{9,11},{10,... | collective-permute-start | bytes 393224 | tf_op jit(solution)/shard_map/ppermute | solution.py:25
  21.9 0.4 collective-permute-start.7
  22.3 0.0 copy-done
  22.3 0.0 copy-done.1
  22.3 1.7 %first.2 = (bf16[512,128]{1,0:T(8,128)(2,1)S(1)}, bf16[512,128]{1,0:T(8,128)(2,1)S(1)}, bf16[8,16,512]{2,1,0:T(8,128)(2,1)S(1)}) custom-call(bf16[32,16,512]{2,1,0:T(8,128)(2,1)S(1)} %get-tuple-element.86.refs_0_.refs_1_, f32[1,512]{1,0:T(1,128)S(1)} %bitcast.30, f32[1,512]{1,0:T(1,128)S(1)} %bitcast.34, ...), custom_call_target="tpu_custom_call" | custom-call | flops 1000000000 | tf_op jit(solution)/shard_map/first/pallas_call | solution.py:196
  24.0 0.0 collective-permute-done.4.refs_6_
  24.0 0.2 collective-permute-start.8
  24.2 0.0 collective-permute-done.5.refs_7_
  24.2 0.0 collective-permute-done.6.refs_8_
  24.2 3.7 %block.2 = (bf16[8,16,512]{2,1,0:T(8,128)(2,1)S(1)}, bf16[8,16,512]{2,1,0:T(8,128)(2,1)S(1)}, bf16[8,16,512]{2,1,0:T(8,128)(2,1)S(1)}, bf16[8,16,512]{2,1,0:T(8,128)(2,1)S(1)}) custom-call(s32[79]{0:T(128)S(4)} %get-tuple-element.80.refs_0_, bf16[32,16,512]{2,1,0:T(8,128)(2,1)S(1)} %get-tuple-element.86.refs_0_.refs_1_, ...), custom_call_target="tpu_custom_call" | custom-call | flops 10000000000 | tf_op jit(solution)/shard_map/block/pallas_call | solution.py:266
  28.0 3.8 %collective-permute-done.1.refs_1_ = bf16[8,16,512]{2,1,0:T(8,128)(2,1)S(1)} collective-permute-done((bf16[8,16,512]{2,1,0:T(8,128)(2,1)S(1)}, bf16[8,16,512]{2,1,0:T(8,128)(2,1)S(1)}, u32[]{:S(2)}, u32[]{:S(2)}) %collective-permute-start.1) | collective-permute-done | bytes 131104 | tf_op jit(solution)/shard_map/ppermute | solution.py:25
  31.8 2.4 %collective-permute-start.12 = (bf16[8,16,512]{2,1,0:T(8,128)(2,1)S(1)}, bf16[8,16,512]{2,1,0:T(8,128)(2,1)S(1)}, u32[]{:S(2)}, u32[]{:S(2)}) collective-permute-start(bf16[8,16,512]{2,1,0:T(8,128)(2,1)S(1)} %get-tuple-element.116), channel_id=1, source_target_pairs={{0,3},{1,2},{2,1},{3,0},{4,7},{5,6},{6,5},{7,4},{8,11},{9,10},{10,... | collective-permute-start | bytes 393224 | tf_op jit(solution)/shard_map/ppermute | solution.py:25
  34.2 0.0 collective-permute-done.7.refs_2_
  34.2 0.1 collective-permute-done.8.refs_3_
  34.3 0.1 select.3
  34.4 0.1 collective-permute-start.9
  34.5 1.6 %collective-permute-start.10 = (bf16[7,16,512]{2,1,0:T(8,128)(2,1)S(1)}, bf16[7,16,512]{2,1,0:T(8,128)(2,1)S(1)}, u32[]{:S(2)}, u32[]{:S(2)}) collective-permute-start(bf16[7,16,512]{2,1,0:T(8,128)(2,1)S(1)} %get-tuple-element.114), channel_id=1, source_target_pairs={{0,8},{4,12},{8,0},{12,4},{1,9},{5,13},{9,1},{13,5},{2,10},{6,14},... | collective-permute-start | bytes 344072 | tf_op jit(solution)/shard_map/ppermute | solution.py:25
  36.1 0.3 collective-permute-start.11
  36.3 1.8 %collective-permute-start.16 = (bf16[8,16,512]{2,1,0:T(8,128)(2,1)S(1)}, bf16[8,16,512]{2,1,0:T(8,128)(2,1)S(1)}, u32[]{:S(2)}, u32[]{:S(2)}) collective-permute-start(bf16[8,16,512]{2,1,0:T(8,128)(2,1)S(1)} %get-tuple-element.125), channel_id=1, source_target_pairs={{0,2},{1,3},{2,0},{3,1},{4,6},{5,7},{6,4},{7,5},{8,10},{9,11},{10,... | collective-permute-start | bytes 393224 | tf_op jit(solution)/shard_map/ppermute | solution.py:25
  38.1 1.7 %first.3 = (bf16[512,128]{1,0:T(8,128)(2,1)S(1)}, bf16[512,128]{1,0:T(8,128)(2,1)S(1)}, bf16[8,16,512]{2,1,0:T(8,128)(2,1)S(1)}) custom-call(bf16[32,16,512]{2,1,0:T(8,128)(2,1)S(1)} %get-tuple-element.108.refs_0_.refs_1_, f32[1,512]{1,0:T(1,128)S(1)} %bitcast.32, f32[1,512]{1,0:T(1,128)S(1)} %bitcast.36, ...), custom_call_target="tpu_custom_call" | custom-call | flops 1000000000 | tf_op jit(solution)/shard_map/first/pallas_call | solution.py:196
  39.8 0.0 collective-permute-done.9.refs_6_
  39.8 0.8 %collective-permute-start.17 = (bf16[8,16,512]{2,1,0:T(8,128)(2,1)S(1)}, bf16[8,16,512]{2,1,0:T(8,128)(2,1)S(1)}, u32[]{:S(2)}, u32[]{:S(2)}) collective-permute-start(bf16[8,16,512]{2,1,0:T(8,128)(2,1)S(1)} %get-tuple-element.127), channel_id=1, source_target_pairs={{0,1},{1,0},{2,3},{3,2},{4,5},{5,4},{6,7},{7,6},{8,9},{9,8},{10,11... | collective-permute-start | bytes 393224 | tf_op jit(solution)/shard_map/ppermute | solution.py:25
  40.6 0.0 collective-permute-done.10.refs_7_
  40.6 1.4 %collective-permute-done.11.refs_8_ = bf16[7,16,512]{2,1,0:T(8,128)(2,1)S(1)} collective-permute-done((bf16[7,16,512]{2,1,0:T(8,128)(2,1)S(1)}, bf16[7,16,512]{2,1,0:T(8,128)(2,1)S(1)}, u32[]{:S(2)}, u32[]{:S(2)}) %collective-permute-start.11) | collective-permute-done | bytes 114720 | tf_op jit(solution)/shard_map/ppermute | solution.py:25
  42.1 0.0 collective-permute-done.12.refs_2_
  42.1 3.7 %block.3 = (bf16[8,16,512]{2,1,0:T(8,128)(2,1)S(1)}, bf16[8,16,512]{2,1,0:T(8,128)(2,1)S(1)}, bf16[8,16,512]{2,1,0:T(8,128)(2,1)S(1)}, bf16[8,16,512]{2,1,0:T(8,128)(2,1)S(1)}) custom-call(s32[79]{0:T(128)S(4)} %get-tuple-element.80.refs_0_, bf16[32,16,512]{2,1,0:T(8,128)(2,1)S(1)} %get-tuple-element.108.refs_0_.refs_1_, ...), custom_call_target="tpu_custom_call" | custom-call | flops 10000000000 | tf_op jit(solution)/shard_map/block/pallas_call | solution.py:266
  45.8 1.8 %collective-permute-start.13 = (bf16[8,16,512]{2,1,0:T(8,128)(2,1)S(1)}, bf16[8,16,512]{2,1,0:T(8,128)(2,1)S(1)}, u32[]{:S(2)}, u32[]{:S(2)}) collective-permute-start(bf16[8,16,512]{2,1,0:T(8,128)(2,1)S(1)} %get-tuple-element.121), channel_id=1, source_target_pairs={{0,2},{1,3},{2,0},{3,1},{4,6},{5,7},{6,4},{7,5},{8,10},{9,11},{10,... | collective-permute-start | bytes 393224 | tf_op jit(solution)/shard_map/ppermute | solution.py:25
  47.6 1.5 %collective-permute-start.14 = (bf16[8,16,512]{2,1,0:T(8,128)(2,1)S(1)}, bf16[8,16,512]{2,1,0:T(8,128)(2,1)S(1)}, u32[]{:S(2)}, u32[]{:S(2)}) collective-permute-start(bf16[8,16,512]{2,1,0:T(8,128)(2,1)S(1)} %get-tuple-element.122), channel_id=1, source_target_pairs={{0,3},{1,2},{2,1},{3,0},{4,7},{5,6},{6,5},{7,4},{8,11},{9,10},{10,... | collective-permute-start | bytes 393224 | tf_op jit(solution)/shard_map/ppermute | solution.py:25
  49.1 0.3 collective-permute-start.15
  49.3 0.0 collective-permute-done.16.refs_1_
  49.3 0.0 collective-permute-done.17.refs_3_
  49.3 0.8 %assemble.2.refs_5_ = bf16[8,8,16,512]{3,2,1,0:T(8,128)(2,1)} custom-call(s32[79]{0:T(128)S(4)} %get-tuple-element.80.refs_0_, bf16[8,16,512]{2,1,0:T(8,128)(2,1)S(1)} %collective-permute-done.16.refs_1_, bf16[8,16,512]{2,1,0:T(8,128)(2,1)S(1)} %collective-permute-done.12.refs_2_, bf16[8,16,512]{2,1,0:T(8,128)(2,1)S(1)} %collective-permute-done.17.refs_3_, ...), custom_call_target="tpu_custom_call" | custom-call | tf_op jit(solution)/shard_map/assemble/pallas_call | solution.py:310
  50.2 8.6 %collective-permute-done.13.refs_1_ = bf16[8,16,512]{2,1,0:T(8,128)(2,1)S(1)} collective-permute-done((bf16[8,16,512]{2,1,0:T(8,128)(2,1)S(1)}, bf16[8,16,512]{2,1,0:T(8,128)(2,1)S(1)}, u32[]{:S(2)}, u32[]{:S(2)}) %collective-permute-start.13) | collective-permute-done | bytes 131104 | tf_op jit(solution)/shard_map/ppermute | solution.py:25
  58.7 0.0 collective-permute-done.14.refs_2_
  58.7 0.7 %collective-permute-done.15.refs_3_ = bf16[8,16,512]{2,1,0:T(8,128)(2,1)S(1)} collective-permute-done((bf16[8,16,512]{2,1,0:T(8,128)(2,1)S(1)}, bf16[8,16,512]{2,1,0:T(8,128)(2,1)S(1)}, u32[]{:S(2)}, u32[]{:S(2)}) %collective-permute-start.15) | collective-permute-done | bytes 131104 | tf_op jit(solution)/shard_map/ppermute | solution.py:25
  59.4 0.8 %assemble.3 = bf16[8,8,16,512]{3,2,1,0:T(8,128)(2,1)} custom-call(s32[79]{0:T(128)S(4)} %get-tuple-element.80.refs_0_, bf16[8,16,512]{2,1,0:T(8,128)(2,1)S(1)} %collective-permute-done.13.refs_1_, bf16[8,16,512]{2,1,0:T(8,128)(2,1)S(1)} %collective-permute-done.14.refs_2_, ...), custom_call_target="tpu_custom_call", output_to_operand_aliasing={{}: (5, {})} | custom-call | tf_op jit(solution)/shard_map/assemble/pallas_call | solution.py:310
Async XLA Ops:
  0.0 8.1 %copy-start.3 = (s32[3,32]{1,0:T(4,128)S(1)}, s32[3,32]{1,0:T(4,128)}, u32[]{:S(2)}) copy-start(s32[3,32]{1,0:T(4,128)} %merge_num) | copy-start | bytes 1156
  0.0 8.1 %copy-start.2 = (s32[3,32]{1,0:T(4,128)S(1)}, s32[3,32]{1,0:T(4,128)}, u32[]{:S(2)}) copy-start(s32[3,32]{1,0:T(4,128)} %src) | copy-start | bytes 1156
  1.2 14.1 %collective-permute-start = (bf16[8,16,512]{2,1,0:T(8,128)(2,1)S(1)}, bf16[8,16,512]{2,1,0:T(8,128)(2,1)S(1)}, u32[]{:S(2)}, u32[]{:S(2)}) collective-permute-start(bf16[8,16,512]{2,1,0:T(8,128)(2,1)S(1)} %get-tuple-element.79), channel_id=1, source_target_pairs={{0,2},{1,3},{2,0},{3,1},{4,6},{5,7},{6,4},{7,5},{8,10},{9,11},{10,... | collective-permute-start | bytes 393224 | tf_op jit(solution)/shard_map/ppermute | solution.py:25
  5.3 10.0 %collective-permute-start.2 = (bf16[8,16,512]{2,1,0:T(8,128)(2,1)S(1)}, bf16[8,16,512]{2,1,0:T(8,128)(2,1)S(1)}, u32[]{:S(2)}, u32[]{:S(2)}) collective-permute-start(bf16[8,16,512]{2,1,0:T(8,128)(2,1)S(1)} %get-tuple-element.83), channel_id=1, source_target_pairs={{0,3},{1,2},{2,1},{3,0},{4,7},{5,6},{6,5},{7,4},{8,11},{9,10},{10,... | collective-permute-start | bytes 393224 | tf_op jit(solution)/shard_map/ppermute | solution.py:25
  6.6 9.2 %collective-permute-start.3 = (bf16[8,16,512]{2,1,0:T(8,128)(2,1)S(1)}, bf16[8,16,512]{2,1,0:T(8,128)(2,1)S(1)}, u32[]{:S(2)}, u32[]{:S(2)}) collective-permute-start(bf16[8,16,512]{2,1,0:T(8,128)(2,1)S(1)} %get-tuple-element.84), channel_id=1, source_target_pairs={{0,1},{1,0},{2,3},{3,2},{4,5},{5,4},{6,7},{7,6},{8,9},{9,8},{10,11... | collective-permute-start | bytes 393224 | tf_op jit(solution)/shard_map/ppermute | solution.py:25
  8.1 14.3 %copy-start = (f32[512]{0:T(512)S(1)}, f32[512]{0:T(512)}, u32[]{:S(2)}) copy-start(f32[512]{0:T(512)} %param.14) | copy-start | bytes 6148
  8.1 14.3 %copy-start.1 = (f32[512]{0:T(512)S(1)}, f32[512]{0:T(512)}, u32[]{:S(2)}) copy-start(f32[512]{0:T(512)} %param.19) | copy-start | bytes 6148
  15.8 8.2 %collective-permute-start.4 = (bf16[7,16,512]{2,1,0:T(8,128)(2,1)S(1)}, bf16[7,16,512]{2,1,0:T(8,128)(2,1)S(1)}, u32[]{:S(2)}, u32[]{:S(2)}) collective-permute-start(bf16[7,16,512]{2,1,0:T(8,128)(2,1)S(1)} %get-tuple-element.97), channel_id=1, source_target_pairs={{0,4},{4,0},{8,12},{12,8},{1,5},{5,1},{9,13},{13,9},{2,6},{6,2},{1... | collective-permute-start | bytes 344072 | tf_op jit(solution)/shard_map/ppermute | solution.py:25
  15.9 8.3 %collective-permute-start.5 = (bf16[7,16,512]{2,1,0:T(8,128)(2,1)S(1)}, bf16[7,16,512]{2,1,0:T(8,128)(2,1)S(1)}, u32[]{:S(2)}, u32[]{:S(2)}) collective-permute-start(bf16[7,16,512]{2,1,0:T(8,128)(2,1)S(1)} %get-tuple-element.98), channel_id=1, source_target_pairs={{0,8},{4,12},{8,0},{12,4},{1,9},{5,13},{9,1},{13,5},{2,10},{6,14},... | collective-permute-start | bytes 344072 | tf_op jit(solution)/shard_map/ppermute | solution.py:25
  17.6 6.7 %collective-permute-start.6 = (bf16[7,16,512]{2,1,0:T(8,128)(2,1)S(1)}, bf16[7,16,512]{2,1,0:T(8,128)(2,1)S(1)}, u32[]{:S(2)}, u32[]{:S(2)}) collective-permute-start(bf16[7,16,512]{2,1,0:T(8,128)(2,1)S(1)} %get-tuple-element.99), channel_id=1, source_target_pairs={{0,12},{4,8},{8,4},{12,0},{1,13},{5,9},{9,5},{13,1},{2,14},{6,10},... | collective-permute-start | bytes 344072 | tf_op jit(solution)/shard_map/ppermute | solution.py:25
  17.8 14.0 %collective-permute-start.1 = (bf16[8,16,512]{2,1,0:T(8,128)(2,1)S(1)}, bf16[8,16,512]{2,1,0:T(8,128)(2,1)S(1)}, u32[]{:S(2)}, u32[]{:S(2)}) collective-permute-start(bf16[8,16,512]{2,1,0:T(8,128)(2,1)S(1)} %get-tuple-element.81), channel_id=1, source_target_pairs={{0,2},{1,3},{2,0},{3,1},{4,6},{5,7},{6,4},{7,5},{8,10},{9,11},{10,... | collective-permute-start | bytes 393224 | tf_op jit(solution)/shard_map/ppermute | solution.py:25
  21.9 12.3 %collective-permute-start.7 = (bf16[8,16,512]{2,1,0:T(8,128)(2,1)S(1)}, bf16[8,16,512]{2,1,0:T(8,128)(2,1)S(1)}, u32[]{:S(2)}, u32[]{:S(2)}) collective-permute-start(bf16[8,16,512]{2,1,0:T(8,128)(2,1)S(1)} %get-tuple-element.105), channel_id=1, source_target_pairs={{0,3},{1,2},{2,1},{3,0},{4,7},{5,6},{6,5},{7,4},{8,11},{9,10},{10,... | collective-permute-start | bytes 393224 | tf_op jit(solution)/shard_map/ppermute | solution.py:25
  24.0 10.3 %collective-permute-start.8 = (bf16[8,16,512]{2,1,0:T(8,128)(2,1)S(1)}, bf16[8,16,512]{2,1,0:T(8,128)(2,1)S(1)}, u32[]{:S(2)}, u32[]{:S(2)}) collective-permute-start(bf16[8,16,512]{2,1,0:T(8,128)(2,1)S(1)} %get-tuple-element.106), channel_id=1, source_target_pairs={{0,1},{1,0},{2,3},{3,2},{4,5},{5,4},{6,7},{7,6},{8,9},{9,8},{10,11... | collective-permute-start | bytes 393224 | tf_op jit(solution)/shard_map/ppermute | solution.py:25
  31.8 10.2 %collective-permute-start.12 = (bf16[8,16,512]{2,1,0:T(8,128)(2,1)S(1)}, bf16[8,16,512]{2,1,0:T(8,128)(2,1)S(1)}, u32[]{:S(2)}, u32[]{:S(2)}) collective-permute-start(bf16[8,16,512]{2,1,0:T(8,128)(2,1)S(1)} %get-tuple-element.116), channel_id=1, source_target_pairs={{0,3},{1,2},{2,1},{3,0},{4,7},{5,6},{6,5},{7,4},{8,11},{9,10},{10,... | collective-permute-start | bytes 393224 | tf_op jit(solution)/shard_map/ppermute | solution.py:25
  34.4 5.4 %collective-permute-start.9 = (bf16[7,16,512]{2,1,0:T(8,128)(2,1)S(1)}, bf16[7,16,512]{2,1,0:T(8,128)(2,1)S(1)}, u32[]{:S(2)}, u32[]{:S(2)}) collective-permute-start(bf16[7,16,512]{2,1,0:T(8,128)(2,1)S(1)} %get-tuple-element.113), channel_id=1, source_target_pairs={{0,4},{4,0},{8,12},{12,8},{1,5},{5,1},{9,13},{13,9},{2,6},{6,2},{1... | collective-permute-start | bytes 344072 | tf_op jit(solution)/shard_map/ppermute | solution.py:25
  34.5 6.1 %collective-permute-start.10 = (bf16[7,16,512]{2,1,0:T(8,128)(2,1)S(1)}, bf16[7,16,512]{2,1,0:T(8,128)(2,1)S(1)}, u32[]{:S(2)}, u32[]{:S(2)}) collective-permute-start(bf16[7,16,512]{2,1,0:T(8,128)(2,1)S(1)} %get-tuple-element.114), channel_id=1, source_target_pairs={{0,8},{4,12},{8,0},{12,4},{1,9},{5,13},{9,1},{13,5},{2,10},{6,14},... | collective-permute-start | bytes 344072 | tf_op jit(solution)/shard_map/ppermute | solution.py:25
  36.1 6.0 %collective-permute-start.11 = (bf16[7,16,512]{2,1,0:T(8,128)(2,1)S(1)}, bf16[7,16,512]{2,1,0:T(8,128)(2,1)S(1)}, u32[]{:S(2)}, u32[]{:S(2)}) collective-permute-start(bf16[7,16,512]{2,1,0:T(8,128)(2,1)S(1)} %get-tuple-element.115), channel_id=1, source_target_pairs={{0,12},{4,8},{8,4},{12,0},{1,13},{5,9},{9,5},{13,1},{2,14},{6,10},... | collective-permute-start | bytes 344072 | tf_op jit(solution)/shard_map/ppermute | solution.py:25
  36.3 13.0 %collective-permute-start.16 = (bf16[8,16,512]{2,1,0:T(8,128)(2,1)S(1)}, bf16[8,16,512]{2,1,0:T(8,128)(2,1)S(1)}, u32[]{:S(2)}, u32[]{:S(2)}) collective-permute-start(bf16[8,16,512]{2,1,0:T(8,128)(2,1)S(1)} %get-tuple-element.125), channel_id=1, source_target_pairs={{0,2},{1,3},{2,0},{3,1},{4,6},{5,7},{6,4},{7,5},{8,10},{9,11},{10,... | collective-permute-start | bytes 393224 | tf_op jit(solution)/shard_map/ppermute | solution.py:25
  39.8 9.5 %collective-permute-start.17 = (bf16[8,16,512]{2,1,0:T(8,128)(2,1)S(1)}, bf16[8,16,512]{2,1,0:T(8,128)(2,1)S(1)}, u32[]{:S(2)}, u32[]{:S(2)}) collective-permute-start(bf16[8,16,512]{2,1,0:T(8,128)(2,1)S(1)} %get-tuple-element.127), channel_id=1, source_target_pairs={{0,1},{1,0},{2,3},{3,2},{4,5},{5,4},{6,7},{7,6},{8,9},{9,8},{10,11... | collective-permute-start | bytes 393224 | tf_op jit(solution)/shard_map/ppermute | solution.py:25
  45.8 12.9 %collective-permute-start.13 = (bf16[8,16,512]{2,1,0:T(8,128)(2,1)S(1)}, bf16[8,16,512]{2,1,0:T(8,128)(2,1)S(1)}, u32[]{:S(2)}, u32[]{:S(2)}) collective-permute-start(bf16[8,16,512]{2,1,0:T(8,128)(2,1)S(1)} %get-tuple-element.121), channel_id=1, source_target_pairs={{0,2},{1,3},{2,0},{3,1},{4,6},{5,7},{6,4},{7,5},{8,10},{9,11},{10,... | collective-permute-start | bytes 393224 | tf_op jit(solution)/shard_map/ppermute | solution.py:25
  47.6 11.1 %collective-permute-start.14 = (bf16[8,16,512]{2,1,0:T(8,128)(2,1)S(1)}, bf16[8,16,512]{2,1,0:T(8,128)(2,1)S(1)}, u32[]{:S(2)}, u32[]{:S(2)}) collective-permute-start(bf16[8,16,512]{2,1,0:T(8,128)(2,1)S(1)} %get-tuple-element.122), channel_id=1, source_target_pairs={{0,3},{1,2},{2,1},{3,0},{4,7},{5,6},{6,5},{7,4},{8,11},{9,10},{10,... | collective-permute-start | bytes 393224 | tf_op jit(solution)/shard_map/ppermute | solution.py:25
  49.1 10.3 %collective-permute-start.15 = (bf16[8,16,512]{2,1,0:T(8,128)(2,1)S(1)}, bf16[8,16,512]{2,1,0:T(8,128)(2,1)S(1)}, u32[]{:S(2)}, u32[]{:S(2)}) collective-permute-start(bf16[8,16,512]{2,1,0:T(8,128)(2,1)S(1)} %get-tuple-element.123), channel_id=1, source_target_pairs={{0,1},{1,0},{2,3},{3,2},{4,5},{5,4},{6,7},{7,6},{8,9},{9,8},{10,11... | collective-permute-start | bytes 393224 | tf_op jit(solution)/shard_map/ppermute | solution.py:25

commit v6 on v5

--- a/solution.py
+++ b/solution.py
@@ -363,6 +363,8 @@
         pieces = across(slots, "space", range(spaces))
         if c > 0:
             pieces, back[0][1] = lax.optimization_barrier((pieces, back[0][1]))
+        if c + 1 < chunks:
+            pieces, arrived[c + 1][-2] = lax.optimization_barrier((pieces, arrived[c + 1][-2]))
         early = run_first(lay, stacked, gains, weights)
         done = run_block(lay, table, stacked, early, pieces, gains, weights)
         if c + 1 < chunks:

time: 60.4 us -> 60.2 us (level)
    ppermute x18, starting transfers between devices: 22.8 us -> 22.2 us  [exchange(): return lax.ppermute(values, axis, [(i, i ^ step) for i in range(size)])]
where the time goes in v6:
time: 60.2 us; the launch traced here: 60 us
  starting transfers between devices  22.2 us (37%)
  waiting for transfers between devices  19 us (32%)
  Pallas kernels  16.3 us (27%)
  local copies, waits for them, and re-layouts  2.3 us (4%)
    ppermute x18, starting transfers between devices, exchange(): return lax.ppermute(values, axis, [(i, i ^ step) for i in range(size)])  22.2 us
    ppermute x18, waiting for transfers between devices, exchange(): return lax.ppermute(values, axis, [(i, i ^ step) for i in range(size)])  19 us
    pallas_call x2, Pallas kernels, run_block(): pl.pallas_call(functools.partial(block_kernel, lay), out_shape=(jax.Shape...  7.45 us
    pallas_call x1, Pallas kernels, prepare(): pl.pallas_call(functools.partial(prepare_kernel, lay), out_shape=(pltpu.S...  3.74 us
    pallas_call x2, Pallas kernels, run_first(): pl.pallas_call(functools.partial(first_kernel, lay), out_shape=(heads, he...  3.36 us
    squeeze x2, local copies, waits for them, and re-layouts, local(): lax.dynamic_index_in_dim(cut, c * frames + (mine ^ k), 1, keepdims=False)  2.29 us
    pallas_call x2, Pallas kernels, assemble(): pl.pallas_call(functools.partial(assemble_kernel, steps, chunk), out_shap...  1.64 us
  transfers between devices with their start and end apart: 18, of which 7 were waited for; matrix products, arithmetic and copies ran while one was open for 2% of the time, Pallas kernels for 26%

profile of v6, /device:TPU:0, one launch (start us, length us, event | category | flops | bytes accessed | tf_op | source)
XLA Modules:
  0.0 60.0 jit_solution(6595725381572872682)
XLA Ops:
  0.0 0.0 copy-start.3
  0.0 0.0 copy-start.2
  0.0 1.2 %dynamic-slice_bitcast_fusion.4 = (bf16[8,16,512]{2,1,0:T(8,128)(2,1)S(1)}, bf16[8,16,512]{2,1,0:T(8,128)(2,1)S(1)}, bf16[8,16,512]{2,1,0:T(8,128)(2,1)S(1)}, bf16[8,16,512]{2,1,0:T(8,128)(2,1)S(1)}) fusion(bf16[8,8,16,512]{3,2,1,0:T(8,128)(2,1)} %bitcast.38, s32[]{:T(128)S(6)} %select_n.28, s32[]{:T(128)S(6)} %select_n.27, s32[]{:T(128)S(6)} %select_n.26, ...), kind=kLoop, calls=%fused_computation.4 | loop fusion | bytes 1048592 | tf_op jit(solution)/shard_map/jit(dynamic_index_in_dim)/squeeze | solution.py:345
  1.2 4.1 %collective-permute-start = (bf16[8,16,512]{2,1,0:T(8,128)(2,1)S(1)}, bf16[8,16,512]{2,1,0:T(8,128)(2,1)S(1)}, u32[]{:S(2)}, u32[]{:S(2)}) collective-permute-start(bf16[8,16,512]{2,1,0:T(8,128)(2,1)S(1)} %get-tuple-element.84), channel_id=1, source_target_pairs={{0,2},{1,3},{2,0},{3,1},{4,6},{5,7},{6,4},{7,5},{8,10},{9,11},{10,... | collective-permute-start | bytes 393224 | tf_op jit(solution)/shard_map/ppermute | solution.py:25
  5.3 1.3 %collective-permute-start.2 = (bf16[8,16,512]{2,1,0:T(8,128)(2,1)S(1)}, bf16[8,16,512]{2,1,0:T(8,128)(2,1)S(1)}, u32[]{:S(2)}, u32[]{:S(2)}) collective-permute-start(bf16[8,16,512]{2,1,0:T(8,128)(2,1)S(1)} %get-tuple-element.88), channel_id=1, source_target_pairs={{0,3},{1,2},{2,1},{3,0},{4,7},{5,6},{6,5},{7,4},{8,11},{9,10},{10,... | collective-permute-start | bytes 393224 | tf_op jit(solution)/shard_map/ppermute | solution.py:25
  6.6 0.2 collective-permute-start.3
  6.8 1.1 %dynamic-slice_bitcast_fusion = (bf16[8,16,512]{2,1,0:T(8,128)(2,1)S(1)}, bf16[8,16,512]{2,1,0:T(8,128)(2,1)S(1)}, bf16[8,16,512]{2,1,0:T(8,128)(2,1)S(1)}, bf16[8,16,512]{2,1,0:T(8,128)(2,1)S(1)}) fusion(s32[]{:T(128)S(6)} %select_n.32, s32[]{:T(128)S(6)} %select_n.31, s32[]{:T(128)S(6)} %select_n.30, s32[]{:T(128)S(6)} %select_n.29, ...), kind=kLoop, calls=%fused_computation | loop fusion | bytes 1048592 | tf_op jit(solution)/shard_map/jit(dynamic_index_in_dim)/squeeze | solution.py:345
  8.0 0.1 pad_add_fusion.ids
  8.1 0.0 copy-done.3
  8.1 0.0 copy-done.2
  8.1 0.0 copy-start
  8.1 0.0 copy-start.1
  8.1 3.7 %prepare.1 = (s32[79]{0:T(128)S(4)}, bf16[512,512]{1,0:T(8,128)(2,1)S(1)}, bf16[512,512]{1,0:T(8,128)(2,1)S(1)}, bf16[512,512]{1,0:T(8,128)(2,1)S(1)}, bf16[512,...) custom-call(s32[2]{0:T(128)S(1)} %pad_add_fusion.ids, s32[3,32]{1,0:T(4,128)S(1)} %copy-done.2, ...), custom_call_target="tpu_custom_call" | custom-call | tf_op jit(solution)/shard_map/prepare/pallas_call | solution.py:98
  11.8 3.4 %collective-permute-done.refs_1_ = bf16[8,16,512]{2,1,0:T(8,128)(2,1)S(1)} collective-permute-done((bf16[8,16,512]{2,1,0:T(8,128)(2,1)S(1)}, bf16[8,16,512]{2,1,0:T(8,128)(2,1)S(1)}, u32[]{:S(2)}, u32[]{:S(2)}) %collective-permute-start) | collective-permute-done | bytes 131104 | tf_op jit(solution)/shard_map/ppermute | solution.py:25
  15.3 0.0 collective-permute-start.7
  15.3 0.0 collective-permute-done.2.refs_2_
  15.3 0.5 collective-permute-done.3.refs_3_
  15.8 0.1 select.2
  15.8 0.1 collective-permute-start.4
  15.9 1.6 %collective-permute-start.5 = (bf16[7,16,512]{2,1,0:T(8,128)(2,1)S(1)}, bf16[7,16,512]{2,1,0:T(8,128)(2,1)S(1)}, u32[]{:S(2)}, u32[]{:S(2)}) collective-permute-start(bf16[7,16,512]{2,1,0:T(8,128)(2,1)S(1)} %get-tuple-element.103), channel_id=1, source_target_pairs={{0,8},{4,12},{8,0},{12,4},{1,9},{5,13},{9,1},{13,5},{2,10},{6,14},... | collective-permute-start | bytes 344072 | tf_op jit(solution)/shard_map/ppermute | solution.py:25
  17.6 0.2 collective-permute-start.6
  17.8 4.1 %collective-permute-start.1 = (bf16[8,16,512]{2,1,0:T(8,128)(2,1)S(1)}, bf16[8,16,512]{2,1,0:T(8,128)(2,1)S(1)}, u32[]{:S(2)}, u32[]{:S(2)}) collective-permute-start(bf16[8,16,512]{2,1,0:T(8,128)(2,1)S(1)} %get-tuple-element.86), channel_id=1, source_target_pairs={{0,2},{1,3},{2,0},{3,1},{4,6},{5,7},{6,4},{7,5},{8,10},{9,11},{10,... | collective-permute-start | bytes 393224 | tf_op jit(solution)/shard_map/ppermute | solution.py:25
  21.9 0.0 copy-done
  21.9 0.0 copy-done.1
  21.9 1.7 %first.2 = (bf16[512,128]{1,0:T(8,128)(2,1)S(1)}, bf16[512,128]{1,0:T(8,128)(2,1)S(1)}, bf16[8,16,512]{2,1,0:T(8,128)(2,1)S(1)}) custom-call(bf16[32,16,512]{2,1,0:T(8,128)(2,1)S(1)} %get-tuple-element.91.refs_0_.refs_1_, f32[1,512]{1,0:T(1,128)S(1)} %bitcast.30, f32[1,512]{1,0:T(1,128)S(1)} %bitcast.34, ...), custom_call_target="tpu_custom_call" | custom-call | flops 1000000000 | tf_op jit(solution)/shard_map/first/pallas_call | solution.py:196
  23.6 0.0 collective-permute-done.4.refs_6_
  23.6 0.5 collective-permute-start.8
  24.1 0.0 collective-permute-done.5.refs_7_
  24.1 0.0 collective-permute-done.6.refs_8_
  24.1 0.0 collective-permute-done.7.refs_3_
  24.1 3.7 %block.2 = (bf16[8,16,512]{2,1,0:T(8,128)(2,1)S(1)}, bf16[8,16,512]{2,1,0:T(8,128)(2,1)S(1)}, bf16[8,16,512]{2,1,0:T(8,128)(2,1)S(1)}, bf16[8,16,512]{2,1,0:T(8,128)(2,1)S(1)}) custom-call(s32[79]{0:T(128)S(4)} %get-tuple-element.85.refs_0_, bf16[32,16,512]{2,1,0:T(8,128)(2,1)S(1)} %get-tuple-element.91.refs_0_.refs_1_, ...), custom_call_target="tpu_custom_call" | custom-call | flops 10000000000 | tf_op jit(solution)/shard_map/block/pallas_call | solution.py:266
  27.9 3.9 %collective-permute-done.1.refs_1_ = bf16[8,16,512]{2,1,0:T(8,128)(2,1)S(1)} collective-permute-done((bf16[8,16,512]{2,1,0:T(8,128)(2,1)S(1)}, bf16[8,16,512]{2,1,0:T(8,128)(2,1)S(1)}, u32[]{:S(2)}, u32[]{:S(2)}) %collective-permute-start.1) | collective-permute-done | bytes 131104 | tf_op jit(solution)/shard_map/ppermute | solution.py:25
  31.8 2.4 %collective-permute-start.12 = (bf16[8,16,512]{2,1,0:T(8,128)(2,1)S(1)}, bf16[8,16,512]{2,1,0:T(8,128)(2,1)S(1)}, u32[]{:S(2)}, u32[]{:S(2)}) collective-permute-start(bf16[8,16,512]{2,1,0:T(8,128)(2,1)S(1)} %get-tuple-element.126), channel_id=1, source_target_pairs={{0,3},{1,2},{2,1},{3,0},{4,7},{5,6},{6,5},{7,4},{8,11},{9,10},{10,... | collective-permute-start | bytes 393224 | tf_op jit(solution)/shard_map/ppermute | solution.py:25
  34.1 0.0 collective-permute-done.8.refs_2_
  34.1 0.1 select.3
  34.2 0.1 collective-permute-start.9
  34.3 1.6 %collective-permute-start.10 = (bf16[7,16,512]{2,1,0:T(8,128)(2,1)S(1)}, bf16[7,16,512]{2,1,0:T(8,128)(2,1)S(1)}, u32[]{:S(2)}, u32[]{:S(2)}) collective-permute-start(bf16[7,16,512]{2,1,0:T(8,128)(2,1)S(1)} %get-tuple-element.124), channel_id=1, source_target_pairs={{0,8},{4,12},{8,0},{12,4},{1,9},{5,13},{9,1},{13,5},{2,10},{6,14},... | collective-permute-start | bytes 344072 | tf_op jit(solution)/shard_map/ppermute | solution.py:25
  35.9 0.3 collective-permute-start.11
  36.2 1.9 %collective-permute-start.16 = (bf16[8,16,512]{2,1,0:T(8,128)(2,1)S(1)}, bf16[8,16,512]{2,1,0:T(8,128)(2,1)S(1)}, u32[]{:S(2)}, u32[]{:S(2)}) collective-permute-start(bf16[8,16,512]{2,1,0:T(8,128)(2,1)S(1)} %get-tuple-element.135), channel_id=1, source_target_pairs={{0,2},{1,3},{2,0},{3,1},{4,6},{5,7},{6,4},{7,5},{8,10},{9,11},{10,... | collective-permute-start | bytes 393224 | tf_op jit(solution)/shard_map/ppermute | solution.py:25
  38.1 1.7 %first.3 = (bf16[512,128]{1,0:T(8,128)(2,1)S(1)}, bf16[512,128]{1,0:T(8,128)(2,1)S(1)}, bf16[8,16,512]{2,1,0:T(8,128)(2,1)S(1)}) custom-call(bf16[32,16,512]{2,1,0:T(8,128)(2,1)S(1)} %get-tuple-element.118.refs_0_.refs_1_, f32[1,512]{1,0:T(1,128)S(1)} %bitcast.32, f32[1,512]{1,0:T(1,128)S(1)} %bitcast.36, ...), custom_call_target="tpu_custom_call" | custom-call | flops 1000000000 | tf_op jit(solution)/shard_map/first/pallas_call | solution.py:196
  39.8 0.0 collective-permute-done.9.refs_6_
  39.8 0.2 collective-permute-start.17
  40.0 0.4 collective-permute-done.10.refs_7_
  40.3 1.6 %collective-permute-done.11.refs_8_ = bf16[7,16,512]{2,1,0:T(8,128)(2,1)S(1)} collective-permute-done((bf16[7,16,512]{2,1,0:T(8,128)(2,1)S(1)}, bf16[7,16,512]{2,1,0:T(8,128)(2,1)S(1)}, u32[]{:S(2)}, u32[]{:S(2)}) %collective-permute-start.11) | collective-permute-done | bytes 114720 | tf_op jit(solution)/shard_map/ppermute | solution.py:25
  41.9 0.0 collective-permute-done.12.refs_2_
  41.9 3.7 %block.3 = (bf16[8,16,512]{2,1,0:T(8,128)(2,1)S(1)}, bf16[8,16,512]{2,1,0:T(8,128)(2,1)S(1)}, bf16[8,16,512]{2,1,0:T(8,128)(2,1)S(1)}, bf16[8,16,512]{2,1,0:T(8,128)(2,1)S(1)}) custom-call(s32[79]{0:T(128)S(4)} %get-tuple-element.85.refs_0_, bf16[32,16,512]{2,1,0:T(8,128)(2,1)S(1)} %get-tuple-element.118.refs_0_.refs_1_, ...), custom_call_target="tpu_custom_call" | custom-call | flops 10000000000 | tf_op jit(solution)/shard_map/block/pallas_call | solution.py:266
  45.6 2.0 %collective-permute-start.13 = (bf16[8,16,512]{2,1,0:T(8,128)(2,1)S(1)}, bf16[8,16,512]{2,1,0:T(8,128)(2,1)S(1)}, u32[]{:S(2)}, u32[]{:S(2)}) collective-permute-start(bf16[8,16,512]{2,1,0:T(8,128)(2,1)S(1)} %get-tuple-element.131), channel_id=1, source_target_pairs={{0,2},{1,3},{2,0},{3,1},{4,6},{5,7},{6,4},{7,5},{8,10},{9,11},{10,... | collective-permute-start | bytes 393224 | tf_op jit(solution)/shard_map/ppermute | solution.py:25
  47.6 1.5 %collective-permute-start.14 = (bf16[8,16,512]{2,1,0:T(8,128)(2,1)S(1)}, bf16[8,16,512]{2,1,0:T(8,128)(2,1)S(1)}, u32[]{:S(2)}, u32[]{:S(2)}) collective-permute-start(bf16[8,16,512]{2,1,0:T(8,128)(2,1)S(1)} %get-tuple-element.132), channel_id=1, source_target_pairs={{0,3},{1,2},{2,1},{3,0},{4,7},{5,6},{6,5},{7,4},{8,11},{9,10},{10,... | collective-permute-start | bytes 393224 | tf_op jit(solution)/shard_map/ppermute | solution.py:25
  49.0 0.1 collective-permute-start.15
  49.2 0.0 collective-permute-done.16.refs_1_
  49.2 0.0 collective-permute-done.17.refs_3_
  49.2 0.8 %assemble.2.refs_5_ = bf16[8,8,16,512]{3,2,1,0:T(8,128)(2,1)} custom-call(s32[79]{0:T(128)S(4)} %get-tuple-element.85.refs_0_, bf16[8,16,512]{2,1,0:T(8,128)(2,1)S(1)} %collective-permute-done.16.refs_1_, bf16[8,16,512]{2,1,0:T(8,128)(2,1)S(1)} %collective-permute-done.12.refs_2_, bf16[8,16,512]{2,1,0:T(8,128)(2,1)S(1)} %collective-permute-done.17.refs_3_, ...), custom_call_target="tpu_custom_call" | custom-call | tf_op jit(solution)/shard_map/assemble/pallas_call | solution.py:310
  50.0 8.6 %collective-permute-done.13.refs_1_ = bf16[8,16,512]{2,1,0:T(8,128)(2,1)S(1)} collective-permute-done((bf16[8,16,512]{2,1,0:T(8,128)(2,1)S(1)}, bf16[8,16,512]{2,1,0:T(8,128)(2,1)S(1)}, u32[]{:S(2)}, u32[]{:S(2)}) %collective-permute-start.13) | collective-permute-done | bytes 131104 | tf_op jit(solution)/shard_map/ppermute | solution.py:25
  58.5 0.0 collective-permute-done.14.refs_2_
  58.6 0.7 %collective-permute-done.15.refs_3_ = bf16[8,16,512]{2,1,0:T(8,128)(2,1)S(1)} collective-permute-done((bf16[8,16,512]{2,1,0:T(8,128)(2,1)S(1)}, bf16[8,16,512]{2,1,0:T(8,128)(2,1)S(1)}, u32[]{:S(2)}, u32[]{:S(2)}) %collective-permute-start.15) | collective-permute-done | bytes 131104 | tf_op jit(solution)/shard_map/ppermute | solution.py:25
  59.2 0.8 %assemble.3 = bf16[8,8,16,512]{3,2,1,0:T(8,128)(2,1)} custom-call(s32[79]{0:T(128)S(4)} %get-tuple-element.85.refs_0_, bf16[8,16,512]{2,1,0:T(8,128)(2,1)S(1)} %collective-permute-done.13.refs_1_, bf16[8,16,512]{2,1,0:T(8,128)(2,1)S(1)} %collective-permute-done.14.refs_2_, ...), custom_call_target="tpu_custom_call", output_to_operand_aliasing={{}: (5, {})} | custom-call | tf_op jit(solution)/shard_map/assemble/pallas_call | solution.py:310
Async XLA Ops:
  0.0 8.1 %copy-start.3 = (s32[3,32]{1,0:T(4,128)S(1)}, s32[3,32]{1,0:T(4,128)}, u32[]{:S(2)}) copy-start(s32[3,32]{1,0:T(4,128)} %merge_num) | copy-start | bytes 1156
  0.0 8.1 %copy-start.2 = (s32[3,32]{1,0:T(4,128)S(1)}, s32[3,32]{1,0:T(4,128)}, u32[]{:S(2)}) copy-start(s32[3,32]{1,0:T(4,128)} %src) | copy-start | bytes 1156
  1.2 14.1 %collective-permute-start = (bf16[8,16,512]{2,1,0:T(8,128)(2,1)S(1)}, bf16[8,16,512]{2,1,0:T(8,128)(2,1)S(1)}, u32[]{:S(2)}, u32[]{:S(2)}) collective-permute-start(bf16[8,16,512]{2,1,0:T(8,128)(2,1)S(1)} %get-tuple-element.84), channel_id=1, source_target_pairs={{0,2},{1,3},{2,0},{3,1},{4,6},{5,7},{6,4},{7,5},{8,10},{9,11},{10,... | collective-permute-start | bytes 393224 | tf_op jit(solution)/shard_map/ppermute | solution.py:25
  5.3 10.0 %collective-permute-start.2 = (bf16[8,16,512]{2,1,0:T(8,128)(2,1)S(1)}, bf16[8,16,512]{2,1,0:T(8,128)(2,1)S(1)}, u32[]{:S(2)}, u32[]{:S(2)}) collective-permute-start(bf16[8,16,512]{2,1,0:T(8,128)(2,1)S(1)} %get-tuple-element.88), channel_id=1, source_target_pairs={{0,3},{1,2},{2,1},{3,0},{4,7},{5,6},{6,5},{7,4},{8,11},{9,10},{10,... | collective-permute-start | bytes 393224 | tf_op jit(solution)/shard_map/ppermute | solution.py:25
  6.6 9.2 %collective-permute-start.3 = (bf16[8,16,512]{2,1,0:T(8,128)(2,1)S(1)}, bf16[8,16,512]{2,1,0:T(8,128)(2,1)S(1)}, u32[]{:S(2)}, u32[]{:S(2)}) collective-permute-start(bf16[8,16,512]{2,1,0:T(8,128)(2,1)S(1)} %get-tuple-element.89), channel_id=1, source_target_pairs={{0,1},{1,0},{2,3},{3,2},{4,5},{5,4},{6,7},{7,6},{8,9},{9,8},{10,11... | collective-permute-start | bytes 393224 | tf_op jit(solution)/shard_map/ppermute | solution.py:25
  8.1 13.8 %copy-start = (f32[512]{0:T(512)S(1)}, f32[512]{0:T(512)}, u32[]{:S(2)}) copy-start(f32[512]{0:T(512)} %param.14) | copy-start | bytes 6148
  8.1 13.8 %copy-start.1 = (f32[512]{0:T(512)S(1)}, f32[512]{0:T(512)}, u32[]{:S(2)}) copy-start(f32[512]{0:T(512)} %param.19) | copy-start | bytes 6148
  15.3 8.9 %collective-permute-start.7 = (bf16[8,16,512]{2,1,0:T(8,128)(2,1)S(1)}, bf16[8,16,512]{2,1,0:T(8,128)(2,1)S(1)}, u32[]{:S(2)}, u32[]{:S(2)}) collective-permute-start(bf16[8,16,512]{2,1,0:T(8,128)(2,1)S(1)} %get-tuple-element.105), channel_id=1, source_target_pairs={{0,1},{1,0},{2,3},{3,2},{4,5},{5,4},{6,7},{7,6},{8,9},{9,8},{10,11... | collective-permute-start | bytes 393224 | tf_op jit(solution)/shard_map/ppermute | solution.py:25
  15.8 7.8 %collective-permute-start.4 = (bf16[7,16,512]{2,1,0:T(8,128)(2,1)S(1)}, bf16[7,16,512]{2,1,0:T(8,128)(2,1)S(1)}, u32[]{:S(2)}, u32[]{:S(2)}) collective-permute-start(bf16[7,16,512]{2,1,0:T(8,128)(2,1)S(1)} %get-tuple-element.102), channel_id=1, source_target_pairs={{0,4},{4,0},{8,12},{12,8},{1,5},{5,1},{9,13},{13,9},{2,6},{6,2},{1... | collective-permute-start | bytes 344072 | tf_op jit(solution)/shard_map/ppermute | solution.py:25
  15.9 8.2 %collective-permute-start.5 = (bf16[7,16,512]{2,1,0:T(8,128)(2,1)S(1)}, bf16[7,16,512]{2,1,0:T(8,128)(2,1)S(1)}, u32[]{:S(2)}, u32[]{:S(2)}) collective-permute-start(bf16[7,16,512]{2,1,0:T(8,128)(2,1)S(1)} %get-tuple-element.103), channel_id=1, source_target_pairs={{0,8},{4,12},{8,0},{12,4},{1,9},{5,13},{9,1},{13,5},{2,10},{6,14},... | collective-permute-start | bytes 344072 | tf_op jit(solution)/shard_map/ppermute | solution.py:25
  17.6 6.5 %collective-permute-start.6 = (bf16[7,16,512]{2,1,0:T(8,128)(2,1)S(1)}, bf16[7,16,512]{2,1,0:T(8,128)(2,1)S(1)}, u32[]{:S(2)}, u32[]{:S(2)}) collective-permute-start(bf16[7,16,512]{2,1,0:T(8,128)(2,1)S(1)} %get-tuple-element.104), channel_id=1, source_target_pairs={{0,12},{4,8},{8,4},{12,0},{1,13},{5,9},{9,5},{13,1},{2,14},{6,10},... | collective-permute-start | bytes 344072 | tf_op jit(solution)/shard_map/ppermute | solution.py:25
  17.8 14.0 %collective-permute-start.1 = (bf16[8,16,512]{2,1,0:T(8,128)(2,1)S(1)}, bf16[8,16,512]{2,1,0:T(8,128)(2,1)S(1)}, u32[]{:S(2)}, u32[]{:S(2)}) collective-permute-start(bf16[8,16,512]{2,1,0:T(8,128)(2,1)S(1)} %get-tuple-element.86), channel_id=1, source_target_pairs={{0,2},{1,3},{2,0},{3,1},{4,6},{5,7},{6,4},{7,5},{8,10},{9,11},{10,... | collective-permute-start | bytes 393224 | tf_op jit(solution)/shard_map/ppermute | solution.py:25
  23.6 10.5 %collective-permute-start.8 = (bf16[8,16,512]{2,1,0:T(8,128)(2,1)S(1)}, bf16[8,16,512]{2,1,0:T(8,128)(2,1)S(1)}, u32[]{:S(2)}, u32[]{:S(2)}) collective-permute-start(bf16[8,16,512]{2,1,0:T(8,128)(2,1)S(1)} %get-tuple-element.115), channel_id=1, source_target_pairs={{0,3},{1,2},{2,1},{3,0},{4,7},{5,6},{6,5},{7,4},{8,11},{9,10},{10,... | collective-permute-start | bytes 393224 | tf_op jit(solution)/shard_map/ppermute | solution.py:25
  31.8 10.1 %collective-permute-start.12 = (bf16[8,16,512]{2,1,0:T(8,128)(2,1)S(1)}, bf16[8,16,512]{2,1,0:T(8,128)(2,1)S(1)}, u32[]{:S(2)}, u32[]{:S(2)}) collective-permute-start(bf16[8,16,512]{2,1,0:T(8,128)(2,1)S(1)} %get-tuple-element.126), channel_id=1, source_target_pairs={{0,3},{1,2},{2,1},{3,0},{4,7},{5,6},{6,5},{7,4},{8,11},{9,10},{10,... | collective-permute-start | bytes 393224 | tf_op jit(solution)/shard_map/ppermute | solution.py:25
  34.2 5.5 %collective-permute-start.9 = (bf16[7,16,512]{2,1,0:T(8,128)(2,1)S(1)}, bf16[7,16,512]{2,1,0:T(8,128)(2,1)S(1)}, u32[]{:S(2)}, u32[]{:S(2)}) collective-permute-start(bf16[7,16,512]{2,1,0:T(8,128)(2,1)S(1)} %get-tuple-element.123), channel_id=1, source_target_pairs={{0,4},{4,0},{8,12},{12,8},{1,5},{5,1},{9,13},{13,9},{2,6},{6,2},{1... | collective-permute-start | bytes 344072 | tf_op jit(solution)/shard_map/ppermute | solution.py:25
  34.3 6.0 %collective-permute-start.10 = (bf16[7,16,512]{2,1,0:T(8,128)(2,1)S(1)}, bf16[7,16,512]{2,1,0:T(8,128)(2,1)S(1)}, u32[]{:S(2)}, u32[]{:S(2)}) collective-permute-start(bf16[7,16,512]{2,1,0:T(8,128)(2,1)S(1)} %get-tuple-element.124), channel_id=1, source_target_pairs={{0,8},{4,12},{8,0},{12,4},{1,9},{5,13},{9,1},{13,5},{2,10},{6,14},... | collective-permute-start | bytes 344072 | tf_op jit(solution)/shard_map/ppermute | solution.py:25
  35.9 6.0 %collective-permute-start.11 = (bf16[7,16,512]{2,1,0:T(8,128)(2,1)S(1)}, bf16[7,16,512]{2,1,0:T(8,128)(2,1)S(1)}, u32[]{:S(2)}, u32[]{:S(2)}) collective-permute-start(bf16[7,16,512]{2,1,0:T(8,128)(2,1)S(1)} %get-tuple-element.125), channel_id=1, source_target_pairs={{0,12},{4,8},{8,4},{12,0},{1,13},{5,9},{9,5},{13,1},{2,14},{6,10},... | collective-permute-start | bytes 344072 | tf_op jit(solution)/shard_map/ppermute | solution.py:25
  36.2 13.0 %collective-permute-start.16 = (bf16[8,16,512]{2,1,0:T(8,128)(2,1)S(1)}, bf16[8,16,512]{2,1,0:T(8,128)(2,1)S(1)}, u32[]{:S(2)}, u32[]{:S(2)}) collective-permute-start(bf16[8,16,512]{2,1,0:T(8,128)(2,1)S(1)} %get-tuple-element.135), channel_id=1, source_target_pairs={{0,2},{1,3},{2,0},{3,1},{4,6},{5,7},{6,4},{7,5},{8,10},{9,11},{10,... | collective-permute-start | bytes 393224 | tf_op jit(solution)/shard_map/ppermute | solution.py:25
  39.8 9.4 %collective-permute-start.17 = (bf16[8,16,512]{2,1,0:T(8,128)(2,1)S(1)}, bf16[8,16,512]{2,1,0:T(8,128)(2,1)S(1)}, u32[]{:S(2)}, u32[]{:S(2)}) collective-permute-start(bf16[8,16,512]{2,1,0:T(8,128)(2,1)S(1)} %get-tuple-element.137), channel_id=1, source_target_pairs={{0,1},{1,0},{2,3},{3,2},{4,5},{5,4},{6,7},{7,6},{8,9},{9,8},{10,11... | collective-permute-start | bytes 393224 | tf_op jit(solution)/shard_map/ppermute | solution.py:25
  45.6 13.0 %collective-permute-start.13 = (bf16[8,16,512]{2,1,0:T(8,128)(2,1)S(1)}, bf16[8,16,512]{2,1,0:T(8,128)(2,1)S(1)}, u32[]{:S(2)}, u32[]{:S(2)}) collective-permute-start(bf16[8,16,512]{2,1,0:T(8,128)(2,1)S(1)} %get-tuple-element.131), channel_id=1, source_target_pairs={{0,2},{1,3},{2,0},{3,1},{4,6},{5,7},{6,4},{7,5},{8,10},{9,11},{10,... | collective-permute-start | bytes 393224 | tf_op jit(solution)/shard_map/ppermute | solution.py:25
  47.6 11.0 %collective-permute-start.14 = (bf16[8,16,512]{2,1,0:T(8,128)(2,1)S(1)}, bf16[8,16,512]{2,1,0:T(8,128)(2,1)S(1)}, u32[]{:S(2)}, u32[]{:S(2)}) collective-permute-start(bf16[8,16,512]{2,1,0:T(8,128)(2,1)S(1)} %get-tuple-element.132), channel_id=1, source_target_pairs={{0,3},{1,2},{2,1},{3,0},{4,7},{5,6},{6,5},{7,4},{8,11},{9,10},{10,... | collective-permute-start | bytes 393224 | tf_op jit(solution)/shard_map/ppermute | solution.py:25
  49.0 10.2 %collective-permute-start.15 = (bf16[8,16,512]{2,1,0:T(8,128)(2,1)S(1)}, bf16[8,16,512]{2,1,0:T(8,128)(2,1)S(1)}, u32[]{:S(2)}, u32[]{:S(2)}) collective-permute-start(bf16[8,16,512]{2,1,0:T(8,128)(2,1)S(1)} %get-tuple-element.133), channel_id=1, source_target_pairs={{0,1},{1,0},{2,3},{3,2},{4,5},{5,4},{6,7},{7,6},{8,9},{9,8},{10,11... | collective-permute-start | bytes 393224 | tf_op jit(solution)/shard_map/ppermute | solution.py:25

commit v7 on v6

--- a/solution.py
+++ b/solution.py
@@ -353,8 +353,8 @@
     arrived = [across(parts[0], "frame", steps)]
     table, *weights = prepare(lay, ids, src_brick, merge_num, weights)
     for c in range(1, chunks):
-        parts[c], table, arrived[-1][0] = lax.optimization_barrier(
-            (parts[c], table, arrived[-1][0])
+        parts[c], table, arrived[-1][1] = lax.optimization_barrier(
+            (parts[c], table, arrived[-1][1])
         )
         arrived.append(across(parts[c], "frame", steps))
     back = []

time: 60.2 us -> 59.3 us (0.985)
  waiting for transfers between devices: 19 us -> 15.1 us
  starting transfers between devices: 22.2 us -> 25.2 us
    ppermute x18, waiting for transfers between devices: 19 us -> 15.1 us  [exchange(): return lax.ppermute(values, axis, [(i, i ^ step) for i in range(size)])]
    ppermute x18, starting transfers between devices: 22.2 us -> 25.2 us  [exchange(): return lax.ppermute(values, axis, [(i, i ^ step) for i in range(size)])]
  transfers between devices with their start and end apart: 18 -> 18, of which waited for: 7 -> 6; matrix products, arithmetic and copies ran while one was open for 2% -> 2% of each run, Pallas kernels for 26% -> 26%
where the time goes in v7:
time: 59.3 us; the launch traced here: 59.2 us
  starting transfers between devices  25.2 us (42%)
  Pallas kernels  16.3 us (27%)
  waiting for transfers between devices  15.1 us (25%)
  local copies, waits for them, and re-layouts  2.3 us (4%)
    ppermute x18, starting transfers between devices, exchange(): return lax.ppermute(values, axis, [(i, i ^ step) for i in range(size)])  25.2 us
    ppermute x18, waiting for transfers between devices, exchange(): return lax.ppermute(values, axis, [(i, i ^ step) for i in range(size)])  15.1 us
    pallas_call x2, Pallas kernels, run_block(): pl.pallas_call(functools.partial(block_kernel, lay), out_shape=(jax.Shape...  7.44 us
    pallas_call x1, Pallas kernels, prepare(): pl.pallas_call(functools.partial(prepare_kernel, lay), out_shape=(pltpu.S...  3.74 us
    pallas_call x2, Pallas kernels, run_first(): pl.pallas_call(functools.partial(first_kernel, lay), out_shape=(heads, he...  3.35 us
    squeeze x2, local copies, waits for them, and re-layouts, local(): lax.dynamic_index_in_dim(cut, c * frames + (mine ^ k), 1, keepdims=False)  2.29 us
    pallas_call x2, Pallas kernels, assemble(): pl.pallas_call(functools.partial(assemble_kernel, steps, chunk), out_shap...  1.64 us
  transfers between devices with their start and end apart: 18, of which 6 were waited for; matrix products, arithmetic and copies ran while one was open for 2% of the time, Pallas kernels for 26%

profile of v7, /device:TPU:0, one launch (start us, length us, event | category | flops | bytes accessed | tf_op | source)
XLA Modules:
  0.0 59.2 jit_solution(16293336038133191605)
XLA Ops:
  0.0 0.0 copy-start.3
  0.0 0.0 copy-start.2
  0.0 1.2 %dynamic-slice_bitcast_fusion.4 = (bf16[8,16,512]{2,1,0:T(8,128)(2,1)S(1)}, bf16[8,16,512]{2,1,0:T(8,128)(2,1)S(1)}, bf16[8,16,512]{2,1,0:T(8,128)(2,1)S(1)}, bf16[8,16,512]{2,1,0:T(8,128)(2,1)S(1)}) fusion(bf16[8,8,16,512]{3,2,1,0:T(8,128)(2,1)} %bitcast.38, s32[]{:T(128)S(6)} %select_n.28, s32[]{:T(128)S(6)} %select_n.27, s32[]{:T(128)S(6)} %select_n.26, ...), kind=kLoop, calls=%fused_computation.4 | loop fusion | bytes 1048592 | tf_op jit(solution)/shard_map/jit(dynamic_index_in_dim)/squeeze | solution.py:345
  1.2 5.1 %collective-permute-start = (bf16[8,16,512]{2,1,0:T(8,128)(2,1)S(1)}, bf16[8,16,512]{2,1,0:T(8,128)(2,1)S(1)}, u32[]{:S(2)}, u32[]{:S(2)}) collective-permute-start(bf16[8,16,512]{2,1,0:T(8,128)(2,1)S(1)} %get-tuple-element.84), channel_id=1, source_target_pairs={{0,3},{1,2},{2,1},{3,0},{4,7},{5,6},{6,5},{7,4},{8,11},{9,10},{10,... | collective-permute-start | bytes 393224 | tf_op jit(solution)/shard_map/ppermute | solution.py:25
  6.3 0.0 collective-permute-start.2
  6.3 0.6 %collective-permute-start.3 = (bf16[8,16,512]{2,1,0:T(8,128)(2,1)S(1)}, bf16[8,16,512]{2,1,0:T(8,128)(2,1)S(1)}, u32[]{:S(2)}, u32[]{:S(2)}) collective-permute-start(bf16[8,16,512]{2,1,0:T(8,128)(2,1)S(1)} %get-tuple-element.89), channel_id=1, source_target_pairs={{0,1},{1,0},{2,3},{3,2},{4,5},{5,4},{6,7},{7,6},{8,9},{9,8},{10,11... | collective-permute-start | bytes 393224 | tf_op jit(solution)/shard_map/ppermute | solution.py:25
  6.9 1.1 %dynamic-slice_bitcast_fusion = (bf16[8,16,512]{2,1,0:T(8,128)(2,1)S(1)}, bf16[8,16,512]{2,1,0:T(8,128)(2,1)S(1)}, bf16[8,16,512]{2,1,0:T(8,128)(2,1)S(1)}, bf16[8,16,512]{2,1,0:T(8,128)(2,1)S(1)}) fusion(s32[]{:T(128)S(6)} %select_n.32, s32[]{:T(128)S(6)} %select_n.31, s32[]{:T(128)S(6)} %select_n.30, s32[]{:T(128)S(6)} %select_n.29, ...), kind=kLoop, calls=%fused_computation | loop fusion | bytes 1048592 | tf_op jit(solution)/shard_map/jit(dynamic_index_in_dim)/squeeze | solution.py:345
  8.1 0.1 pad_add_fusion.ids
  8.1 0.0 copy-done.3
  8.1 0.0 copy-done.2
  8.1 0.0 copy-start
  8.1 0.0 copy-start.1
  8.2 3.7 %prepare.1 = (s32[79]{0:T(128)S(4)}, bf16[512,512]{1,0:T(8,128)(2,1)S(1)}, bf16[512,512]{1,0:T(8,128)(2,1)S(1)}, bf16[512,512]{1,0:T(8,128)(2,1)S(1)}, bf16[512,...) custom-call(s32[2]{0:T(128)S(1)} %pad_add_fusion.ids, s32[3,32]{1,0:T(4,128)S(1)} %copy-done.2, ...), custom_call_target="tpu_custom_call" | custom-call | tf_op jit(solution)/shard_map/prepare/pallas_call | solution.py:98
  11.9 0.0 collective-permute-done.refs_2_
  11.9 4.2 %collective-permute-start.7 = (bf16[8,16,512]{2,1,0:T(8,128)(2,1)S(1)}, bf16[8,16,512]{2,1,0:T(8,128)(2,1)S(1)}, u32[]{:S(2)}, u32[]{:S(2)}) collective-permute-start(bf16[8,16,512]{2,1,0:T(8,128)(2,1)S(1)} %get-tuple-element.105), channel_id=1, source_target_pairs={{0,1},{1,0},{2,3},{3,2},{4,5},{5,4},{6,7},{7,6},{8,9},{9,8},{10,11... | collective-permute-start | bytes 393224 | tf_op jit(solution)/shard_map/ppermute | solution.py:25
  16.1 1.4 %collective-permute-done.2.refs_1_ = bf16[8,16,512]{2,1,0:T(8,128)(2,1)S(1)} collective-permute-done((bf16[8,16,512]{2,1,0:T(8,128)(2,1)S(1)}, bf16[8,16,512]{2,1,0:T(8,128)(2,1)S(1)}, u32[]{:S(2)}, u32[]{:S(2)}) %collective-permute-start.2) | collective-permute-done | bytes 131104 | tf_op jit(solution)/shard_map/ppermute | solution.py:25
  17.5 0.0 collective-permute-done.3.refs_3_
  17.5 0.1 select.2
  17.5 0.1 collective-permute-start.4
  17.6 1.6 %collective-permute-start.5 = (bf16[7,16,512]{2,1,0:T(8,128)(2,1)S(1)}, bf16[7,16,512]{2,1,0:T(8,128)(2,1)S(1)}, u32[]{:S(2)}, u32[]{:S(2)}) collective-permute-start(bf16[7,16,512]{2,1,0:T(8,128)(2,1)S(1)} %get-tuple-element.103), channel_id=1, source_target_pairs={{0,8},{4,12},{8,0},{12,4},{1,9},{5,13},{9,1},{13,5},{2,10},{6,14},... | collective-permute-start | bytes 344072 | tf_op jit(solution)/shard_map/ppermute | solution.py:25
  19.2 0.3 collective-permute-start.6
  19.5 0.0 collective-permute-start.1
  19.5 0.0 copy-done
  19.5 0.0 copy-done.1
  19.5 1.7 %first.2 = (bf16[512,128]{1,0:T(8,128)(2,1)S(1)}, bf16[512,128]{1,0:T(8,128)(2,1)S(1)}, bf16[8,16,512]{2,1,0:T(8,128)(2,1)S(1)}) custom-call(bf16[32,16,512]{2,1,0:T(8,128)(2,1)S(1)} %get-tuple-element.91.refs_0_.refs_1_, f32[1,512]{1,0:T(1,128)S(1)} %bitcast.30, f32[1,512]{1,0:T(1,128)S(1)} %bitcast.34, ...), custom_call_target="tpu_custom_call" | custom-call | flops 1000000000 | tf_op jit(solution)/shard_map/first/pallas_call | solution.py:196
  21.2 0.0 collective-permute-done.4.refs_6_
  21.2 2.5 %collective-permute-start.8 = (bf16[8,16,512]{2,1,0:T(8,128)(2,1)S(1)}, bf16[8,16,512]{2,1,0:T(8,128)(2,1)S(1)}, u32[]{:S(2)}, u32[]{:S(2)}) collective-permute-start(bf16[8,16,512]{2,1,0:T(8,128)(2,1)S(1)} %get-tuple-element.115), channel_id=1, source_target_pairs={{0,3},{1,2},{2,1},{3,0},{4,7},{5,6},{6,5},{7,4},{8,11},{9,10},{10,... | collective-permute-start | bytes 393224 | tf_op jit(solution)/shard_map/ppermute | solution.py:25
  23.7 0.0 collective-permute-done.5.refs_7_
  23.7 1.4 %collective-permute-done.6.refs_8_ = bf16[7,16,512]{2,1,0:T(8,128)(2,1)S(1)} collective-permute-done((bf16[7,16,512]{2,1,0:T(8,128)(2,1)S(1)}, bf16[7,16,512]{2,1,0:T(8,128)(2,1)S(1)}, u32[]{:S(2)}, u32[]{:S(2)}) %collective-permute-start.6) | collective-permute-done | bytes 114720 | tf_op jit(solution)/shard_map/ppermute | solution.py:25
  25.2 0.0 collective-permute-done.7.refs_3_
  25.2 3.7 %block.2 = (bf16[8,16,512]{2,1,0:T(8,128)(2,1)S(1)}, bf16[8,16,512]{2,1,0:T(8,128)(2,1)S(1)}, bf16[8,16,512]{2,1,0:T(8,128)(2,1)S(1)}, bf16[8,16,512]{2,1,0:T(8,128)(2,1)S(1)}) custom-call(s32[79]{0:T(128)S(4)} %get-tuple-element.85.refs_0_, bf16[32,16,512]{2,1,0:T(8,128)(2,1)S(1)} %get-tuple-element.91.refs_0_.refs_1_, ...), custom_call_target="tpu_custom_call" | custom-call | flops 10000000000 | tf_op jit(solution)/shard_map/block/pallas_call | solution.py:266
  28.9 2.7 %collective-permute-done.1.refs_1_ = bf16[8,16,512]{2,1,0:T(8,128)(2,1)S(1)} collective-permute-done((bf16[8,16,512]{2,1,0:T(8,128)(2,1)S(1)}, bf16[8,16,512]{2,1,0:T(8,128)(2,1)S(1)}, u32[]{:S(2)}, u32[]{:S(2)}) %collective-permute-start.1) | collective-permute-done | bytes 131104 | tf_op jit(solution)/shard_map/ppermute | solution.py:25
  31.6 1.3 %collective-permute-start.12 = (bf16[8,16,512]{2,1,0:T(8,128)(2,1)S(1)}, bf16[8,16,512]{2,1,0:T(8,128)(2,1)S(1)}, u32[]{:S(2)}, u32[]{:S(2)}) collective-permute-start(bf16[8,16,512]{2,1,0:T(8,128)(2,1)S(1)} %get-tuple-element.126), channel_id=1, source_target_pairs={{0,3},{1,2},{2,1},{3,0},{4,7},{5,6},{6,5},{7,4},{8,11},{9,10},{10,... | collective-permute-start | bytes 393224 | tf_op jit(solution)/shard_map/ppermute | solution.py:25
  33.0 0.0 collective-permute-done.8.refs_2_
  33.0 0.1 select.3
  33.1 0.1 collective-permute-start.9
  33.1 1.6 %collective-permute-start.10 = (bf16[7,16,512]{2,1,0:T(8,128)(2,1)S(1)}, bf16[7,16,512]{2,1,0:T(8,128)(2,1)S(1)}, u32[]{:S(2)}, u32[]{:S(2)}) collective-permute-start(bf16[7,16,512]{2,1,0:T(8,128)(2,1)S(1)} %get-tuple-element.124), channel_id=1, source_target_pairs={{0,8},{4,12},{8,0},{12,4},{1,9},{5,13},{9,1},{13,5},{2,10},{6,14},... | collective-permute-start | bytes 344072 | tf_op jit(solution)/shard_map/ppermute | solution.py:25
  34.7 0.3 collective-permute-start.11
  35.0 1.9 %collective-permute-start.16 = (bf16[8,16,512]{2,1,0:T(8,128)(2,1)S(1)}, bf16[8,16,512]{2,1,0:T(8,128)(2,1)S(1)}, u32[]{:S(2)}, u32[]{:S(2)}) collective-permute-start(bf16[8,16,512]{2,1,0:T(8,128)(2,1)S(1)} %get-tuple-element.135), channel_id=1, source_target_pairs={{0,2},{1,3},{2,0},{3,1},{4,6},{5,7},{6,4},{7,5},{8,10},{9,11},{10,... | collective-permute-start | bytes 393224 | tf_op jit(solution)/shard_map/ppermute | solution.py:25
  36.9 1.7 %first.3 = (bf16[512,128]{1,0:T(8,128)(2,1)S(1)}, bf16[512,128]{1,0:T(8,128)(2,1)S(1)}, bf16[8,16,512]{2,1,0:T(8,128)(2,1)S(1)}) custom-call(bf16[32,16,512]{2,1,0:T(8,128)(2,1)S(1)} %get-tuple-element.118.refs_0_.refs_1_, f32[1,512]{1,0:T(1,128)S(1)} %bitcast.32, f32[1,512]{1,0:T(1,128)S(1)} %bitcast.36, ...), custom_call_target="tpu_custom_call" | custom-call | flops 1000000000 | tf_op jit(solution)/shard_map/first/pallas_call | solution.py:196
  38.6 0.0 collective-permute-done.9.refs_6_
  38.6 1.2 %collective-permute-start.17 = (bf16[8,16,512]{2,1,0:T(8,128)(2,1)S(1)}, bf16[8,16,512]{2,1,0:T(8,128)(2,1)S(1)}, u32[]{:S(2)}, u32[]{:S(2)}) collective-permute-start(bf16[8,16,512]{2,1,0:T(8,128)(2,1)S(1)} %get-tuple-element.137), channel_id=1, source_target_pairs={{0,1},{1,0},{2,3},{3,2},{4,5},{5,4},{6,7},{7,6},{8,9},{9,8},{10,11... | collective-permute-start | bytes 393224 | tf_op jit(solution)/shard_map/ppermute | solution.py:25
  39.8 0.0 collective-permute-done.10.refs_7_
  39.8 0.9 %collective-permute-done.11.refs_8_ = bf16[7,16,512]{2,1,0:T(8,128)(2,1)S(1)} collective-permute-done((bf16[7,16,512]{2,1,0:T(8,128)(2,1)S(1)}, bf16[7,16,512]{2,1,0:T(8,128)(2,1)S(1)}, u32[]{:S(2)}, u32[]{:S(2)}) %collective-permute-start.11) | collective-permute-done | bytes 114720 | tf_op jit(solution)/shard_map/ppermute | solution.py:25
  40.7 0.0 collective-permute-done.12.refs_2_
  40.7 3.7 %block.3 = (bf16[8,16,512]{2,1,0:T(8,128)(2,1)S(1)}, bf16[8,16,512]{2,1,0:T(8,128)(2,1)S(1)}, bf16[8,16,512]{2,1,0:T(8,128)(2,1)S(1)}, bf16[8,16,512]{2,1,0:T(8,128)(2,1)S(1)}) custom-call(s32[79]{0:T(128)S(4)} %get-tuple-element.85.refs_0_, bf16[32,16,512]{2,1,0:T(8,128)(2,1)S(1)} %get-tuple-element.118.refs_0_.refs_1_, ...), custom_call_target="tpu_custom_call" | custom-call | flops 10000000000 | tf_op jit(solution)/shard_map/block/pallas_call | solution.py:266
  44.4 2.0 %collective-permute-start.13 = (bf16[8,16,512]{2,1,0:T(8,128)(2,1)S(1)}, bf16[8,16,512]{2,1,0:T(8,128)(2,1)S(1)}, u32[]{:S(2)}, u32[]{:S(2)}) collective-permute-start(bf16[8,16,512]{2,1,0:T(8,128)(2,1)S(1)} %get-tuple-element.131), channel_id=1, source_target_pairs={{0,2},{1,3},{2,0},{3,1},{4,6},{5,7},{6,4},{7,5},{8,10},{9,11},{10,... | collective-permute-start | bytes 393224 | tf_op jit(solution)/shard_map/ppermute | solution.py:25
  46.4 2.5 %collective-permute-start.14 = (bf16[8,16,512]{2,1,0:T(8,128)(2,1)S(1)}, bf16[8,16,512]{2,1,0:T(8,128)(2,1)S(1)}, u32[]{:S(2)}, u32[]{:S(2)}) collective-permute-start(bf16[8,16,512]{2,1,0:T(8,128)(2,1)S(1)} %get-tuple-element.132), channel_id=1, source_target_pairs={{0,3},{1,2},{2,1},{3,0},{4,7},{5,6},{6,5},{7,4},{8,11},{9,10},{10,... | collective-permute-start | bytes 393224 | tf_op jit(solution)/shard_map/ppermute | solution.py:25
  48.9 0.0 collective-permute-start.15
  48.9 0.0 collective-permute-done.16.refs_1_
  48.9 0.0 collective-permute-done.17.refs_3_
  48.9 0.8 %assemble.2.refs_5_ = bf16[8,8,16,512]{3,2,1,0:T(8,128)(2,1)} custom-call(s32[79]{0:T(128)S(4)} %get-tuple-element.85.refs_0_, bf16[8,16,512]{2,1,0:T(8,128)(2,1)S(1)} %collective-permute-done.16.refs_1_, bf16[8,16,512]{2,1,0:T(8,128)(2,1)S(1)} %collective-permute-done.12.refs_2_, bf16[8,16,512]{2,1,0:T(8,128)(2,1)S(1)} %collective-permute-done.17.refs_3_, ...), custom_call_target="tpu_custom_call" | custom-call | tf_op jit(solution)/shard_map/assemble/pallas_call | solution.py:310
  49.7 7.6 %collective-permute-done.13.refs_1_ = bf16[8,16,512]{2,1,0:T(8,128)(2,1)S(1)} collective-permute-done((bf16[8,16,512]{2,1,0:T(8,128)(2,1)S(1)}, bf16[8,16,512]{2,1,0:T(8,128)(2,1)S(1)}, u32[]{:S(2)}, u32[]{:S(2)}) %collective-permute-start.13) | collective-permute-done | bytes 131104 | tf_op jit(solution)/shard_map/ppermute | solution.py:25
  57.4 0.0 collective-permute-done.14.refs_2_
  57.4 1.0 %collective-permute-done.15.refs_3_ = bf16[8,16,512]{2,1,0:T(8,128)(2,1)S(1)} collective-permute-done((bf16[8,16,512]{2,1,0:T(8,128)(2,1)S(1)}, bf16[8,16,512]{2,1,0:T(8,128)(2,1)S(1)}, u32[]{:S(2)}, u32[]{:S(2)}) %collective-permute-start.15) | collective-permute-done | bytes 131104 | tf_op jit(solution)/shard_map/ppermute | solution.py:25
  58.4 0.8 %assemble.3 = bf16[8,8,16,512]{3,2,1,0:T(8,128)(2,1)} custom-call(s32[79]{0:T(128)S(4)} %get-tuple-element.85.refs_0_, bf16[8,16,512]{2,1,0:T(8,128)(2,1)S(1)} %collective-permute-done.13.refs_1_, bf16[8,16,512]{2,1,0:T(8,128)(2,1)S(1)} %collective-permute-done.14.refs_2_, ...), custom_call_target="tpu_custom_call", output_to_operand_aliasing={{}: (5, {})} | custom-call | tf_op jit(solution)/shard_map/assemble/pallas_call | solution.py:310
Async XLA Ops:
  0.0 8.1 %copy-start.3 = (s32[3,32]{1,0:T(4,128)S(1)}, s32[3,32]{1,0:T(4,128)}, u32[]{:S(2)}) copy-start(s32[3,32]{1,0:T(4,128)} %merge_num) | copy-start | bytes 1156
  0.0 8.1 %copy-start.2 = (s32[3,32]{1,0:T(4,128)S(1)}, s32[3,32]{1,0:T(4,128)}, u32[]{:S(2)}) copy-start(s32[3,32]{1,0:T(4,128)} %src) | copy-start | bytes 1156
  1.2 10.7 %collective-permute-start = (bf16[8,16,512]{2,1,0:T(8,128)(2,1)S(1)}, bf16[8,16,512]{2,1,0:T(8,128)(2,1)S(1)}, u32[]{:S(2)}, u32[]{:S(2)}) collective-permute-start(bf16[8,16,512]{2,1,0:T(8,128)(2,1)S(1)} %get-tuple-element.84), channel_id=1, source_target_pairs={{0,3},{1,2},{2,1},{3,0},{4,7},{5,6},{6,5},{7,4},{8,11},{9,10},{10,... | collective-permute-start | bytes 393224 | tf_op jit(solution)/shard_map/ppermute | solution.py:25
  6.3 11.2 %collective-permute-start.2 = (bf16[8,16,512]{2,1,0:T(8,128)(2,1)S(1)}, bf16[8,16,512]{2,1,0:T(8,128)(2,1)S(1)}, u32[]{:S(2)}, u32[]{:S(2)}) collective-permute-start(bf16[8,16,512]{2,1,0:T(8,128)(2,1)S(1)} %get-tuple-element.87), channel_id=1, source_target_pairs={{0,2},{1,3},{2,0},{3,1},{4,6},{5,7},{6,4},{7,5},{8,10},{9,11},{10,... | collective-permute-start | bytes 393224 | tf_op jit(solution)/shard_map/ppermute | solution.py:25
  6.3 11.2 %collective-permute-start.3 = (bf16[8,16,512]{2,1,0:T(8,128)(2,1)S(1)}, bf16[8,16,512]{2,1,0:T(8,128)(2,1)S(1)}, u32[]{:S(2)}, u32[]{:S(2)}) collective-permute-start(bf16[8,16,512]{2,1,0:T(8,128)(2,1)S(1)} %get-tuple-element.89), channel_id=1, source_target_pairs={{0,1},{1,0},{2,3},{3,2},{4,5},{5,4},{6,7},{7,6},{8,9},{9,8},{10,11... | collective-permute-start | bytes 393224 | tf_op jit(solution)/shard_map/ppermute | solution.py:25
  8.1 11.3 %copy-start = (f32[512]{0:T(512)S(1)}, f32[512]{0:T(512)}, u32[]{:S(2)}) copy-start(f32[512]{0:T(512)} %param.14) | copy-start | bytes 6148
  8.1 11.3 %copy-start.1 = (f32[512]{0:T(512)S(1)}, f32[512]{0:T(512)}, u32[]{:S(2)}) copy-start(f32[512]{0:T(512)} %param.19) | copy-start | bytes 6148
  11.9 13.3 %collective-permute-start.7 = (bf16[8,16,512]{2,1,0:T(8,128)(2,1)S(1)}, bf16[8,16,512]{2,1,0:T(8,128)(2,1)S(1)}, u32[]{:S(2)}, u32[]{:S(2)}) collective-permute-start(bf16[8,16,512]{2,1,0:T(8,128)(2,1)S(1)} %get-tuple-element.105), channel_id=1, source_target_pairs={{0,1},{1,0},{2,3},{3,2},{4,5},{5,4},{6,7},{7,6},{8,9},{9,8},{10,11... | collective-permute-start | bytes 393224 | tf_op jit(solution)/shard_map/ppermute | solution.py:25
  17.5 3.6 %collective-permute-start.4 = (bf16[7,16,512]{2,1,0:T(8,128)(2,1)S(1)}, bf16[7,16,512]{2,1,0:T(8,128)(2,1)S(1)}, u32[]{:S(2)}, u32[]{:S(2)}) collective-permute-start(bf16[7,16,512]{2,1,0:T(8,128)(2,1)S(1)} %get-tuple-element.102), channel_id=1, source_target_pairs={{0,4},{4,0},{8,12},{12,8},{1,5},{5,1},{9,13},{13,9},{2,6},{6,2},{1... | collective-permute-start | bytes 344072 | tf_op jit(solution)/shard_map/ppermute | solution.py:25
  17.6 6.1 %collective-permute-start.5 = (bf16[7,16,512]{2,1,0:T(8,128)(2,1)S(1)}, bf16[7,16,512]{2,1,0:T(8,128)(2,1)S(1)}, u32[]{:S(2)}, u32[]{:S(2)}) collective-permute-start(bf16[7,16,512]{2,1,0:T(8,128)(2,1)S(1)} %get-tuple-element.103), channel_id=1, source_target_pairs={{0,8},{4,12},{8,0},{12,4},{1,9},{5,13},{9,1},{13,5},{2,10},{6,14},... | collective-permute-start | bytes 344072 | tf_op jit(solution)/shard_map/ppermute | solution.py:25
  19.2 6.0 %collective-permute-start.6 = (bf16[7,16,512]{2,1,0:T(8,128)(2,1)S(1)}, bf16[7,16,512]{2,1,0:T(8,128)(2,1)S(1)}, u32[]{:S(2)}, u32[]{:S(2)}) collective-permute-start(bf16[7,16,512]{2,1,0:T(8,128)(2,1)S(1)} %get-tuple-element.104), channel_id=1, source_target_pairs={{0,12},{4,8},{8,4},{12,0},{1,13},{5,9},{9,5},{13,1},{2,14},{6,10},... | collective-permute-start | bytes 344072 | tf_op jit(solution)/shard_map/ppermute | solution.py:25
  19.5 12.2 %collective-permute-start.1 = (bf16[8,16,512]{2,1,0:T(8,128)(2,1)S(1)}, bf16[8,16,512]{2,1,0:T(8,128)(2,1)S(1)}, u32[]{:S(2)}, u32[]{:S(2)}) collective-permute-start(bf16[8,16,512]{2,1,0:T(8,128)(2,1)S(1)} %get-tuple-element.86), channel_id=1, source_target_pairs={{0,2},{1,3},{2,0},{3,1},{4,6},{5,7},{6,4},{7,5},{8,10},{9,11},{10,... | collective-permute-start | bytes 393224 | tf_op jit(solution)/shard_map/ppermute | solution.py:25
  21.2 11.8 %collective-permute-start.8 = (bf16[8,16,512]{2,1,0:T(8,128)(2,1)S(1)}, bf16[8,16,512]{2,1,0:T(8,128)(2,1)S(1)}, u32[]{:S(2)}, u32[]{:S(2)}) collective-permute-start(bf16[8,16,512]{2,1,0:T(8,128)(2,1)S(1)} %get-tuple-element.115), channel_id=1, source_target_pairs={{0,3},{1,2},{2,1},{3,0},{4,7},{5,6},{6,5},{7,4},{8,11},{9,10},{10,... | collective-permute-start | bytes 393224 | tf_op jit(solution)/shard_map/ppermute | solution.py:25
  31.6 9.1 %collective-permute-start.12 = (bf16[8,16,512]{2,1,0:T(8,128)(2,1)S(1)}, bf16[8,16,512]{2,1,0:T(8,128)(2,1)S(1)}, u32[]{:S(2)}, u32[]{:S(2)}) collective-permute-start(bf16[8,16,512]{2,1,0:T(8,128)(2,1)S(1)} %get-tuple-element.126), channel_id=1, source_target_pairs={{0,3},{1,2},{2,1},{3,0},{4,7},{5,6},{6,5},{7,4},{8,11},{9,10},{10,... | collective-permute-start | bytes 393224 | tf_op jit(solution)/shard_map/ppermute | solution.py:25
  33.1 5.5 %collective-permute-start.9 = (bf16[7,16,512]{2,1,0:T(8,128)(2,1)S(1)}, bf16[7,16,512]{2,1,0:T(8,128)(2,1)S(1)}, u32[]{:S(2)}, u32[]{:S(2)}) collective-permute-start(bf16[7,16,512]{2,1,0:T(8,128)(2,1)S(1)} %get-tuple-element.123), channel_id=1, source_target_pairs={{0,4},{4,0},{8,12},{12,8},{1,5},{5,1},{9,13},{13,9},{2,6},{6,2},{1... | collective-permute-start | bytes 344072 | tf_op jit(solution)/shard_map/ppermute | solution.py:25
  33.1 6.7 %collective-permute-start.10 = (bf16[7,16,512]{2,1,0:T(8,128)(2,1)S(1)}, bf16[7,16,512]{2,1,0:T(8,128)(2,1)S(1)}, u32[]{:S(2)}, u32[]{:S(2)}) collective-permute-start(bf16[7,16,512]{2,1,0:T(8,128)(2,1)S(1)} %get-tuple-element.124), channel_id=1, source_target_pairs={{0,8},{4,12},{8,0},{12,4},{1,9},{5,13},{9,1},{13,5},{2,10},{6,14},... | collective-permute-start | bytes 344072 | tf_op jit(solution)/shard_map/ppermute | solution.py:25
  34.7 6.0 %collective-permute-start.11 = (bf16[7,16,512]{2,1,0:T(8,128)(2,1)S(1)}, bf16[7,16,512]{2,1,0:T(8,128)(2,1)S(1)}, u32[]{:S(2)}, u32[]{:S(2)}) collective-permute-start(bf16[7,16,512]{2,1,0:T(8,128)(2,1)S(1)} %get-tuple-element.125), channel_id=1, source_target_pairs={{0,12},{4,8},{8,4},{12,0},{1,13},{5,9},{9,5},{13,1},{2,14},{6,10},... | collective-permute-start | bytes 344072 | tf_op jit(solution)/shard_map/ppermute | solution.py:25
  35.0 13.9 %collective-permute-start.16 = (bf16[8,16,512]{2,1,0:T(8,128)(2,1)S(1)}, bf16[8,16,512]{2,1,0:T(8,128)(2,1)S(1)}, u32[]{:S(2)}, u32[]{:S(2)}) collective-permute-start(bf16[8,16,512]{2,1,0:T(8,128)(2,1)S(1)} %get-tuple-element.135), channel_id=1, source_target_pairs={{0,2},{1,3},{2,0},{3,1},{4,6},{5,7},{6,4},{7,5},{8,10},{9,11},{10,... | collective-permute-start | bytes 393224 | tf_op jit(solution)/shard_map/ppermute | solution.py:25
  38.6 10.3 %collective-permute-start.17 = (bf16[8,16,512]{2,1,0:T(8,128)(2,1)S(1)}, bf16[8,16,512]{2,1,0:T(8,128)(2,1)S(1)}, u32[]{:S(2)}, u32[]{:S(2)}) collective-permute-start(bf16[8,16,512]{2,1,0:T(8,128)(2,1)S(1)} %get-tuple-element.137), channel_id=1, source_target_pairs={{0,1},{1,0},{2,3},{3,2},{4,5},{5,4},{6,7},{7,6},{8,9},{9,8},{10,11... | collective-permute-start | bytes 393224 | tf_op jit(solution)/shard_map/ppermute | solution.py:25
  44.4 12.9 %collective-permute-start.13 = (bf16[8,16,512]{2,1,0:T(8,128)(2,1)S(1)}, bf16[8,16,512]{2,1,0:T(8,128)(2,1)S(1)}, u32[]{:S(2)}, u32[]{:S(2)}) collective-permute-start(bf16[8,16,512]{2,1,0:T(8,128)(2,1)S(1)} %get-tuple-element.131), channel_id=1, source_target_pairs={{0,2},{1,3},{2,0},{3,1},{4,6},{5,7},{6,4},{7,5},{8,10},{9,11},{10,... | collective-permute-start | bytes 393224 | tf_op jit(solution)/shard_map/ppermute | solution.py:25
  46.4 10.9 %collective-permute-start.14 = (bf16[8,16,512]{2,1,0:T(8,128)(2,1)S(1)}, bf16[8,16,512]{2,1,0:T(8,128)(2,1)S(1)}, u32[]{:S(2)}, u32[]{:S(2)}) collective-permute-start(bf16[8,16,512]{2,1,0:T(8,128)(2,1)S(1)} %get-tuple-element.132), channel_id=1, source_target_pairs={{0,3},{1,2},{2,1},{3,0},{4,7},{5,6},{6,5},{7,4},{8,11},{9,10},{10,... | collective-permute-start | bytes 393224 | tf_op jit(solution)/shard_map/ppermute | solution.py:25
  48.9 9.5 %collective-permute-start.15 = (bf16[8,16,512]{2,1,0:T(8,128)(2,1)S(1)}, bf16[8,16,512]{2,1,0:T(8,128)(2,1)S(1)}, u32[]{:S(2)}, u32[]{:S(2)}) collective-permute-start(bf16[8,16,512]{2,1,0:T(8,128)(2,1)S(1)} %get-tuple-element.133), channel_id=1, source_target_pairs={{0,1},{1,0},{2,3},{3,2},{4,5},{5,4},{6,7},{7,6},{8,9},{9,8},{10,11... | collective-permute-start | bytes 393224 | tf_op jit(solution)/shard_map/ppermute | solution.py:25
